TPU v7x, 256 devices: a whole 4x4x8 slice. The times are simulated.
256 devices in a mesh: dp: 32 (over y, z_lo, core), tensor: 8 (over z_hi, x).
Axes of the slice: x: 4, y: 4, z: 8 (z_hi: 2, z_lo: 4; z = z_hi * 4 + z_lo), core: 2. Of those that a mesh axis runs over, the one named last changes fastest.
Arguments:
- stream_in: bfloat16 [4096, 4096], P(('dp', 'tensor')), may hold values from -6 to 6
- pending: bfloat16 [8, 4096, 4096], P('tensor', 'dp'), may hold values from -6 to 6
- gain: float32 [4096], replicated, may hold values from 0.5 to 1.5
- q_weight: bfloat16 [4096, 4096], P('dp', 'tensor'), may hold values from -1 to 1
- k_weight: bfloat16 [4096, 512], P('dp'), may hold values from -4 to 4
- v_weight: bfloat16 [4096, 512], P('dp'), may hold values from -0.09375 to 0.09375
- out_weight: bfloat16 [4096, 4096], P('dp', 'tensor'), may hold values from -0.09375 to 0.09375
- grad_out: bfloat16 [4096, 4096], P(('dp', 'tensor')), may hold values from -6 to 6
- doc_ids: int32 [4096], replicated, may hold values from 0 to 5, never falling along the last dimension, each value on 1 to 3072 neighbouring positions
Outputs:
- hidden_out: bfloat16 [4096, 4096], P(('dp', 'tensor'))
- grad_stream: bfloat16 [4096, 4096], P(('dp', 'tensor'))
- grad_gain: float32 [4096], replicated
- grad_q: float32 [4096, 4096], P('dp', 'tensor')
- grad_k: float32 [4096, 512], P('dp')
- grad_v: float32 [4096, 512], P('dp')
- grad_o: float32 [4096, 4096], P('dp', 'tensor')
Inputs may be any that keep to these rules, and one draw needn't show every extreme that they name: `doc_ids`: never falls along the positions; the longest document has exactly 3072 positions.
All inputs are finite; a program needn't handle non-finite values.
Results may differ from a plain program's by a relative error of at most 0.035.
The roundings to bfloat16 on the way count: a program that leaves them out, or rounds other values in their place, can miss the bound.
Values may be sent and summed in bfloat16 or wider, within the bound.
No kernel may reach another device: no remote copies, remote signals or barrier semaphores. Data moves between devices by JAX's collectives and lax.ppermute only.
A program may use at most 128 MiB of HBM per device.

v0:
```python
import jax
import jax.numpy as jnp
from jax import lax
from jax.experimental import pallas as pl
from jax.experimental.pallas import tpu as pltpu
from jax.sharding import Mesh
from jax.sharding import PartitionSpec as P

HEADS = 32
KV_HEADS = 4
HEAD_DIM = 128
HALF_DIM = HEAD_DIM // 2

eps = 1e-05
rope_base = 500000.0

SIZES = {"y": 4, "z": 4, "c": 2, "h": 2, "x": 4}
DP = ("y", "z", "c")
TENSOR = ("h", "x")
NX = SIZES["x"]
wide = jnp.float32
low = jnp.bfloat16


def dot(a, b, dims):
    return lax.dot_general(a, b, (dims, ((), ())), preferred_element_type=wide)


def swap(a, axis):
    return lax.ppermute(a, axis, [(0, 1), (1, 0)])


def shift(a, step):
    return lax.ppermute(a, "x", [((i + step) % NX, i) for i in range(NX)])


def spread(a, axis):
    size = SIZES[axis]
    return lax.all_to_all(
        jnp.broadcast_to(a[None], (size,) + a.shape), axis, 0, 0, tiled=True
    )


def spread_yz(a):
    rows, cols = a.shape
    a = spread(a, "z").reshape(SIZES["z"] * rows, cols)
    return spread(a, "y").reshape(SIZES["y"] * SIZES["z"] * rows, cols)


def collect(a, axis):
    return jnp.sum(lax.all_to_all(a, axis, 0, 0, tiled=True).astype(wide), axis=0)


def collect_yz(a):
    rows, cols = a.shape
    a = collect(a.reshape(SIZES["y"], rows // SIZES["y"], cols), "y").astype(low)
    return collect(a.reshape(SIZES["z"], a.shape[0] // SIZES["z"], cols), "z")


def all_sum(a, axis):
    if SIZES[axis] == 2:
        return a + swap(a, axis)
    far = [lax.ppermute(a, axis, [(i, i ^ k) for i in range(4)]) for k in range(1, 4)]
    return (a + far[0]) + (far[1] + far[2])


def spread_tensor(a):
    both = jnp.stack([a, swap(a, "h")])
    return jnp.stack([both] + [shift(both, k) for k in range(1, NX)])


def collect_tensor(a):
    total = a[0].astype(wide)
    for k in range(1, NX):
        total = total + shift(a[k], NX - k).astype(wide)
    return total[0] + swap(total[1].astype(low), "h").astype(wide)


def turn(field, cosine, sine):
    return field * cosine + pltpu.roll(field, HALF_DIM, 1) * sine


PARAMS = pltpu.CompilerParams(vmem_limit_bytes=48 * 2**20)
ANY = pl.BlockSpec(memory_space=pl.ANY)


def project_kernel(normed, grads, weights, cosine, sine, rows, pend, query, grad_heads, total):
    step = pl.program_id(0)
    tok, half = normed.shape[0], weights.shape[1] // 2

    @pl.when(step == 0)
    def _():
        total[...] = jnp.zeros_like(total)

    total[:, :half] += dot(normed[...], weights[:, :half], ((1,), (0,)))
    total[:, half:] += dot(grads[...], weights[:, half:], ((1,), (0,)))

    @pl.when(step == pl.num_programs(0) - 1)
    def _():
        for i in range(half // HEAD_DIM):
            at = pl.ds(i * tok, tok)
            query[at, :] = turn(
                total[:, i * HEAD_DIM : (i + 1) * HEAD_DIM], cosine[...], sine[...]
            ).astype(low)
            grad_heads[at, :] = total[
                :, half + i * HEAD_DIM : half + (i + 1) * HEAD_DIM
            ].astype(low)


def project(normed, grads, weights, cosine, sine, rows, pend, step=512):
    tok, width = normed.shape
    cols = weights.shape[1]
    out = jax.ShapeDtypeStruct((cols // 2 // HEAD_DIM * tok, HEAD_DIM), low)
    fixed = pl.BlockSpec((tok, HEAD_DIM), lambda i: (0, 0))
    return pl.pallas_call(
        project_kernel,
        grid=(width // step,),
        in_specs=[
            pl.BlockSpec((tok, step), lambda i: (0, i)),
            pl.BlockSpec((tok, step), lambda i: (0, i)),
            pl.BlockSpec((step, cols), lambda i: (i, 0)),
            fixed,
            fixed,
            ANY,
            ANY,
        ],
        out_specs=[pl.BlockSpec(out.shape, lambda i: (0, 0))] * 2,
        out_shape=[out, out],
        scratch_shapes=[pltpu.VMEM((tok, cols), wide)],
        compiler_params=PARAMS,
    )(normed, grads, weights, cosine, sine, rows, pend)


def attend_kernel(
    query, grad_heads, near, far, key_place, bounds, cosine, sine, att_gq, near_grad, far_grad, score
):
    rows = query.shape[0]
    tok = cosine.shape[0]
    heads = rows // tok
    half = near.shape[0]
    step = 512
    scale = HEAD_DIM ** (-0.5)
    q, g = query[...], grad_heads[...]
    last, first = bounds[0:1, :], bounds[1:2, :]

    peak = jnp.full((1, rows), -1e30, wide)
    for kv, base in ((near, 0), (far, half)):

        def mark(i, peak, kv=kv, base=base):
            at = pl.multiple_of(i * step, step)
            s = dot(kv[pl.ds(at, step), :HEAD_DIM], q, ((1,), (1,))) * scale
            place = key_place[pl.ds(base + at, step), :]
            place = jnp.broadcast_to(place, (step, tok))
            bias = jnp.where((place <= last) & (place >= first), 0.0, -1e30)
            s = s + jnp.concatenate([bias] * heads, axis=1)
            score[pl.ds(base + at, step), :] = s
            return jnp.maximum(peak, jnp.max(s, axis=0, keepdims=True))

        peak = lax.fori_loop(0, half // step, mark, peak)

    carry = (jnp.zeros((1, rows), wide), jnp.zeros((HEAD_DIM, rows), wide))
    for kv, base in ((near, 0), (far, half)):

        def weigh(i, carry, kv=kv, base=base):
            norm, out = carry
            at = pl.multiple_of(i * step, step)
            e = jnp.exp(score[pl.ds(base + at, step), :] - peak)
            score[pl.ds(base + at, step), :] = e
            out = out + dot(kv[pl.ds(at, step), HEAD_DIM:], e.astype(low), ((0,), (0,)))
            return norm + jnp.sum(e, axis=0, keepdims=True), out

        carry = lax.fori_loop(0, half // step, weigh, carry)
    norm, out = carry
    inverse = 1.0 / norm
    out = (out * inverse).astype(low).astype(wide)
    delta = jnp.sum(out * g.astype(wide).T, axis=0, keepdims=True)

    grad_query = jnp.zeros((HEAD_DIM, rows), wide)
    for kv, grad, base in ((near, near_grad, 0), (far, far_grad, half)):

        def back(i, grad_query, kv=kv, grad=grad, base=base):
            at = pl.multiple_of(i * step, step)
            p = score[pl.ds(base + at, step), :] * inverse
            gp = dot(kv[pl.ds(at, step), HEAD_DIM:], g, ((1,), (1,)))
            gs = (p * (gp - delta)).astype(low)
            grad[pl.ds(at, step), :HEAD_DIM] = (dot(gs, q, ((1,), (0,))) * scale).astype(low)
            grad[pl.ds(at, step), HEAD_DIM:] = dot(p.astype(low), g, ((1,), (0,))).astype(low)
            return grad_query + dot(kv[pl.ds(at, step), :HEAD_DIM], gs, ((0,), (0,)))

        grad_query = lax.fori_loop(0, half // step, back, grad_query)

    for i in range(heads):
        at, cols = slice(i * tok, (i + 1) * tok), slice(i * HEAD_DIM, (i + 1) * HEAD_DIM)
        att_gq[:, cols] = out[:, at].T.astype(low)
        back_cols = slice(heads * HEAD_DIM + cols.start, heads * HEAD_DIM + cols.stop)
        att_gq[:, back_cols] = turn(
            grad_query[:, at].T * scale, cosine[...], -sine[...]
        ).astype(low)


def attend(query, grad_heads, near, far, key_place, bounds, cosine, sine):
    rows, tok = query.shape[0], cosine.shape[0]
    half = near.shape[0]
    return pl.pallas_call(
        attend_kernel,
        out_shape=[
            jax.ShapeDtypeStruct((tok, 2 * rows // tok * HEAD_DIM), low),
            jax.ShapeDtypeStruct(near.shape, low),
            jax.ShapeDtypeStruct(far.shape, low),
        ],
        scratch_shapes=[pltpu.VMEM((2 * half, rows), wide)],
        compiler_params=PARAMS,
    )(query, grad_heads, near, far, key_place, bounds, cosine, sine)


def back_project_kernel(att_gq, weights, terms, grad):
    half = weights.shape[1] // 2
    terms[...] = dot(att_gq[:, :half], weights[:, half:], ((1,), (1,))).astype(low)
    grad[...] = dot(att_gq[:, half:], weights[:, :half], ((1,), (1,)))


def back_project(att_gq, weights, step=512):
    tok = att_gq.shape[0]
    width, cols = weights.shape
    out = pl.BlockSpec((tok, step), lambda i: (0, i))
    return pl.pallas_call(
        back_project_kernel,
        grid=(width // step,),
        in_specs=[
            pl.BlockSpec(att_gq.shape, lambda i: (0, 0)),
            pl.BlockSpec((step, cols), lambda i: (i, 0)),
        ],
        out_specs=[out, out],
        out_shape=[
            jax.ShapeDtypeStruct((tok, width), low),
            jax.ShapeDtypeStruct((tok, width), wide),
        ],
        compiler_params=PARAMS,
    )(att_gq, weights)


def weight_grad_kernel(rows, att_gq, grad_o, grad_q):
    half, block = att_gq.shape[1] // 2, rows.shape[1] // 2

    @pl.when(pl.program_id(0) == 0)
    def _():
        grad_o[...] = jnp.zeros_like(grad_o)
        grad_q[...] = jnp.zeros_like(grad_q)

    grad_o[...] += dot(rows[:, :block], att_gq[:, :half], ((0,), (0,)))
    grad_q[...] += dot(rows[:, block:], att_gq[:, half:], ((0,), (0,)))


def weight_grads(rows, att_gq, step=512):
    seq_len, cols = att_gq.shape
    out = jax.ShapeDtypeStruct((rows.shape[1] // 2, cols // 2), wide)
    return pl.pallas_call(
        weight_grad_kernel,
        grid=(seq_len // step,),
        in_specs=[
            pl.BlockSpec((step, rows.shape[1]), lambda i: (i, 0)),
            pl.BlockSpec((step, cols), lambda i: (i, 0)),
        ],
        out_specs=[pl.BlockSpec(out.shape, lambda i: (0, 0))] * 2,
        out_shape=[out, out],
        compiler_params=PARAMS,
    )(rows, att_gq)


def on_device(
    stream_in, pending, gain, q_weight, k_weight, v_weight, out_weight, grad_out, doc_ids
):
    y, z, c, h, x = (lax.axis_index(a) for a in ("y", "z", "c", "h", "x"))
    tens_index = h * NX + x
    rows_own, width = stream_in.shape
    tok = pending.shape[1]
    outer = SIZES["y"] * SIZES["z"]
    n_dp = outer * 2
    block = width // n_dp
    q_width = q_weight.shape[1]
    seq_len = doc_ids.shape[0]

    def by_core(near):
        cols = near.shape[1]
        far = swap(near, "c")
        near, far = (a.reshape(outer, 1, near.shape[0] // outer, cols) for a in (near, far))
        pair = [jnp.where(c == 0, near, far), jnp.where(c == 0, far, near)]
        return jnp.concatenate(pair, axis=1).reshape(-1, cols)

    weights = lax.all_gather(
        jnp.concatenate([q_weight, out_weight], axis=1), DP, axis=0, tiled=True
    )

    kv_first = tens_index * (q_width // HEAD_DIM) // (HEADS // KV_HEADS) * HEAD_DIM
    kv_weight = jnp.concatenate(
        [lax.dynamic_slice_in_dim(w, kv_first, HEAD_DIM, 1) for w in (k_weight, v_weight)], axis=1
    )
    wkv = by_core(spread_yz(kv_weight))

    stream_f = stream_in.astype(wide)
    inv_rms = lax.rsqrt(jnp.mean(stream_f * stream_f, axis=-1, keepdims=True) + eps)
    unit_rows = stream_f * inv_rms
    normed_own = (unit_rows * gain).astype(low)
    normed = spread_tensor(normed_own).reshape(tok, width)

    def index(axis):
        return lax.broadcasted_iota(jnp.int32, (NX, 2, rows_own), axis)

    local = (((h ^ index(1)) * NX + (x + index(0)) % NX) * rows_own + index(2)).reshape(tok)
    block_first = ((y * SIZES["z"] + z) * 2 + c) * tok
    places = block_first + local
    rel_c = jnp.arange(2, dtype=jnp.int32)[:, None, None]
    at_yz = jnp.arange(outer, dtype=jnp.int32)[None, :, None]
    key_place = ((at_yz * 2 + (c ^ rel_c)) * tok + local[None, None, :]).reshape(seq_len, 1)

    def relative(a):
        a = a.reshape((2, NX, rows_own) + a.shape[1:])
        a = jnp.where(h == 0, a, a[::-1])
        a = lax.dynamic_slice_in_dim(jnp.concatenate([a, a], axis=1), x, NX, 1)
        return jnp.swapaxes(a, 0, 1)

    doc_query = relative(lax.dynamic_slice_in_dim(doc_ids, block_first, tok)).reshape(tok)
    first_place = jnp.sum((doc_ids[None, :] < doc_query[:, None]).astype(jnp.int32), axis=1)

    frequency = rope_base ** (-2.0 * jnp.arange(HALF_DIM).astype(wide) / HEAD_DIM)
    angles = places.astype(wide)[:, None] * frequency[None, :]
    cosine, sine = jnp.cos(angles), jnp.sin(angles)
    cosine = jnp.concatenate([cosine, cosine], axis=1)
    sine = jnp.concatenate([-sine, sine], axis=1)

    def rotate(field, sign):
        flipped = jnp.concatenate([field[:, HALF_DIM:], field[:, :HALF_DIM]], axis=1)
        return field * cosine + sign * flipped * sine

    kv_proj = dot(normed, wkv, ((1,), (0,)))
    keys_own = rotate(kv_proj[:, :HEAD_DIM], 1.0)
    kv_own = jnp.concatenate([keys_own, kv_proj[:, HEAD_DIM:]], axis=1).astype(low)
    kv_near = spread_yz(kv_own)
    kv_far = swap(kv_near, "c")

    grads = spread_tensor(grad_out).reshape(tok, width)

    split = [a.reshape(rows_own, n_dp, block) for a in (grad_out, normed_own)]
    rows = jnp.transpose(jnp.concatenate(split, axis=2), (1, 0, 2))
    rows = spread_tensor(lax.all_to_all(rows, DP, 0, 0, tiled=True))
    rows = jnp.transpose(rows, (2, 0, 1, 3, 4)).reshape(seq_len, 2 * block)
    normed_cores = rows[:, block:].reshape(outer, 2, tok, block)
    rows_near, rows_far = (
        lax.dynamic_index_in_dim(normed_cores, i, 1, keepdims=False).reshape(-1, block)
        for i in (c, 1 - c)
    )
    pend = relative(pending[0])

    query, grad_heads = project(normed, grads, weights, cosine, sine, rows, pend)
    bounds = jnp.stack([places, first_place])
    att_gq, near_piece, far_piece = attend(
        query, grad_heads, kv_near, kv_far, key_place, bounds, cosine, sine
    )
    att_gq_all = lax.all_gather(att_gq, DP, axis=0, tiled=True)

    kv_sum = near_piece.astype(wide) + swap(far_piece, "c").astype(wide)
    kv_grad = collect_yz(kv_sum.astype(low))
    grad_key = rotate(kv_grad[:, :HEAD_DIM], -1.0)
    grad_kv = jnp.concatenate([grad_key, kv_grad[:, HEAD_DIM:]], axis=1).astype(low)

    gkv_near = spread_yz(grad_kv)
    gkv_far = swap(gkv_near, "c")
    grad_w_kv = dot(rows_near, gkv_near, ((0,), (0,))) + dot(rows_far, gkv_far, ((0,), (0,)))

    terms, query_terms = back_project(att_gq, weights)
    terms = terms.reshape(NX, 2, rows_own, width).astype(wide) + pend.astype(wide)
    hidden_out = (stream_f + collect_tensor(terms.astype(low))).astype(low)

    normed_terms = query_terms + dot(grad_kv, wkv, ((1,), (1,)))
    grad_normed = collect_tensor(normed_terms.astype(low).reshape(NX, 2, rows_own, width))
    gain_sum = jnp.sum(normed_terms * normed.astype(wide), axis=0).reshape(n_dp, block)
    for axis in ("c", "h", "x", "y", "z"):
        gain_sum = all_sum(gain_sum, axis)
    grad_gain = gain_sum.reshape(width) / gain

    grad_o, grad_q = weight_grads(rows, att_gq_all)

    kv_own_w = grad_w_kv.astype(low)
    kv_blocks = [kv_own_w.astype(wide)] + [shift(kv_own_w, k).astype(wide) for k in range(1, NX)]
    odd = x % 2 == 1
    near = kv_blocks[0] + jnp.where(odd, kv_blocks[3], kv_blocks[1])
    far = kv_blocks[2] + jnp.where(odd, kv_blocks[1], kv_blocks[3])
    pair = jnp.stack([jnp.where(x < 2, near, far), jnp.where(x < 2, far, near)]).astype(low)
    other = swap(pair, "h")
    pair = jnp.concatenate(
        [jnp.where(h == 0, pair, other), jnp.where(h == 0, other, pair)], axis=0
    ).astype(wide)
    grad_k, grad_v = (
        jnp.transpose(pair[:, :, i : i + HEAD_DIM], (1, 0, 2)).reshape(k_weight.shape)
        for i in (0, HEAD_DIM)
    )

    scaled_grad = grad_normed * gain
    grad_stream = (
        inv_rms
        * (scaled_grad - unit_rows * jnp.mean(scaled_grad * unit_rows, axis=-1, keepdims=True))
        + grad_out.astype(wide)
    ).astype(low)
    return (hidden_out, grad_stream, grad_gain, grad_q, grad_k, grad_v, grad_o)


def solution(mesh):
    fine = Mesh(mesh.devices.reshape(tuple(SIZES.values())), tuple(SIZES))
    whole = P(DP + TENSOR, None)
    in_specs = (
        whole,
        P(TENSOR, DP, None),
        P(),
        P(DP, TENSOR),
        P(DP, None),
        P(DP, None),
        P(DP, TENSOR),
        whole,
        P(),
    )
    out_specs = (whole, whole, P(), P(DP, TENSOR), P(DP, None), P(DP, None), P(DP, TENSOR))
    return jax.shard_map(
        on_device, mesh=fine, in_specs=in_specs, out_specs=out_specs, check_vma=False
    )
```

profile of v0, /device:TPU:64, one launch (start us, length us, event | category | flops | bytes accessed | tf_op | source)
XLA Modules:
  0.0 379.1 jit_solution(13752440259695102105)
XLA Ops:
  7.3 1.8 pad_maximum_fusion.7
  10.6 5.5 %all-to-all-start.1 = ((bf16[4,128,256]{2,1,0:T(8,128)(2,1)}), bf16[4,128,256]{2,1,0:T(8,128)(2,1)S(1)}, u32[]{:S(2)}, u32[]{:S(2)}) async-start(bf16[4,128,256]{2,1,0:T(8,128)(2,1)} %broadcast_in_dim.18), calls=%async_computation.1 | async-start | bytes 524288 | tf_op jit(solution)/shard_map/all_to_all | solution.py:39
  17.4 4.8 %collective-permute-start = (bf16[16,4096]{1,0:T(8,128)(2,1)S(1)}, bf16[16,4096]{1,0:T(8,128)(2,1)S(1)}, u32[]{:S(2)}, u32[]{:S(2)}) collective-permute-start(bf16[16,4096]{1,0:T(8,128)(2,1)S(1)} %fusion.11), channel_id=1, source_target_pairs={{0,4},{4,0},{1,5},{5,1},{2,6},{6,2},{3,7},{7,3},{8,12},{12,8},{9,1... | collective-permute-start | bytes 393224 | tf_op jit(solution)/shard_map/ppermute | solution.py:30
  26.7 4.5 %all-to-all-start.2 = ((bf16[4,512,256]{2,1,0:T(8,128)(2,1)}), bf16[4,512,256]{2,1,0:T(8,128)(2,1)S(1)}, u32[]{:S(2)}, u32[]{:S(2)}) async-start(bf16[4,512,256]{2,1,0:T(8,128)(2,1)} %broadcast_in_dim.20), calls=%async_computation.2 | async-start | bytes 2097152 | tf_op jit(solution)/shard_map/all_to_all | solution.py:39
  32.6 14.7 %all-to-all-done.2 = bf16[4,512,256]{2,1,0:T(8,128)(2,1)S(1)} async-done(((bf16[4,512,256]{2,1,0:T(8,128)(2,1)}), bf16[4,512,256]{2,1,0:T(8,128)(2,1)S(1)}, u32[]{:S(2)}, u32[]{:S(2)}) %all-to-all-start.2) | async-done | bytes 1048608 | tf_op jit(solution)/shard_map/all_to_all | solution.py:39
  47.2 15.8 %all-to-all-start = ((bf16[32,16,256]{2,1,0:T(8,128)(2,1)}), bf16[32,16,256]{2,1,0:T(8,128)(2,1)}, u32[]{:S(2)}, u32[]{:S(2)}) async-start(bf16[32,16,256]{2,1,0:T(8,128)(2,1)} %maximum_bitcast_fusion), calls=%async_computation | async-start | bytes 524288 | tf_op jit(solution)/shard_map/all_to_all | solution.py:345
  64.0 2.8 collective-permute-start.1
  69.6 9.0 %collective-permute-done.1 = bf16[2,16,4096]{2,1,0:T(8,128)(2,1)S(1)} collective-permute-done((bf16[2,16,4096]{2,1,0:T(8,128)(2,1)S(1)}, bf16[2,16,4096]{2,1,0:T(8,128)(2,1)S(1)}, u32[]{:S(2)}, u32[]{:S(2)}) %collective-permute-start.1) | collective-permute-done | bytes 262176 | tf_op jit(solution)/shard_map/ppermute | solution.py:34
  78.6 3.7 collective-permute-done.3
  84.3 1.4 broadcast_select_fusion.1
  88.1 5.0 %all-to-all-start.3 = ((bf16[4,128,256]{2,1,0:T(8,128)(2,1)}), bf16[4,128,256]{2,1,0:T(8,128)(2,1)S(1)}, u32[]{:S(2)}, u32[]{:S(2)}) async-start(bf16[4,128,256]{2,1,0:T(8,128)(2,1)} %broadcast_in_dim.21), calls=%async_computation.3 | async-start | bytes 524288 | tf_op jit(solution)/shard_map/all_to_all | solution.py:39
  93.9 5.8 %all-to-all-done.3 = bf16[4,128,256]{2,1,0:T(8,128)(2,1)S(1)} async-done(((bf16[4,128,256]{2,1,0:T(8,128)(2,1)}), bf16[4,128,256]{2,1,0:T(8,128)(2,1)S(1)}, u32[]{:S(2)}, u32[]{:S(2)}) %all-to-all-start.3) | async-done | bytes 262176 | tf_op jit(solution)/shard_map/all_to_all | solution.py:39
  100.9 4.4 %all-to-all-start.4 = ((bf16[4,512,256]{2,1,0:T(8,128)(2,1)}), bf16[4,512,256]{2,1,0:T(8,128)(2,1)}, u32[]{:S(2)}, u32[]{:S(2)}) async-start(bf16[4,512,256]{2,1,0:T(8,128)(2,1)} %broadcast_in_dim.23), calls=%async_computation.4 | async-start | bytes 2097152 | tf_op jit(solution)/shard_map/all_to_all | solution.py:39
  105.5 1.4 fusion.3.pend
  107.4 11.9 %collective-permute-start.8 = (bf16[32,16,256]{2,1,0:T(8,128)(2,1)}, bf16[32,16,256]{2,1,0:T(8,128)(2,1)S(1)}, u32[]{:S(2)}, u32[]{:S(2)}) collective-permute-start(bf16[32,16,256]{2,1,0:T(8,128)(2,1)} %all-to-all-done), channel_id=1, source_target_pairs={{0,4},{4,0},{1,5},{5,1},{2,6},{6,2},{3,7},{7,3},{8,12},{12,8},{9,1... | collective-permute-start | bytes 786440 | tf_op jit(solution)/shard_map/ppermute | solution.py:30
  123.8 2.7 collective-permute-done.8
  126.5 1.9 fusion.43
  128.3 3.0 collective-permute-start.9
  132.3 3.8 %collective-permute-start.11 = (bf16[2,32,16,256]{3,2,0,1:T(8,128)(2,1)S(1)}, bf16[2,32,16,256]{3,2,0,1:T(8,128)(2,1)}, u32[]{:S(2)}, u32[]{:S(2)}) collective-permute-start(bf16[2,32,16,256]{3,2,0,1:T(8,128)(2,1)S(1)} %get-tuple-element.59), channel_id=1, source_target_pairs={{3,0},{0,1},{1,2},{2,3},{7,4},{4,5},{5,6},{6,7},{11,8},{8,9},{9,10... | collective-permute-start | bytes 1572872 | tf_op jit(solution)/shard_map/ppermute | solution.py:34
  136.2 2.7 copy.46.key_place
  138.8 2.3 pad_maximum_fusion.3
  141.1 6.0 %collective-permute-done.9 = bf16[2,32,16,256]{3,2,0,1:T(8,128)(2,1)S(1)} collective-permute-done((bf16[2,32,16,256]{3,2,0,1:T(8,128)(2,1)S(1)}, bf16[2,32,16,256]{3,2,0,1:T(8,128)(2,1)S(1)}, u32[]{:S(2)}, u32[]{:S(2)}) %collective-permute-start.9) | collective-permute-done | bytes 524320 | tf_op jit(solution)/shard_map/ppermute | solution.py:34
  147.1 1.6 collective-permute-done.10
  148.7 10.9 %collective-permute-done.11 = bf16[2,32,16,256]{3,2,0,1:T(8,128)(2,1)} collective-permute-done((bf16[2,32,16,256]{3,2,0,1:T(8,128)(2,1)S(1)}, bf16[2,32,16,256]{3,2,0,1:T(8,128)(2,1)}, u32[]{:S(2)}, u32[]{:S(2)}) %collective-permute-start.11) | collective-permute-done | bytes 524320 | tf_op jit(solution)/shard_map/ppermute | solution.py:34
  159.6 1.6 pad_maximum_fusion
  163.7 7.0 %shard_map.144 = (bf16[512,128]{1,0:T(8,128)(2,1)S(1)}, bf16[512,128]{1,0:T(8,128)(2,1)S(1)}) custom-call(bf16[128,4096]{1,0:T(8,128)(2,1)S(1)} %bitcast.136, bf16[128,4096]{1,0:T(8,128)(2,1)S(1)} %bitcast.137, bf16[4096,1024]{1,0:T(8,128)(2,1)} %all-gather.3.cloned.1.call-done.weights, f32[128,128]{1,0:T(8,128)S(1)} %get-tuple-element.74.cosine, ...), custom_call_target="tpu_custom_call" | custom-call | tf_op jit(solution)/shard_map/pallas_call | solution.py:115
  170.8 14.3 %shard_map.145 = (bf16[128,1024]{1,0:T(8,128)(2,1)}, bf16[2048,256]{1,0:T(8,128)(2,1)S(1)}, bf16[2048,256]{1,0:T(8,128)(2,1)S(1)}) custom-call(bf16[512,128]{1,0:T(8,128)(2,1)S(1)} %get-tuple-element.16.query, bf16[512,128]{1,0:T(8,128)(2,1)S(1)} %get-tuple-element.17.grad_heads, bf16[2048,256]{1,0:T(8,128)(2,1)} %bitcast.35.near, ...), custom_call_target="tpu_custom_call" | custom-call | tf_op jit(solution)/shard_map/pallas_call | solution.py:204
  188.4 7.8 %shard_map.146 = (bf16[128,4096]{1,0:T(8,128)(2,1)S(1)}, f32[128,4096]{1,0:T(8,128)S(1)}) custom-call(bf16[128,1024]{1,0:T(8,128)(2,1)} %get-tuple-element.18.att_gq, bf16[4096,1024]{1,0:T(8,128)(2,1)} %all-gather.3.cloned.1.call-done.weights), custom_call_target="tpu_custom_call" | custom-call | tf_op jit(solution)/shard_map/pallas_call | solution.py:226
  197.6 2.9 add_convert_fusion
  200.4 4.2 %all-to-all-start.5 = ((bf16[4,512,256]{2,1,0:T(8,128)(2,1)}), bf16[4,512,256]{2,1,0:T(8,128)(2,1)}, u32[]{:S(2)}, u32[]{:S(2)}) async-start(bf16[4,512,256]{2,1,0:T(8,128)(2,1)} %bitcast.143), calls=%async_computation.5 | async-start | bytes 2097152 | tf_op jit(solution)/shard_map/all_to_all | solution.py:51
  204.7 3.1 fusion
  207.8 20.5 %all-to-all-done.5 = bf16[4,512,256]{2,1,0:T(8,128)(2,1)} async-done(((bf16[4,512,256]{2,1,0:T(8,128)(2,1)}), bf16[4,512,256]{2,1,0:T(8,128)(2,1)}, u32[]{:S(2)}, u32[]{:S(2)}) %all-to-all-start.5) | async-done | bytes 1048608 | tf_op jit(solution)/shard_map/all_to_all | solution.py:51
  228.3 2.1 reduce_sum.59
  230.5 11.1 %all-to-all-start.6 = ((bf16[4,128,256]{2,1,0:T(8,128)(2,1)}), bf16[4,128,256]{2,1,0:T(8,128)(2,1)}, u32[]{:S(2)}, u32[]{:S(2)}) async-start(bf16[4,128,256]{2,1,0:T(8,128)(2,1)} %bitcast.151), calls=%async_computation.6 | async-start | bytes 524288 | tf_op jit(solution)/shard_map/all_to_all | solution.py:51
  241.6 2.0 slice_bitcast_fusion.6
  244.0 3.0 collective-permute-start.15
  248.1 3.0 all-to-all-done.6
  252.3 2.6 fusion.40
  254.9 1.5 multiply_reduce_fusion
  257.6 20.5 %collective-permute-start.24 = (f32[32,128]{1,0:T(8,128)S(1)}, f32[32,128]{1,0:T(8,128)S(1)}, u32[]{:S(2)}, u32[]{:S(2)}) collective-permute-start(f32[32,128]{1,0:T(8,128)S(1)} %bitcast_add_fusion), channel_id=1, source_target_pairs={{0,4},{4,0},{1,5},{5,1},{2,6},{6,2},{3,7},{7,3},{8,12},{12,8},{9,1... | collective-permute-start | bytes 49160 | tf_op jit(solution)/shard_map/ppermute | solution.py:30
  278.1 2.1 fusion.7
  280.3 3.0 collective-permute-start.26
  283.4 1.6 collective-permute-start.27
  285.7 6.5 %all-to-all-start.7 = ((bf16[4,128,256]{2,1,0:T(8,128)(2,1)}), bf16[4,128,256]{2,1,0:T(8,128)(2,1)}, u32[]{:S(2)}, u32[]{:S(2)}) async-start(bf16[4,128,256]{2,1,0:T(8,128)(2,1)} %broadcast_in_dim.24), calls=%async_computation.7 | async-start | bytes 524288 | tf_op jit(solution)/shard_map/all_to_all | solution.py:39
  293.8 3.3 collective-permute-start.20
  297.7 3.7 collective-permute-start.30
  301.4 1.6 fusion.24
  303.0 5.4 %collective-permute-start.17 = (bf16[16,4096]{1,0:T(8,128)(2,1)}, bf16[16,4096]{1,0:T(8,128)(2,1)}, u32[]{:S(2)}, u32[]{:S(2)}) collective-permute-start(bf16[16,4096]{1,0:T(8,128)(2,1)} %fusion.24), channel_id=1, source_target_pairs={{0,4},{4,0},{1,5},{5,1},{2,6},{6,2},{3,7},{7,3},{8,12},{12,8},{9,1... | collective-permute-start | bytes 393224 | tf_op jit(solution)/shard_map/ppermute | solution.py:30
  308.5 1.6 collective-permute-start.31
  310.0 2.0 broadcast_in_dim.26
  312.0 3.6 all-to-all-start.8
  316.4 1.5 collective-permute-start.33
  317.8 2.1 fusion.5
  319.9 7.5 %all-to-all-done.8 = bf16[4,512,256]{2,1,0:T(8,128)(2,1)S(1)} async-done(((bf16[4,512,256]{2,1,0:T(8,128)(2,1)}), bf16[4,512,256]{2,1,0:T(8,128)(2,1)S(1)}, u32[]{:S(2)}, u32[]{:S(2)}) %all-to-all-start.8) | async-done | bytes 1048608 | tf_op jit(solution)/shard_map/all_to_all | solution.py:39
  328.5 1.5 collective-permute-start.22
  330.6 10.6 %collective-permute-done.22 = bf16[16,4096]{1,0:T(8,128)(2,1)S(1)} collective-permute-done((bf16[16,4096]{1,0:T(8,128)(2,1)S(1)}, bf16[16,4096]{1,0:T(8,128)(2,1)S(1)}, u32[]{:S(2)}, u32[]{:S(2)}) %collective-permute-start.22) | collective-permute-done | bytes 131104 | tf_op jit(solution)/shard_map/ppermute | solution.py:30
  342.4 1.5 fusion.48
  344.2 1.8 collective-permute-start.35
  346.1 1.5 collective-permute-start.36
  350.6 2.8 collective-permute-done.37
  353.4 1.5 collective-permute-start.38
  354.9 1.8 fusion.16
  356.6 5.8 %collective-permute-done.38 = bf16[2,128,256]{2,1,0:T(8,128)(2,1)S(1)} collective-permute-done((bf16[2,128,256]{2,1,0:T(8,128)(2,1)S(1)}, bf16[2,128,256]{2,1,0:T(8,128)(2,1)S(1)}, u32[]{:S(2)}, u32[]{:S(2)}) %collective-permute-start.38) | collective-permute-done | bytes 131104 | tf_op jit(solution)/shard_map/ppermute | solution.py:30
  364.5 7.6 %shard_map.147 = (f32[128,512]{1,0:T(8,128)}, f32[128,512]{1,0:T(8,128)}) custom-call(bf16[4096,256]{1,0:T(8,128)(2,1)S(1)} %bitcast.134, bf16[4096,1024]{1,0:T(8,128)(2,1)} %all-gather.5.cloned.1.call-done.att_gq), custom_call_target="tpu_custom_call" | custom-call | tf_op jit(solution)/shard_map/pallas_call | solution.py:257
  (208 shorter events, 47.8 us)
Async XLA Ops:
  7.2 14.9 %copy-start.17 = (bf16[16,4096]{1,0:T(8,128)(2,1)S(1)}, bf16[16,4096]{1,0:T(8,128)(2,1)}, u32[]{:S(2)}) copy-start(bf16[16,4096]{1,0:T(8,128)(2,1)} %param.16) | copy-start | bytes 393220
  7.2 16.6 %copy-start.18 = (bf16[1,128,4096]{2,1,0:T(8,128)(2,1)S(1)}, bf16[1,128,4096]{2,1,0:T(8,128)(2,1)}, u32[]{:S(2)}) copy-start(bf16[1,128,4096]{2,1,0:T(8,128)(2,1)} %param.10) | copy-start | bytes 3145732
  7.2 154.1 %all-gather.3.cloned.1.call-start = ((), (), s32[]{:S(2)}) async-start(), calls=%async_computation.9 | async-start | bytes 8650752 | tf_op jit(solution)/shard_map/all_gather | solution.py:290
  10.6 15.0 %all-to-all-start.1 = ((bf16[4,128,256]{2,1,0:T(8,128)(2,1)}), bf16[4,128,256]{2,1,0:T(8,128)(2,1)S(1)}, u32[]{:S(2)}, u32[]{:S(2)}) async-start(bf16[4,128,256]{2,1,0:T(8,128)(2,1)} %broadcast_in_dim.18), calls=%async_computation.1 | async-start | bytes 524288 | tf_op jit(solution)/shard_map/all_to_all | solution.py:39
  17.4 45.9 %collective-permute-start = (bf16[16,4096]{1,0:T(8,128)(2,1)S(1)}, bf16[16,4096]{1,0:T(8,128)(2,1)S(1)}, u32[]{:S(2)}, u32[]{:S(2)}) collective-permute-start(bf16[16,4096]{1,0:T(8,128)(2,1)S(1)} %fusion.11), channel_id=1, source_target_pairs={{0,4},{4,0},{1,5},{5,1},{2,6},{6,2},{3,7},{7,3},{8,12},{12,8},{9,1... | collective-permute-start | bytes 393224 | tf_op jit(solution)/shard_map/ppermute | solution.py:30
  22.1 97.9 %collective-permute-start.4 = (bf16[16,4096]{1,0:T(8,128)(2,1)S(1)}, bf16[16,4096]{1,0:T(8,128)(2,1)}, u32[]{:S(2)}, u32[]{:S(2)}) collective-permute-start(bf16[16,4096]{1,0:T(8,128)(2,1)S(1)} %copy-done.17), channel_id=1, source_target_pairs={{0,4},{4,0},{1,5},{5,1},{2,6},{6,2},{3,7},{7,3},{8,12},{12,8},{9,1... | collective-permute-start | bytes 393224 | tf_op jit(solution)/shard_map/ppermute | solution.py:30
  25.1 80.4 %copy-start.9 = (bf16[2,4,16,4096]{3,2,0,1:T(8,128)(2,1)}, bf16[2,4,16,4096]{3,2,0,1:T(8,128)(2,1)S(1)}, u32[]{:S(2)}) copy-start(bf16[2,4,16,4096]{3,2,0,1:T(8,128)(2,1)S(1)} %reverse_select_fusion) | copy-start | bytes 3145732
  26.7 20.5 %all-to-all-start.2 = ((bf16[4,512,256]{2,1,0:T(8,128)(2,1)}), bf16[4,512,256]{2,1,0:T(8,128)(2,1)S(1)}, u32[]{:S(2)}, u32[]{:S(2)}) async-start(bf16[4,512,256]{2,1,0:T(8,128)(2,1)} %broadcast_in_dim.20), calls=%async_computation.2 | async-start | bytes 2097152 | tf_op jit(solution)/shard_map/all_to_all | solution.py:39
  47.2 40.2 %all-to-all-start = ((bf16[32,16,256]{2,1,0:T(8,128)(2,1)}), bf16[32,16,256]{2,1,0:T(8,128)(2,1)}, u32[]{:S(2)}, u32[]{:S(2)}) async-start(bf16[32,16,256]{2,1,0:T(8,128)(2,1)} %maximum_bitcast_fusion), calls=%async_computation | async-start | bytes 524288 | tf_op jit(solution)/shard_map/all_to_all | solution.py:345
  63.1 21.2 %collective-permute-start.12 = (bf16[2048,256]{1,0:T(8,128)(2,1)S(1)}, bf16[2048,256]{1,0:T(8,128)(2,1)}, u32[]{:S(2)}, u32[]{:S(2)}) collective-permute-start(bf16[2048,256]{1,0:T(8,128)(2,1)S(1)} %bitcast.141), channel_id=1, source_target_pairs={{0,8},{8,0},{1,9},{9,1},{2,10},{10,2},{3,11},{11,3},{4,12},{12,4},... | collective-permute-start | bytes 3145736 | tf_op jit(solution)/shard_map/ppermute | solution.py:30
  64.0 14.5 %collective-permute-start.1 = (bf16[2,16,4096]{2,1,0:T(8,128)(2,1)S(1)}, bf16[2,16,4096]{2,1,0:T(8,128)(2,1)S(1)}, u32[]{:S(2)}, u32[]{:S(2)}) collective-permute-start(bf16[2,16,4096]{2,1,0:T(8,128)(2,1)S(1)} %get-tuple-element.67), channel_id=1, source_target_pairs={{1,0},{2,1},{3,2},{0,3},{5,4},{6,5},{7,6},{4,7},{9,8},{10,9},{11,1... | collective-permute-start | bytes 786440 | tf_op jit(solution)/shard_map/ppermute | solution.py:34
  66.9 11.7 %collective-permute-start.2 = (bf16[2,16,4096]{2,1,0:T(8,128)(2,1)S(1)}, bf16[2,16,4096]{2,1,0:T(8,128)(2,1)S(1)}, u32[]{:S(2)}, u32[]{:S(2)}) collective-permute-start(bf16[2,16,4096]{2,1,0:T(8,128)(2,1)S(1)} %get-tuple-element.67), channel_id=1, source_target_pairs={{2,0},{3,1},{0,2},{1,3},{6,4},{7,5},{4,6},{5,7},{10,8},{11,9},{8,1... | collective-permute-start | bytes 786440 | tf_op jit(solution)/shard_map/ppermute | solution.py:34
  67.7 14.6 %collective-permute-start.3 = (bf16[2,16,4096]{2,1,0:T(8,128)(2,1)S(1)}, bf16[2,16,4096]{2,1,0:T(8,128)(2,1)S(1)}, u32[]{:S(2)}, u32[]{:S(2)}) collective-permute-start(bf16[2,16,4096]{2,1,0:T(8,128)(2,1)S(1)} %get-tuple-element.67), channel_id=1, source_target_pairs={{3,0},{0,1},{1,2},{2,3},{7,4},{4,5},{5,6},{6,7},{11,8},{8,9},{9,10... | collective-permute-start | bytes 786440 | tf_op jit(solution)/shard_map/ppermute | solution.py:34
  69.6 17.7 %copy-start.21 = (f32[128,64]{1,0:T(8,128)}, f32[128,64]{1,0:T(8,128)S(1)}, u32[]{:S(2)}) copy-start(f32[128,64]{1,0:T(8,128)S(1)} %get-tuple-element.77) | copy-start | bytes 98308
  88.1 11.6 %all-to-all-start.3 = ((bf16[4,128,256]{2,1,0:T(8,128)(2,1)}), bf16[4,128,256]{2,1,0:T(8,128)(2,1)S(1)}, u32[]{:S(2)}, u32[]{:S(2)}) async-start(bf16[4,128,256]{2,1,0:T(8,128)(2,1)} %broadcast_in_dim.21), calls=%async_computation.3 | async-start | bytes 524288 | tf_op jit(solution)/shard_map/all_to_all | solution.py:39
  100.8 22.5 %copy-start.29 = (s32[4096]{0:T(1024)S(1)}, s32[4096]{0:T(1024)}, u32[]{:S(2)}) copy-start(s32[4096]{0:T(1024)} %param.17) | copy-start | bytes 49156
  100.9 19.2 %all-to-all-start.4 = ((bf16[4,512,256]{2,1,0:T(8,128)(2,1)}), bf16[4,512,256]{2,1,0:T(8,128)(2,1)}, u32[]{:S(2)}, u32[]{:S(2)}) async-start(bf16[4,512,256]{2,1,0:T(8,128)(2,1)} %broadcast_in_dim.23), calls=%async_computation.4 | async-start | bytes 2097152 | tf_op jit(solution)/shard_map/all_to_all | solution.py:39
  105.2 259.3 %all-gather.5.cloned.1.call-start = ((), (), s32[]{:S(2)}) async-start(), calls=%async_computation.10 | async-start | bytes 8650752 | tf_op jit(solution)/shard_map/all_gather | solution.py:359
  107.4 28.7 %copy-start.31 = (s32[1,128]{1,0:T(1,128)S(1)}, s32[1,128]{1,0:T(1,128)}, u32[]{:S(2)}) copy-start(s32[1,128]{1,0:T(1,128)} %add_add_fusion.2) | copy-start | bytes 1540
  107.4 19.1 %collective-permute-start.8 = (bf16[32,16,256]{2,1,0:T(8,128)(2,1)}, bf16[32,16,256]{2,1,0:T(8,128)(2,1)S(1)}, u32[]{:S(2)}, u32[]{:S(2)}) collective-permute-start(bf16[32,16,256]{2,1,0:T(8,128)(2,1)} %all-to-all-done), channel_id=1, source_target_pairs={{0,4},{4,0},{1,5},{5,1},{2,6},{6,2},{3,7},{7,3},{8,12},{12,8},{9,1... | collective-permute-start | bytes 786440 | tf_op jit(solution)/shard_map/ppermute | solution.py:30
  120.0 50.8 %collective-permute-start.13 = (bf16[2048,256]{1,0:T(8,128)(2,1)}, bf16[2048,256]{1,0:T(8,128)(2,1)}, u32[]{:S(2)}, u32[]{:S(2)}) collective-permute-start(bf16[2048,256]{1,0:T(8,128)(2,1)} %bitcast.35.near), channel_id=1, source_target_pairs={{0,8},{8,0},{1,9},{9,1},{2,10},{10,2},{3,11},{11,3},{4,12},{12,4},... | collective-permute-start | bytes 3145736 | tf_op jit(solution)/shard_map/ppermute | solution.py:30
  121.0 10.3 %collective-permute-start.5 = (bf16[2,16,4096]{2,1,0:T(8,128)(2,1)S(1)}, bf16[2,16,4096]{2,1,0:T(8,128)(2,1)}, u32[]{:S(2)}, u32[]{:S(2)}) collective-permute-start(bf16[2,16,4096]{2,1,0:T(8,128)(2,1)S(1)} %get-tuple-element.65), channel_id=1, source_target_pairs={{1,0},{2,1},{3,2},{0,3},{5,4},{6,5},{7,6},{4,7},{9,8},{10,9},{11,1... | collective-permute-start | bytes 786440 | tf_op jit(solution)/shard_map/ppermute | solution.py:34
  121.1 11.2 %collective-permute-start.6 = (bf16[2,16,4096]{2,1,0:T(8,128)(2,1)S(1)}, bf16[2,16,4096]{2,1,0:T(8,128)(2,1)S(1)}, u32[]{:S(2)}, u32[]{:S(2)}) collective-permute-start(bf16[2,16,4096]{2,1,0:T(8,128)(2,1)S(1)} %get-tuple-element.65), channel_id=1, source_target_pairs={{2,0},{3,1},{0,2},{1,3},{6,4},{7,5},{4,6},{5,7},{10,8},{11,9},{8,1... | collective-permute-start | bytes 786440 | tf_op jit(solution)/shard_map/ppermute | solution.py:34
  122.1 16.8 %collective-permute-start.7 = (bf16[2,16,4096]{2,1,0:T(8,128)(2,1)S(1)}, bf16[2,16,4096]{2,1,0:T(8,128)(2,1)}, u32[]{:S(2)}, u32[]{:S(2)}) collective-permute-start(bf16[2,16,4096]{2,1,0:T(8,128)(2,1)S(1)} %get-tuple-element.65), channel_id=1, source_target_pairs={{3,0},{0,1},{1,2},{2,3},{7,4},{4,5},{5,6},{6,7},{11,8},{8,9},{9,10... | collective-permute-start | bytes 786440 | tf_op jit(solution)/shard_map/ppermute | solution.py:34
  128.3 18.7 %collective-permute-start.9 = (bf16[2,32,16,256]{3,2,0,1:T(8,128)(2,1)S(1)}, bf16[2,32,16,256]{3,2,0,1:T(8,128)(2,1)S(1)}, u32[]{:S(2)}, u32[]{:S(2)}) collective-permute-start(bf16[2,32,16,256]{3,2,0,1:T(8,128)(2,1)S(1)} %get-tuple-element.59), channel_id=1, source_target_pairs={{1,0},{2,1},{3,2},{0,3},{5,4},{6,5},{7,6},{4,7},{9,8},{10,9},{11,1... | collective-permute-start | bytes 1572872 | tf_op jit(solution)/shard_map/ppermute | solution.py:34
  131.3 17.4 %collective-permute-start.10 = (bf16[2,32,16,256]{3,2,0,1:T(8,128)(2,1)S(1)}, bf16[2,32,16,256]{3,2,0,1:T(8,128)(2,1)S(1)}, u32[]{:S(2)}, u32[]{:S(2)}) collective-permute-start(bf16[2,32,16,256]{3,2,0,1:T(8,128)(2,1)S(1)} %get-tuple-element.59), channel_id=1, source_target_pairs={{2,0},{3,1},{0,2},{1,3},{6,4},{7,5},{4,6},{5,7},{10,8},{11,9},{8,1... | collective-permute-start | bytes 1572872 | tf_op jit(solution)/shard_map/ppermute | solution.py:34
  132.3 27.3 %collective-permute-start.11 = (bf16[2,32,16,256]{3,2,0,1:T(8,128)(2,1)S(1)}, bf16[2,32,16,256]{3,2,0,1:T(8,128)(2,1)}, u32[]{:S(2)}, u32[]{:S(2)}) collective-permute-start(bf16[2,32,16,256]{3,2,0,1:T(8,128)(2,1)S(1)} %get-tuple-element.59), channel_id=1, source_target_pairs={{3,0},{0,1},{1,2},{2,3},{7,4},{4,5},{5,6},{6,7},{11,8},{8,9},{9,10... | collective-permute-start | bytes 1572872 | tf_op jit(solution)/shard_map/ppermute | solution.py:34
  138.8 20.8 %copy-start.15 = (bf16[1,2,32,16,256]{4,3,1,0,2:T(8,128)(2,1)S(1)}, bf16[1,2,32,16,256]{4,3,1,0,2:T(8,128)(2,1)}, u32[]{:S(2)}) copy-start(bf16[1,2,32,16,256]{4,3,1,0,2:T(8,128)(2,1)} %get-tuple-element.58) | copy-start | bytes 1572868
  147.1 12.6 %copy-start.23 = (bf16[2,32,16,256]{3,2,0,1:T(8,128)(2,1)}, bf16[2,32,16,256]{3,2,0,1:T(8,128)(2,1)S(1)}, u32[]{:S(2)}) copy-start(bf16[2,32,16,256]{3,2,0,1:T(8,128)(2,1)S(1)} %collective-permute-done.9) | copy-start | bytes 1572868
  187.2 10.4 %collective-permute-start.18 = (bf16[2048,256]{1,0:T(8,128)(2,1)}, bf16[2048,256]{1,0:T(8,128)(2,1)}, u32[]{:S(2)}, u32[]{:S(2)}) collective-permute-start(bf16[2048,256]{1,0:T(8,128)(2,1)} %copy-done.7), channel_id=1, source_target_pairs={{0,8},{8,0},{1,9},{9,1},{2,10},{10,2},{3,11},{11,3},{4,12},{12,4},... | collective-permute-start | bytes 3145736 | tf_op jit(solution)/shard_map/ppermute | solution.py:30
  200.4 27.9 %all-to-all-start.5 = ((bf16[4,512,256]{2,1,0:T(8,128)(2,1)}), bf16[4,512,256]{2,1,0:T(8,128)(2,1)}, u32[]{:S(2)}, u32[]{:S(2)}) async-start(bf16[4,512,256]{2,1,0:T(8,128)(2,1)} %bitcast.143), calls=%async_computation.5 | async-start | bytes 2097152 | tf_op jit(solution)/shard_map/all_to_all | solution.py:51
  207.8 44.4 %copy-start.22 = (f32[128,64]{1,0:T(8,128)S(1)}, f32[128,64]{1,0:T(8,128)}, u32[]{:S(2)}) copy-start(f32[128,64]{1,0:T(8,128)} %copy-done.21) | copy-start | bytes 98308
  230.5 20.6 %all-to-all-start.6 = ((bf16[4,128,256]{2,1,0:T(8,128)(2,1)}), bf16[4,128,256]{2,1,0:T(8,128)(2,1)}, u32[]{:S(2)}, u32[]{:S(2)}) async-start(bf16[4,128,256]{2,1,0:T(8,128)(2,1)} %bitcast.151), calls=%async_computation.6 | async-start | bytes 524288 | tf_op jit(solution)/shard_map/all_to_all | solution.py:51
  243.6 34.5 %collective-permute-start.14 = (bf16[2,16,4096]{2,1,0:T(8,128)(2,1)}, bf16[2,16,4096]{2,1,0:T(8,128)(2,1)}, u32[]{:S(2)}, u32[]{:S(2)}) collective-permute-start(bf16[2,16,4096]{2,1,0:T(8,128)(2,1)} %get-tuple-element.53), channel_id=1, source_target_pairs={{3,0},{0,1},{1,2},{2,3},{7,4},{4,5},{5,6},{6,7},{11,8},{8,9},{9,10... | collective-permute-start | bytes 786440 | tf_op jit(solution)/shard_map/ppermute | solution.py:34
  244.0 34.1 %collective-permute-start.15 = (bf16[2,16,4096]{2,1,0:T(8,128)(2,1)}, bf16[2,16,4096]{2,1,0:T(8,128)(2,1)}, u32[]{:S(2)}, u32[]{:S(2)}) collective-permute-start(bf16[2,16,4096]{2,1,0:T(8,128)(2,1)} %get-tuple-element.55), channel_id=1, source_target_pairs={{2,0},{3,1},{0,2},{1,3},{6,4},{7,5},{4,6},{5,7},{10,8},{11,9},{8,1... | collective-permute-start | bytes 786440 | tf_op jit(solution)/shard_map/ppermute | solution.py:34
  247.0 31.1 %collective-permute-start.16 = (bf16[2,16,4096]{2,1,0:T(8,128)(2,1)}, bf16[2,16,4096]{2,1,0:T(8,128)(2,1)}, u32[]{:S(2)}, u32[]{:S(2)}) collective-permute-start(bf16[2,16,4096]{2,1,0:T(8,128)(2,1)} %get-tuple-element.54), channel_id=1, source_target_pairs={{1,0},{2,1},{3,2},{0,3},{5,4},{6,5},{7,6},{4,7},{9,8},{10,9},{11,1... | collective-permute-start | bytes 786440 | tf_op jit(solution)/shard_map/ppermute | solution.py:34
  256.4 1.2 collective-permute-start.23
  256.4 36.4 %copy-start.12 = (bf16[128,4096]{1,0:T(8,128)(2,1)S(1)}, bf16[128,4096]{1,0:T(8,128)(2,1)}, u32[]{:S(2)}) copy-start(bf16[128,4096]{1,0:T(8,128)(2,1)} %get-tuple-element.44) | copy-start | bytes 3145732
  257.6 22.6 %collective-permute-start.24 = (f32[32,128]{1,0:T(8,128)S(1)}, f32[32,128]{1,0:T(8,128)S(1)}, u32[]{:S(2)}, u32[]{:S(2)}) collective-permute-start(f32[32,128]{1,0:T(8,128)S(1)} %bitcast_add_fusion), channel_id=1, source_target_pairs={{0,4},{4,0},{1,5},{5,1},{2,6},{6,2},{3,7},{7,3},{8,12},{12,8},{9,1... | collective-permute-start | bytes 49160 | tf_op jit(solution)/shard_map/ppermute | solution.py:30
  280.2 12.0 %collective-permute-start.25 = (f32[32,128]{1,0:T(8,128)S(1)}, f32[32,128]{1,0:T(8,128)S(1)}, u32[]{:S(2)}, u32[]{:S(2)}) collective-permute-start(f32[32,128]{1,0:T(8,128)S(1)} %fusion.56), channel_id=1, source_target_pairs={{0,1},{1,0},{2,3},{3,2},{4,5},{5,4},{6,7},{7,6},{8,9},{9,8},{10,11... | collective-permute-start | bytes 49160 | tf_op jit(solution)/shard_map/ppermute | solution.py:63
  280.3 11.9 %collective-permute-start.26 = (f32[32,128]{1,0:T(8,128)S(1)}, f32[32,128]{1,0:T(8,128)S(1)}, u32[]{:S(2)}, u32[]{:S(2)}) collective-permute-start(f32[32,128]{1,0:T(8,128)S(1)} %fusion.56), channel_id=1, source_target_pairs={{0,2},{1,3},{2,0},{3,1},{4,6},{5,7},{6,4},{7,5},{8,10},{9,11},{10,... | collective-permute-start | bytes 49160 | tf_op jit(solution)/shard_map/ppermute | solution.py:63
  283.4 8.9 %collective-permute-start.27 = (f32[32,128]{1,0:T(8,128)S(1)}, f32[32,128]{1,0:T(8,128)S(1)}, u32[]{:S(2)}, u32[]{:S(2)}) collective-permute-start(f32[32,128]{1,0:T(8,128)S(1)} %fusion.56), channel_id=1, source_target_pairs={{0,3},{1,2},{2,1},{3,0},{4,7},{5,6},{6,5},{7,4},{8,11},{9,10},{10,... | collective-permute-start | bytes 49160 | tf_op jit(solution)/shard_map/ppermute | solution.py:63
  285.7 24.3 %all-to-all-start.7 = ((bf16[4,128,256]{2,1,0:T(8,128)(2,1)}), bf16[4,128,256]{2,1,0:T(8,128)(2,1)}, u32[]{:S(2)}, u32[]{:S(2)}) async-start(bf16[4,128,256]{2,1,0:T(8,128)(2,1)} %broadcast_in_dim.24), calls=%async_computation.7 | async-start | bytes 524288 | tf_op jit(solution)/shard_map/all_to_all | solution.py:39
  292.3 5.5 %collective-permute-start.28 = (f32[32,128]{1,0:T(8,128)S(1)}, f32[32,128]{1,0:T(8,128)S(1)}, u32[]{:S(2)}, u32[]{:S(2)}) collective-permute-start(f32[32,128]{1,0:T(8,128)S(1)} %add_add_fusion.1), channel_id=1, source_target_pairs={{0,64},{64,0},{128,192},{192,128},{1,65},{65,1},{129,193},{193,129... | collective-permute-start | bytes 49160 | tf_op jit(solution)/shard_map/ppermute | solution.py:63
  293.8 21.9 %collective-permute-start.19 = (bf16[2,16,4096]{2,1,0:T(8,128)(2,1)}, bf16[2,16,4096]{2,1,0:T(8,128)(2,1)}, u32[]{:S(2)}, u32[]{:S(2)}) collective-permute-start(bf16[2,16,4096]{2,1,0:T(8,128)(2,1)} %bitcast.49), channel_id=1, source_target_pairs={{3,0},{0,1},{1,2},{2,3},{7,4},{4,5},{5,6},{6,7},{11,8},{8,9},{9,10... | collective-permute-start | bytes 786440 | tf_op jit(solution)/shard_map/ppermute | solution.py:34
  293.8 22.6 %collective-permute-start.20 = (bf16[2,16,4096]{2,1,0:T(8,128)(2,1)}, bf16[2,16,4096]{2,1,0:T(8,128)(2,1)}, u32[]{:S(2)}, u32[]{:S(2)}) collective-permute-start(bf16[2,16,4096]{2,1,0:T(8,128)(2,1)} %bitcast.50), channel_id=1, source_target_pairs={{2,0},{3,1},{0,2},{1,3},{6,4},{7,5},{4,6},{5,7},{10,8},{11,9},{8,1... | collective-permute-start | bytes 786440 | tf_op jit(solution)/shard_map/ppermute | solution.py:34
  297.1 20.7 %collective-permute-start.21 = (bf16[2,16,4096]{2,1,0:T(8,128)(2,1)}, bf16[2,16,4096]{2,1,0:T(8,128)(2,1)}, u32[]{:S(2)}, u32[]{:S(2)}) collective-permute-start(bf16[2,16,4096]{2,1,0:T(8,128)(2,1)} %bitcast.51), channel_id=1, source_target_pairs={{1,0},{2,1},{3,2},{0,3},{5,4},{6,5},{7,6},{4,7},{9,8},{10,9},{11,1... | collective-permute-start | bytes 786440 | tf_op jit(solution)/shard_map/ppermute | solution.py:34
  297.1 6.0 %collective-permute-start.29 = (f32[32,128]{1,0:T(8,128)S(1)}, f32[32,128]{1,0:T(8,128)S(1)}, u32[]{:S(2)}, u32[]{:S(2)}) collective-permute-start(f32[32,128]{1,0:T(8,128)S(1)} %add_add_fusion.1), channel_id=1, source_target_pairs={{0,128},{64,192},{128,0},{192,64},{1,129},{65,193},{129,1},{193,65... | collective-permute-start | bytes 49160 | tf_op jit(solution)/shard_map/ppermute | solution.py:63
  297.7 10.8 %collective-permute-start.30 = (f32[32,128]{1,0:T(8,128)S(1)}, f32[32,128]{1,0:T(8,128)S(1)}, u32[]{:S(2)}, u32[]{:S(2)}) collective-permute-start(f32[32,128]{1,0:T(8,128)S(1)} %add_add_fusion.1), channel_id=1, source_target_pairs={{0,192},{64,128},{128,64},{192,0},{1,193},{65,129},{129,65},{193,1... | collective-permute-start | bytes 49160 | tf_op jit(solution)/shard_map/ppermute | solution.py:63
  303.0 51.8 %collective-permute-start.17 = (bf16[16,4096]{1,0:T(8,128)(2,1)}, bf16[16,4096]{1,0:T(8,128)(2,1)}, u32[]{:S(2)}, u32[]{:S(2)}) collective-permute-start(bf16[16,4096]{1,0:T(8,128)(2,1)} %fusion.24), channel_id=1, source_target_pairs={{0,4},{4,0},{1,5},{5,1},{2,6},{6,2},{3,7},{7,3},{8,12},{12,8},{9,1... | collective-permute-start | bytes 393224 | tf_op jit(solution)/shard_map/ppermute | solution.py:30
  308.5 20.0 %collective-permute-start.31 = (f32[32,128]{1,0:T(8,128)S(1)}, f32[32,128]{1,0:T(8,128)S(1)}, u32[]{:S(2)}, u32[]{:S(2)}) collective-permute-start(f32[32,128]{1,0:T(8,128)S(1)} %add_add_fusion), channel_id=1, source_target_pairs={{0,16},{16,0},{32,48},{48,32},{1,17},{17,1},{33,49},{49,33},{2,18}... | collective-permute-start | bytes 49160 | tf_op jit(solution)/shard_map/ppermute | solution.py:63
  312.0 17.9 %copy-start.20 = (f32[4096]{0:T(1024)S(1)}, f32[4096]{0:T(1024)}, u32[]{:S(2)}) copy-start(f32[4096]{0:T(1024)} %param.11) | copy-start | bytes 49156
  312.0 15.4 %all-to-all-start.8 = ((bf16[4,512,256]{2,1,0:T(8,128)(2,1)}), bf16[4,512,256]{2,1,0:T(8,128)(2,1)S(1)}, u32[]{:S(2)}, u32[]{:S(2)}) async-start(bf16[4,512,256]{2,1,0:T(8,128)(2,1)} %broadcast_in_dim.26), calls=%async_computation.8 | async-start | bytes 2097152 | tf_op jit(solution)/shard_map/all_to_all | solution.py:39
  315.7 14.3 %collective-permute-start.32 = (f32[32,128]{1,0:T(8,128)S(1)}, f32[32,128]{1,0:T(8,128)S(1)}, u32[]{:S(2)}, u32[]{:S(2)}) collective-permute-start(f32[32,128]{1,0:T(8,128)S(1)} %add_add_fusion), channel_id=1, source_target_pairs={{0,32},{16,48},{32,0},{48,16},{1,33},{17,49},{33,1},{49,17},{2,34}... | collective-permute-start | bytes 49160 | tf_op jit(solution)/shard_map/ppermute | solution.py:63
  316.4 13.6 %collective-permute-start.33 = (f32[32,128]{1,0:T(8,128)S(1)}, f32[32,128]{1,0:T(8,128)S(1)}, u32[]{:S(2)}, u32[]{:S(2)}) collective-permute-start(f32[32,128]{1,0:T(8,128)S(1)} %add_add_fusion), channel_id=1, source_target_pairs={{0,48},{16,32},{32,16},{48,0},{1,49},{17,33},{33,17},{49,1},{2,50}... | collective-permute-start | bytes 49160 | tf_op jit(solution)/shard_map/ppermute | solution.py:63
  327.5 16.4 %copy-start.14 = (bf16[16,1,128,128]{3,2,1,0:T(8,128)(2,1)S(1)}, bf16[16,1,128,128]{3,2,1,0:T(8,128)(2,1)}, u32[]{:S(2)}) copy-start(bf16[16,1,128,128]{3,2,1,0:T(8,128)(2,1)} %get-tuple-element.47) | copy-start | bytes 1572868
  327.5 16.4 %collective-permute-start.34 = (bf16[2048,256]{1,0:T(8,128)(2,1)S(1)}, bf16[2048,256]{1,0:T(8,128)(2,1)S(1)}, u32[]{:S(2)}, u32[]{:S(2)}) collective-permute-start(bf16[2048,256]{1,0:T(8,128)(2,1)S(1)} %bitcast.145), channel_id=1, source_target_pairs={{0,8},{8,0},{1,9},{9,1},{2,10},{10,2},{3,11},{11,3},{4,12},{12,4},... | collective-permute-start | bytes 3145736 | tf_op jit(solution)/shard_map/ppermute | solution.py:30
  328.5 12.7 %collective-permute-start.22 = (bf16[16,4096]{1,0:T(8,128)(2,1)S(1)}, bf16[16,4096]{1,0:T(8,128)(2,1)S(1)}, u32[]{:S(2)}, u32[]{:S(2)}) collective-permute-start(bf16[16,4096]{1,0:T(8,128)(2,1)S(1)} %fusion.25), channel_id=1, source_target_pairs={{0,4},{4,0},{1,5},{5,1},{2,6},{6,2},{3,7},{7,3},{8,12},{12,8},{9,1... | collective-permute-start | bytes 393224 | tf_op jit(solution)/shard_map/ppermute | solution.py:30
  342.3 12.5 %copy-start.13 = (f32[2,16,4096]{2,1,0:T(8,128)S(1)}, f32[2,16,4096]{2,1,0:T(8,128)}, u32[]{:S(2)}) copy-start(f32[2,16,4096]{2,1,0:T(8,128)} %fusion.5) | copy-start | bytes 1572868
  342.4 12.5 %copy-start.16 = (f32[2,16,4096]{2,1,0:T(8,128)S(1)}, f32[2,16,4096]{2,1,0:T(8,128)}, u32[]{:S(2)}) copy-start(f32[2,16,4096]{2,1,0:T(8,128)} %fusion.7) | copy-start | bytes 1572868
  344.2 5.6 %collective-permute-start.35 = (bf16[128,256]{1,0:T(8,128)(2,1)S(1)}, bf16[128,256]{1,0:T(8,128)(2,1)S(1)}, u32[]{:S(2)}, u32[]{:S(2)}) collective-permute-start(bf16[128,256]{1,0:T(8,128)(2,1)S(1)} %fusion.1), channel_id=1, source_target_pairs={{3,0},{0,1},{1,2},{2,3},{7,4},{4,5},{5,6},{6,7},{11,8},{8,9},{9,10... | collective-permute-start | bytes 196616 | tf_op jit(solution)/shard_map/ppermute | solution.py:34
  346.1 4.5 %collective-permute-start.36 = (bf16[128,256]{1,0:T(8,128)(2,1)S(1)}, bf16[128,256]{1,0:T(8,128)(2,1)S(1)}, u32[]{:S(2)}, u32[]{:S(2)}) collective-permute-start(bf16[128,256]{1,0:T(8,128)(2,1)S(1)} %fusion.1), channel_id=1, source_target_pairs={{1,0},{2,1},{3,2},{0,3},{5,4},{6,5},{7,6},{4,7},{9,8},{10,9},{11,1... | collective-permute-start | bytes 196616 | tf_op jit(solution)/shard_map/ppermute | solution.py:34
  347.6 5.8 %collective-permute-start.37 = (bf16[128,256]{1,0:T(8,128)(2,1)S(1)}, bf16[128,256]{1,0:T(8,128)(2,1)S(1)}, u32[]{:S(2)}, u32[]{:S(2)}) collective-permute-start(bf16[128,256]{1,0:T(8,128)(2,1)S(1)} %fusion.1), channel_id=1, source_target_pairs={{2,0},{3,1},{0,2},{1,3},{6,4},{7,5},{4,6},{5,7},{10,8},{11,9},{8,1... | collective-permute-start | bytes 196616 | tf_op jit(solution)/shard_map/ppermute | solution.py:34
  353.4 9.0 %collective-permute-start.38 = (bf16[2,128,256]{2,1,0:T(8,128)(2,1)S(1)}, bf16[2,128,256]{2,1,0:T(8,128)(2,1)S(1)}, u32[]{:S(2)}, u32[]{:S(2)}) collective-permute-start(bf16[2,128,256]{2,1,0:T(8,128)(2,1)S(1)} %pad_maximum_fusion.8), channel_id=1, source_target_pairs={{0,4},{4,0},{1,5},{5,1},{2,6},{6,2},{3,7},{7,3},{8,12},{12,8},{9,1... | collective-permute-start | bytes 393224 | tf_op jit(solution)/shard_map/ppermute | solution.py:30
  (20 other events, 88.1 us)
Sparse Core Ops, SparseCore 0:
  9.9 92.0 all-gather.2
  187.3 89.1 all-gather.4
where the time goes:
time: 385 us; the launch traced here: 379 us
  starting transfers between devices  148 us (38%)
  waiting for transfers between devices  107 us (28%)
  other arithmetic  38.3 us (10%)
  Pallas kernels  36.8 us (10%)
  local copies, waits for them, and re-layouts  28.8 us (7%)
  between operations  14.9 us (4%)
  matrix products  4.92 us (1%)
    ppermute x12, starting transfers between devices, swap(): return lax.ppermute(a, axis, [(0, 1), (1, 0)])  47.1 us
    ppermute x18, waiting for transfers between devices, shift(): return lax.ppermute(a, 'x', [((i + step) % NX, i) for i in range(NX)])  35.7 us
    all_to_all x6, starting transfers between devices, spread(): lax.all_to_all(jnp.broadcast_to(a[None], (size,) + a.shape), axis, 0, 0,...  29.6 us
    all_to_all x6, waiting for transfers between devices, spread(): lax.all_to_all(jnp.broadcast_to(a[None], (size,) + a.shape), axis, 0, 0,...  28.8 us
    ppermute x18, starting transfers between devices, shift(): return lax.ppermute(a, 'x', [((i + step) % NX, i) for i in range(NX)])  27.1 us
    all_to_all x2, waiting for transfers between devices, collect(): lax.all_to_all(a, axis, 0, 0, tiled=True).astype(wide)  23.5 us
    ppermute x12, waiting for transfers between devices, swap(): return lax.ppermute(a, axis, [(0, 1), (1, 0)])  19.1 us
    all_to_all x1, starting transfers between devices, on_device(): rows = spread_tensor(lax.all_to_all(rows, DP, 0, 0, tiled=True))  15.8 us
  transfers between devices with their start and end apart: 50, of which 18 were waited for; matrix products, arithmetic and copies ran while one was open for 17% of the time, Pallas kernels for 4%

commit v1 on v0

--- a/solution.py
+++ b/solution.py
@@ -51,12 +51,6 @@
     return jnp.sum(lax.all_to_all(a, axis, 0, 0, tiled=True).astype(wide), axis=0)
 
 
-def collect_yz(a):
-    rows, cols = a.shape
-    a = collect(a.reshape(SIZES["y"], rows // SIZES["y"], cols), "y").astype(low)
-    return collect(a.reshape(SIZES["z"], a.shape[0] // SIZES["z"], cols), "z")
-
-
 def all_sum(a, axis):
     if SIZES[axis] == 2:
         return a + swap(a, axis)
@@ -84,7 +78,45 @@
 ANY = pl.BlockSpec(memory_space=pl.ANY)
 
 
-def project_kernel(normed, grads, weights, cosine, sine, rows, pend, query, grad_heads, total):
+def kv_project_kernel(both, weights, cosine, sine, rows, pend, kv, total):
+    step = pl.program_id(0)
+
+    @pl.when(step == 0)
+    def _():
+        total[...] = jnp.zeros_like(total)
+
+    total[...] += dot(both[...], weights[...], ((1,), (0,)))
+
+    @pl.when(step == pl.num_programs(0) - 1)
+    def _():
+        kv[:, :HEAD_DIM] = turn(total[:, :HEAD_DIM], cosine[...], sine[...]).astype(low)
+        kv[:, HEAD_DIM:] = total[:, HEAD_DIM:].astype(low)
+
+
+def kv_project(both, weights, cosine, sine, rows, pend, step=1024):
+    tok = both.shape[0]
+    width, cols = weights.shape
+    kv_cols = 2 * HEAD_DIM
+    fixed = pl.BlockSpec((tok, HEAD_DIM), lambda i: (0, 0))
+    return pl.pallas_call(
+        kv_project_kernel,
+        grid=(width // step,),
+        in_specs=[
+            pl.BlockSpec((tok, step), lambda i: (0, i)),
+            pl.BlockSpec((step, kv_cols), lambda i: (i, cols // kv_cols - 1)),
+            fixed,
+            fixed,
+            ANY,
+            ANY,
+        ],
+        out_specs=pl.BlockSpec((tok, kv_cols), lambda i: (0, 0)),
+        out_shape=jax.ShapeDtypeStruct((tok, kv_cols), low),
+        scratch_shapes=[pltpu.VMEM((tok, kv_cols), wide)],
+        compiler_params=PARAMS,
+    )(both, weights, cosine, sine, rows, pend)
+
+
+def project_kernel(normed, grads, weights, cosine, sine, query, grad_heads, total):
     step = pl.program_id(0)
     tok, half = normed.shape[0], weights.shape[1] // 2
 
@@ -107,28 +139,39 @@
             ].astype(low)
 
 
-def project(normed, grads, weights, cosine, sine, rows, pend, step=512):
-    tok, width = normed.shape
-    cols = weights.shape[1]
+def project(both, weights, cosine, sine, cols, step=512):
+    tok = both.shape[0]
+    width = weights.shape[0]
+    steps = width // step
     out = jax.ShapeDtypeStruct((cols // 2 // HEAD_DIM * tok, HEAD_DIM), low)
     fixed = pl.BlockSpec((tok, HEAD_DIM), lambda i: (0, 0))
     return pl.pallas_call(
         project_kernel,
-        grid=(width // step,),
+        grid=(steps,),
         in_specs=[
             pl.BlockSpec((tok, step), lambda i: (0, i)),
-            pl.BlockSpec((tok, step), lambda i: (0, i)),
+            pl.BlockSpec((tok, step), lambda i: (0, i + steps)),
             pl.BlockSpec((step, cols), lambda i: (i, 0)),
             fixed,
             fixed,
-            ANY,
-            ANY,
         ],
         out_specs=[pl.BlockSpec(out.shape, lambda i: (0, 0))] * 2,
         out_shape=[out, out],
         scratch_shapes=[pltpu.VMEM((tok, cols), wide)],
         compiler_params=PARAMS,
-    )(normed, grads, weights, cosine, sine, rows, pend)
+    )(both, both, weights, cosine, sine)
+
+
+def hold_kernel(value, other, out):
+    out[...] = value[...]
+
+
+def hold(value, other):
+    return pl.pallas_call(
+        hold_kernel,
+        in_specs=[pl.BlockSpec(memory_space=pltpu.VMEM), ANY],
+        out_shape=jax.ShapeDtypeStruct(value.shape, value.dtype),
+    )(value, other)
 
 
 def attend_kernel(
@@ -214,14 +257,14 @@
 
 
 def back_project_kernel(att_gq, weights, terms, grad):
-    half = weights.shape[1] // 2
+    half = att_gq.shape[1] // 2
     terms[...] = dot(att_gq[:, :half], weights[:, half:], ((1,), (1,))).astype(low)
     grad[...] = dot(att_gq[:, half:], weights[:, :half], ((1,), (1,)))
 
 
 def back_project(att_gq, weights, step=512):
     tok = att_gq.shape[0]
-    width, cols = weights.shape
+    width, cols = weights.shape[0], att_gq.shape[1]
     out = pl.BlockSpec((tok, step), lambda i: (0, i))
     return pl.pallas_call(
         back_project_kernel,
@@ -280,28 +323,20 @@
     q_width = q_weight.shape[1]
     seq_len = doc_ids.shape[0]
 
-    def by_core(near):
-        cols = near.shape[1]
-        far = swap(near, "c")
-        near, far = (a.reshape(outer, 1, near.shape[0] // outer, cols) for a in (near, far))
-        pair = [jnp.where(c == 0, near, far), jnp.where(c == 0, far, near)]
-        return jnp.concatenate(pair, axis=1).reshape(-1, cols)
-
+    kv_first = tens_index * (q_width // HEAD_DIM) // (HEADS // KV_HEADS) * HEAD_DIM
+    kv_weights = [
+        lax.dynamic_slice_in_dim(w, kv_first, HEAD_DIM, 1) for w in (k_weight, v_weight)
+    ]
     weights = lax.all_gather(
-        jnp.concatenate([q_weight, out_weight], axis=1), DP, axis=0, tiled=True
-    )
-
-    kv_first = tens_index * (q_width // HEAD_DIM) // (HEADS // KV_HEADS) * HEAD_DIM
-    kv_weight = jnp.concatenate(
-        [lax.dynamic_slice_in_dim(w, kv_first, HEAD_DIM, 1) for w in (k_weight, v_weight)], axis=1
-    )
-    wkv = by_core(spread_yz(kv_weight))
+        jnp.concatenate([q_weight, out_weight] + kv_weights, axis=1), DP, axis=0, tiled=True
+    )
 
     stream_f = stream_in.astype(wide)
     inv_rms = lax.rsqrt(jnp.mean(stream_f * stream_f, axis=-1, keepdims=True) + eps)
     unit_rows = stream_f * inv_rms
     normed_own = (unit_rows * gain).astype(low)
-    normed = spread_tensor(normed_own).reshape(tok, width)
+    both = jnp.concatenate([normed_own, grad_out], axis=1)
+    both = spread_tensor(both).reshape(tok, 2 * width)
 
     def index(axis):
         return lax.broadcasted_iota(jnp.int32, (NX, 2, rows_own), axis)
@@ -331,14 +366,6 @@
     def rotate(field, sign):
         flipped = jnp.concatenate([field[:, HALF_DIM:], field[:, :HALF_DIM]], axis=1)
         return field * cosine + sign * flipped * sine
-
-    kv_proj = dot(normed, wkv, ((1,), (0,)))
-    keys_own = rotate(kv_proj[:, :HEAD_DIM], 1.0)
-    kv_own = jnp.concatenate([keys_own, kv_proj[:, HEAD_DIM:]], axis=1).astype(low)
-    kv_near = spread_yz(kv_own)
-    kv_far = swap(kv_near, "c")
-
-    grads = spread_tensor(grad_out).reshape(tok, width)
 
     split = [a.reshape(rows_own, n_dp, block) for a in (grad_out, normed_own)]
     rows = jnp.transpose(jnp.concatenate(split, axis=2), (1, 0, 2))
@@ -351,15 +378,19 @@
     )
     pend = relative(pending[0])
 
-    query, grad_heads = project(normed, grads, weights, cosine, sine, rows, pend)
+    kv_own = kv_project(both, weights, cosine, sine, rows, pend)
+    kv_near = spread_yz(kv_own)
+    kv_far = swap(kv_near, "c")
+    query, grad_heads = project(both, weights, cosine, sine, 2 * q_width)
     bounds = jnp.stack([places, first_place])
     att_gq, near_piece, far_piece = attend(
         query, grad_heads, kv_near, kv_far, key_place, bounds, cosine, sine
     )
-    att_gq_all = lax.all_gather(att_gq, DP, axis=0, tiled=True)
-
     kv_sum = near_piece.astype(wide) + swap(far_piece, "c").astype(wide)
-    kv_grad = collect_yz(kv_sum.astype(low))
+    kv_sum = kv_sum.astype(low).reshape(SIZES["y"], -1, 2 * HEAD_DIM)
+    kv_sum = collect(kv_sum, "y").astype(low)
+    att_gq_all = lax.all_gather(hold(att_gq, kv_sum), DP, axis=0, tiled=True)
+    kv_grad = collect(kv_sum.reshape(SIZES["z"], tok, 2 * HEAD_DIM), "z")
     grad_key = rotate(kv_grad[:, :HEAD_DIM], -1.0)
     grad_kv = jnp.concatenate([grad_key, kv_grad[:, HEAD_DIM:]], axis=1).astype(low)
 
@@ -371,9 +402,10 @@
     terms = terms.reshape(NX, 2, rows_own, width).astype(wide) + pend.astype(wide)
     hidden_out = (stream_f + collect_tensor(terms.astype(low))).astype(low)
 
+    wkv = weights[:, 2 * q_width :]
     normed_terms = query_terms + dot(grad_kv, wkv, ((1,), (1,)))
     grad_normed = collect_tensor(normed_terms.astype(low).reshape(NX, 2, rows_own, width))
-    gain_sum = jnp.sum(normed_terms * normed.astype(wide), axis=0).reshape(n_dp, block)
+    gain_sum = jnp.sum(normed_terms * both[:, :width].astype(wide), axis=0).reshape(n_dp, block)
     for axis in ("c", "h", "x", "y", "z"):
         gain_sum = all_sum(gain_sum, axis)
     grad_gain = gain_sum.reshape(width) / gain

time: 385 us -> 327 us (0.85)
  the two profiles are of different devices: /device:TPU:64 before, /device:TPU:32 now
where the time goes in v1:
time: 327 us; the launch traced here: 324 us
  waiting for transfers between devices  105 us (32%)
  starting transfers between devices  86 us (26%)
  Pallas kernels  40.6 us (12%)
  blocking collectives  30.1 us (9%)
  other arithmetic  23.6 us (7%)
  local copies, waits for them, and re-layouts  20.4 us (6%)
  between operations  14.7 us (4%)
  matrix products  3.33 us (1%)
    ppermute x10, waiting for transfers between devices, swap(): return lax.ppermute(a, axis, [(0, 1), (1, 0)])  40.8 us
    ppermute x10, starting transfers between devices, swap(): return lax.ppermute(a, axis, [(0, 1), (1, 0)])  27.6 us
    all_to_all x3, waiting for transfers between devices, spread(): lax.all_to_all(jnp.broadcast_to(a[None], (size,) + a.shape), axis, 0, 0,...  23.2 us
    ppermute x15, starting transfers between devices, shift(): return lax.ppermute(a, 'x', [((i + step) % NX, i) for i in range(NX)])  22.5 us
    ppermute x15, waiting for transfers between devices, shift(): return lax.ppermute(a, 'x', [((i + step) % NX, i) for i in range(NX)])  20.8 us
    all_to_all x1, blocking collectives, collect(): lax.all_to_all(a, axis, 0, 0, tiled=True).astype(wide)  18.3 us
    pallas_call x1, Pallas kernels, attend(): pl.pallas_call(attend_kernel, out_shape=[jax.ShapeDtypeStruct((tok, 2 * r...  13.3 us
    ppermute x9, starting transfers between devices, all_sum(): lax.ppermute(a, axis, [(i, i ^ k) for i in range(4)])  13.1 us
  transfers between devices with their start and end apart: 41, of which 19 were waited for; matrix products, arithmetic and copies ran while one was open for 11% of the time, Pallas kernels for 5%

profile of v1, /device:TPU:32, one launch (start us, length us, event | category | flops | bytes accessed | tf_op | source)
XLA Modules:
  0.0 324.2 jit_solution(4730737283585597566)
XLA Ops:
  8.2 1.8 pad_maximum_fusion.4
  12.0 1.6 fusion.40
  13.7 6.3 %collective-permute-start = (bf16[16,8192]{1,0:T(8,128)(2,1)}, bf16[16,8192]{1,0:T(8,128)(2,1)}, u32[]{:S(2)}, u32[]{:S(2)}) collective-permute-start(bf16[16,8192]{1,0:T(8,128)(2,1)} %get-tuple-element.63), channel_id=1, source_target_pairs={{0,4},{4,0},{1,5},{5,1},{2,6},{6,2},{3,7},{7,3},{8,12},{12,8},{9,1... | collective-permute-start | bytes 786440 | tf_op jit(solution)/shard_map/ppermute | solution.py:30
  20.8 7.0 %all-to-all-start = ((bf16[32,16,256]{2,1,0:T(8,128)(2,1)}), bf16[32,16,256]{2,1,0:T(8,128)(2,1)}, u32[]{:S(2)}, u32[]{:S(2)}) async-start(bf16[32,16,256]{2,1,0:T(8,128)(2,1)} %maximum_bitcast_fusion), calls=%async_computation | async-start | bytes 524288 | tf_op jit(solution)/shard_map/all_to_all | solution.py:372
  30.1 8.1 %collective-permute-done = bf16[16,8192]{1,0:T(8,128)(2,1)} collective-permute-done((bf16[16,8192]{1,0:T(8,128)(2,1)}, bf16[16,8192]{1,0:T(8,128)(2,1)}, u32[]{:S(2)}, u32[]{:S(2)}) %collective-permute-start) | collective-permute-done | bytes 262176 | tf_op jit(solution)/shard_map/ppermute | solution.py:30
  38.1 1.8 fusion.42
  40.0 1.5 collective-permute-start.3
  41.5 2.7 collective-permute-start.2
  44.2 1.4 collective-permute-start.1
  45.6 7.1 %collective-permute-start.4 = (bf16[32,16,256]{2,1,0:T(8,128)(2,1)}, bf16[32,16,256]{2,1,0:T(8,128)(2,1)S(1)}, u32[]{:S(2)}, u32[]{:S(2)}) collective-permute-start(bf16[32,16,256]{2,1,0:T(8,128)(2,1)} %all-to-all-done), channel_id=1, source_target_pairs={{0,4},{4,0},{1,5},{5,1},{2,6},{6,2},{3,7},{7,3},{8,12},{12,8},{9,1... | collective-permute-start | bytes 786440 | tf_op jit(solution)/shard_map/ppermute | solution.py:30
  53.2 16.2 %collective-permute-done.4 = bf16[32,16,256]{2,1,0:T(8,128)(2,1)S(1)} collective-permute-done((bf16[32,16,256]{2,1,0:T(8,128)(2,1)}, bf16[32,16,256]{2,1,0:T(8,128)(2,1)S(1)}, u32[]{:S(2)}, u32[]{:S(2)}) %collective-permute-start.4) | collective-permute-done | bytes 262176 | tf_op jit(solution)/shard_map/ppermute | solution.py:30
  70.4 1.1 collective-permute-start.7
  71.5 2.1 collective-permute-start.6
  73.6 1.4 collective-permute-start.5
  75.8 1.7 pad_maximum_fusion
  77.5 6.7 %collective-permute-done.7 = bf16[2,32,16,256]{3,2,0,1:T(8,128)(2,1)S(1)} collective-permute-done((bf16[2,32,16,256]{3,2,0,1:T(8,128)(2,1)S(1)}, bf16[2,32,16,256]{3,2,0,1:T(8,128)(2,1)S(1)}, u32[]{:S(2)}, u32[]{:S(2)}) %collective-permute-start.7) | collective-permute-done | bytes 524320 | tf_op jit(solution)/shard_map/ppermute | solution.py:34
  84.2 9.5 %collective-permute-done.6 = bf16[2,32,16,256]{3,2,0,1:T(8,128)(2,1)S(1)} collective-permute-done((bf16[2,32,16,256]{3,2,0,1:T(8,128)(2,1)S(1)}, bf16[2,32,16,256]{3,2,0,1:T(8,128)(2,1)S(1)}, u32[]{:S(2)}, u32[]{:S(2)}) %collective-permute-start.6) | collective-permute-done | bytes 524320 | tf_op jit(solution)/shard_map/ppermute | solution.py:34
  93.7 1.6 pad_maximum_fusion.1
  95.3 10.2 %all-gather.3.cloned.1.call-done.weights = bf16[4096,1280]{1,0:T(8,128)(2,1)} async-done(((bf16[128,1280]{1,0:T(8,128)(2,1)}), bf16[4096,1280]{1,0:T(8,128)(2,1)}) %all-gather.3.cloned.1.call-update) | async-done | bytes 10485776 | tf_op jit(solution)/shard_map/all_gather | solution.py:330
  105.5 1.6 copy-done
  107.1 3.0 shard_map.145
  110.2 11.8 %all_to_all.35 = bf16[4,128,256]{2,1,0:T(8,128)(2,1)S(1)} all-to-all(bf16[4,128,256]{2,1,0:T(8,128)(2,1)S(1)} %broadcast_in_dim.12), channel_id=1, replica_groups=mesh['y'=4,'z'=4,'c'=2,'h'=2,'x'=4] {'z'}, dimensions={0} | all-to-all | bytes 524288 | tf_op jit(solution)/shard_map/all_to_all | solution.py:39
  123.1 3.6 %all-to-all-start.2 = ((bf16[4,512,256]{2,1,0:T(8,128)(2,1)}), bf16[4,512,256]{2,1,0:T(8,128)(2,1)S(1)}, u32[]{:S(2)}, u32[]{:S(2)}) async-start(bf16[4,512,256]{2,1,0:T(8,128)(2,1)} %broadcast_in_dim.14), calls=%async_computation.2 | async-start | bytes 2097152 | tf_op jit(solution)/shard_map/all_to_all | solution.py:39
  126.8 14.3 %all-to-all-done.2 = bf16[4,512,256]{2,1,0:T(8,128)(2,1)S(1)} async-done(((bf16[4,512,256]{2,1,0:T(8,128)(2,1)}), bf16[4,512,256]{2,1,0:T(8,128)(2,1)S(1)}, u32[]{:S(2)}, u32[]{:S(2)}) %all-to-all-start.2) | async-done | bytes 1048608 | tf_op jit(solution)/shard_map/all_to_all | solution.py:39
  141.4 2.1 copy.46.key_place
  144.3 7.1 %shard_map.144 = (bf16[512,128]{1,0:T(8,128)(2,1)S(1)}, bf16[512,128]{1,0:T(8,128)(2,1)S(1)}) custom-call(bf16[128,8192]{1,0:T(8,128)(2,1)S(1)} %bitcast.116, bf16[128,8192]{1,0:T(8,128)(2,1)S(1)} %bitcast.117, bf16[4096,1280]{1,0:T(8,128)(2,1)} %all-gather.3.cloned.1.call-done.weights, f32[128,128]{1,0:T(8,128)S(1)} %get-tuple-element.73.cosine, ...), custom_call_target="tpu_custom_call" | custom-call | tf_op jit(solution)/shard_map/pallas_call | solution.py:148
  151.4 13.3 %shard_map.146 = (bf16[128,1024]{1,0:T(8,128)(2,1)S(1)}, bf16[2048,256]{1,0:T(8,128)(2,1)S(1)}, bf16[2048,256]{1,0:T(8,128)(2,1)S(1)}) custom-call(bf16[512,128]{1,0:T(8,128)(2,1)S(1)} %get-tuple-element.16.query, bf16[512,128]{1,0:T(8,128)(2,1)S(1)} %get-tuple-element.17.grad_heads, bf16[2048,256]{1,0:T(8,128)(2,1)S(1)} %bitcast.123, ...), custom_call_target="tpu_custom_call" | custom-call | tf_op jit(solution)/shard_map/pallas_call | solution.py:247
  165.3 2.3 collective-permute-done.13
  167.9 18.3 %all_to_all.36 = bf16[4,512,256]{2,1,0:T(8,128)(2,1)S(1)} all-to-all(bf16[4,512,256]{2,1,0:T(8,128)(2,1)S(1)} %bitcast.125), channel_id=1, replica_groups=mesh['y'=4,'z'=4,'c'=2,'h'=2,'x'=4] {'y'}, dimensions={0} | all-to-all | bytes 2097152 | tf_op jit(solution)/shard_map/all_to_all | solution.py:51
  187.1 1.7 shard_map.148
  188.8 2.4 slice.111
  191.2 7.9 %shard_map.147 = (bf16[128,4096]{1,0:T(8,128)(2,1)S(1)}, f32[128,4096]{1,0:T(8,128)S(1)}) custom-call(bf16[128,1024]{1,0:T(8,128)(2,1)S(1)} %copy-done.5, bf16[4096,1280]{1,0:T(8,128)(2,1)} %all-gather.3.cloned.1.call-done.weights), custom_call_target="tpu_custom_call" | custom-call | tf_op jit(solution)/shard_map/pallas_call | solution.py:269
  199.2 1.4 copy-done.2
  201.2 5.1 %all-to-all-start.4 = ((bf16[4,128,256]{2,1,0:T(8,128)(2,1)}), bf16[4,128,256]{2,1,0:T(8,128)(2,1)S(1)}, u32[]{:S(2)}, u32[]{:S(2)}) async-start(bf16[4,128,256]{2,1,0:T(8,128)(2,1)} %bitcast.35), calls=%async_computation.4 | async-start | bytes 524288 | tf_op jit(solution)/shard_map/all_to_all | solution.py:51
  207.1 2.9 collective-permute-start.11
  210.3 1.3 collective-permute-start.9
  211.6 6.2 %all-to-all-done.4 = bf16[4,128,256]{2,1,0:T(8,128)(2,1)S(1)} async-done(((bf16[4,128,256]{2,1,0:T(8,128)(2,1)}), bf16[4,128,256]{2,1,0:T(8,128)(2,1)S(1)}, u32[]{:S(2)}, u32[]{:S(2)}) %all-to-all-start.4) | async-done | bytes 262176 | tf_op jit(solution)/shard_map/all_to_all | solution.py:51
  218.1 2.6 fusion
  221.9 1.1 constant_dynamic-slice_fusion
  223.0 2.3 collective-permute-start.19
  225.3 1.2 fusion.9
  226.6 4.5 %collective-permute-done.19 = f32[32,128]{1,0:T(8,128)S(1)} collective-permute-done((f32[32,128]{1,0:T(8,128)S(1)}, f32[32,128]{1,0:T(8,128)S(1)}, u32[]{:S(2)}, u32[]{:S(2)}) %collective-permute-start.19) | collective-permute-done | bytes 16416 | tf_op jit(solution)/shard_map/ppermute | solution.py:30
  231.1 3.1 collective-permute-start.21
  236.4 2.8 collective-permute-done.22
  239.3 2.1 collective-permute-start.16
  243.1 3.4 %all-to-all-start.5 = ((bf16[4,128,256]{2,1,0:T(8,128)(2,1)}), bf16[4,128,256]{2,1,0:T(8,128)(2,1)S(1)}, u32[]{:S(2)}, u32[]{:S(2)}) async-start(bf16[4,128,256]{2,1,0:T(8,128)(2,1)} %broadcast_in_dim.15), calls=%async_computation.5 | async-start | bytes 524288 | tf_op jit(solution)/shard_map/all_to_all | solution.py:39
  246.5 2.6 collective-permute-start.25
  251.6 2.2 collective-permute-start.12
  254.4 2.4 collective-permute-start.27
  256.8 2.2 all-to-all-done.5
  260.0 3.6 %all-to-all-start.6 = ((bf16[4,512,256]{2,1,0:T(8,128)(2,1)}), bf16[4,512,256]{2,1,0:T(8,128)(2,1)S(1)}, u32[]{:S(2)}, u32[]{:S(2)}) async-start(bf16[4,512,256]{2,1,0:T(8,128)(2,1)} %broadcast_in_dim.17), calls=%async_computation.6 | async-start | bytes 2097152 | tf_op jit(solution)/shard_map/all_to_all | solution.py:39
  264.4 2.6 collective-permute-start.26
  268.1 6.7 %all-to-all-done.6 = bf16[4,512,256]{2,1,0:T(8,128)(2,1)S(1)} async-done(((bf16[4,512,256]{2,1,0:T(8,128)(2,1)}), bf16[4,512,256]{2,1,0:T(8,128)(2,1)S(1)}, u32[]{:S(2)}, u32[]{:S(2)}) %all-to-all-start.6) | async-done | bytes 1048608 | tf_op jit(solution)/shard_map/all_to_all | solution.py:39
  274.9 4.9 %collective-permute-start.17 = (bf16[16,4096]{1,0:T(8,128)(2,1)S(1)}, bf16[16,4096]{1,0:T(8,128)(2,1)S(1)}, u32[]{:S(2)}, u32[]{:S(2)}) collective-permute-start(bf16[16,4096]{1,0:T(8,128)(2,1)S(1)} %fusion.27), channel_id=1, source_target_pairs={{0,4},{4,0},{1,5},{5,1},{2,6},{6,2},{3,7},{7,3},{8,12},{12,8},{9,1... | collective-permute-start | bytes 393224 | tf_op jit(solution)/shard_map/ppermute | solution.py:30
  279.8 1.4 bitcast_divide_fusion
  281.2 6.5 %collective-permute-done.17 = bf16[16,4096]{1,0:T(8,128)(2,1)S(1)} collective-permute-done((bf16[16,4096]{1,0:T(8,128)(2,1)S(1)}, bf16[16,4096]{1,0:T(8,128)(2,1)S(1)}, u32[]{:S(2)}, u32[]{:S(2)}) %collective-permute-start.17) | collective-permute-done | bytes 131104 | tf_op jit(solution)/shard_map/ppermute | solution.py:30
  289.3 2.7 collective-permute-start.32
  292.0 1.1 collective-permute-start.31
  294.0 1.6 collective-permute-done.32
  296.2 2.3 collective-permute-done.30
  298.6 4.1 %collective-permute-start.33 = (bf16[2,128,256]{2,1,0:T(8,128)(2,1)S(1)}, bf16[2,128,256]{2,1,0:T(8,128)(2,1)S(1)}, u32[]{:S(2)}, u32[]{:S(2)}) collective-permute-start(bf16[2,128,256]{2,1,0:T(8,128)(2,1)S(1)} %pad_maximum_fusion.6), channel_id=1, source_target_pairs={{0,4},{4,0},{1,5},{5,1},{2,6},{6,2},{3,7},{7,3},{8,12},{12,8},{9,1... | collective-permute-start | bytes 393224 | tf_op jit(solution)/shard_map/ppermute | solution.py:30
  302.8 1.8 fusion.18
  304.5 3.2 collective-permute-done.33
  309.8 7.6 %shard_map.149 = (f32[128,512]{1,0:T(8,128)}, f32[128,512]{1,0:T(8,128)}) custom-call(bf16[4096,256]{1,0:T(8,128)(2,1)S(1)} %bitcast.121, bf16[4096,1024]{1,0:T(8,128)(2,1)} %all-gather.5.cloned.1.call-done.att_gq), custom_call_target="tpu_custom_call" | custom-call | tf_op jit(solution)/shard_map/pallas_call | solution.py:300
  (164 shorter events, 30.8 us)
Async XLA Ops:
  7.2 12.8 %copy-start.9 = (bf16[16,4096]{1,0:T(8,128)(2,1)S(1)}, bf16[16,4096]{1,0:T(8,128)(2,1)}, u32[]{:S(2)}) copy-start(bf16[16,4096]{1,0:T(8,128)(2,1)} %param.9) | copy-start | bytes 393220
  7.2 12.8 %copy-start.21 = (f32[4096]{0:T(1024)S(1)}, f32[4096]{0:T(1024)}, u32[]{:S(2)}) copy-start(f32[4096]{0:T(1024)} %param.11) | copy-start | bytes 49156
  7.2 12.8 %copy-start.16 = (bf16[16,4096]{1,0:T(8,128)(2,1)S(1)}, bf16[16,4096]{1,0:T(8,128)(2,1)}, u32[]{:S(2)}) copy-start(bf16[16,4096]{1,0:T(8,128)(2,1)} %param.16) | copy-start | bytes 393220
  7.2 20.7 %copy-start.18 = (bf16[1,128,4096]{2,1,0:T(8,128)(2,1)S(1)}, bf16[1,128,4096]{2,1,0:T(8,128)(2,1)}, u32[]{:S(2)}) copy-start(bf16[1,128,4096]{2,1,0:T(8,128)(2,1)} %param.10) | copy-start | bytes 3145732
  7.2 98.3 %all-gather.3.cloned.1.call-start = ((), (), s32[]{:S(2)}) async-start(), calls=%async_computation.7 | async-start | bytes 10813440 | tf_op jit(solution)/shard_map/all_gather | solution.py:330
  11.0 16.9 %copy-start.23 = (f32[16]{0:T(128)}, f32[16]{0:T(128)S(1)}, u32[]{:S(2)}) copy-start(f32[16]{0:T(128)S(1)} %add_rsqrt_fusion) | copy-start | bytes 196
  13.7 24.5 %collective-permute-start = (bf16[16,8192]{1,0:T(8,128)(2,1)}, bf16[16,8192]{1,0:T(8,128)(2,1)}, u32[]{:S(2)}, u32[]{:S(2)}) collective-permute-start(bf16[16,8192]{1,0:T(8,128)(2,1)} %get-tuple-element.63), channel_id=1, source_target_pairs={{0,4},{4,0},{1,5},{5,1},{2,6},{6,2},{3,7},{7,3},{8,12},{12,8},{9,1... | collective-permute-start | bytes 786440 | tf_op jit(solution)/shard_map/ppermute | solution.py:30
  20.8 24.8 %all-to-all-start = ((bf16[32,16,256]{2,1,0:T(8,128)(2,1)}), bf16[32,16,256]{2,1,0:T(8,128)(2,1)}, u32[]{:S(2)}, u32[]{:S(2)}) async-start(bf16[32,16,256]{2,1,0:T(8,128)(2,1)} %maximum_bitcast_fusion), calls=%async_computation | async-start | bytes 524288 | tf_op jit(solution)/shard_map/all_to_all | solution.py:372
  40.0 33.6 %collective-permute-start.3 = (bf16[2,16,8192]{2,1,0:T(8,128)(2,1)S(1)}, bf16[2,16,8192]{2,1,0:T(8,128)(2,1)S(1)}, u32[]{:S(2)}, u32[]{:S(2)}) collective-permute-start(bf16[2,16,8192]{2,1,0:T(8,128)(2,1)S(1)} %get-tuple-element.57), channel_id=1, source_target_pairs={{3,0},{0,1},{1,2},{2,3},{7,4},{4,5},{5,6},{6,7},{11,8},{8,9},{9,10... | collective-permute-start | bytes 1572872 | tf_op jit(solution)/shard_map/ppermute | solution.py:34
  41.5 33.6 %collective-permute-start.2 = (bf16[2,16,8192]{2,1,0:T(8,128)(2,1)S(1)}, bf16[2,16,8192]{2,1,0:T(8,128)(2,1)S(1)}, u32[]{:S(2)}, u32[]{:S(2)}) collective-permute-start(bf16[2,16,8192]{2,1,0:T(8,128)(2,1)S(1)} %get-tuple-element.57), channel_id=1, source_target_pairs={{2,0},{3,1},{0,2},{1,3},{6,4},{7,5},{4,6},{5,7},{10,8},{11,9},{8,1... | collective-permute-start | bytes 1572872 | tf_op jit(solution)/shard_map/ppermute | solution.py:34
  44.2 30.8 %collective-permute-start.1 = (bf16[2,16,8192]{2,1,0:T(8,128)(2,1)S(1)}, bf16[2,16,8192]{2,1,0:T(8,128)(2,1)}, u32[]{:S(2)}, u32[]{:S(2)}) collective-permute-start(bf16[2,16,8192]{2,1,0:T(8,128)(2,1)S(1)} %get-tuple-element.57), channel_id=1, source_target_pairs={{1,0},{2,1},{3,2},{0,3},{5,4},{6,5},{7,6},{4,7},{9,8},{10,9},{11,1... | collective-permute-start | bytes 1572872 | tf_op jit(solution)/shard_map/ppermute | solution.py:34
  45.6 30.2 %copy-start.13 = (bf16[1,2,16,8192]{3,2,1,0:T(8,128)(2,1)S(1)}, bf16[1,2,16,8192]{3,2,1,0:T(8,128)(2,1)}, u32[]{:S(2)}) copy-start(bf16[1,2,16,8192]{3,2,1,0:T(8,128)(2,1)} %get-tuple-element.56) | copy-start | bytes 1572868
  45.6 23.8 %collective-permute-start.4 = (bf16[32,16,256]{2,1,0:T(8,128)(2,1)}, bf16[32,16,256]{2,1,0:T(8,128)(2,1)S(1)}, u32[]{:S(2)}, u32[]{:S(2)}) collective-permute-start(bf16[32,16,256]{2,1,0:T(8,128)(2,1)} %all-to-all-done), channel_id=1, source_target_pairs={{0,4},{4,0},{1,5},{5,1},{2,6},{6,2},{3,7},{7,3},{8,12},{12,8},{9,1... | collective-permute-start | bytes 786440 | tf_op jit(solution)/shard_map/ppermute | solution.py:30
  70.4 13.8 %collective-permute-start.7 = (bf16[2,32,16,256]{3,2,0,1:T(8,128)(2,1)S(1)}, bf16[2,32,16,256]{3,2,0,1:T(8,128)(2,1)S(1)}, u32[]{:S(2)}, u32[]{:S(2)}) collective-permute-start(bf16[2,32,16,256]{3,2,0,1:T(8,128)(2,1)S(1)} %get-tuple-element.55), channel_id=1, source_target_pairs={{3,0},{0,1},{1,2},{2,3},{7,4},{4,5},{5,6},{6,7},{11,8},{8,9},{9,10... | collective-permute-start | bytes 1572872 | tf_op jit(solution)/shard_map/ppermute | solution.py:34
  71.5 22.2 %collective-permute-start.6 = (bf16[2,32,16,256]{3,2,0,1:T(8,128)(2,1)S(1)}, bf16[2,32,16,256]{3,2,0,1:T(8,128)(2,1)S(1)}, u32[]{:S(2)}, u32[]{:S(2)}) collective-permute-start(bf16[2,32,16,256]{3,2,0,1:T(8,128)(2,1)S(1)} %get-tuple-element.55), channel_id=1, source_target_pairs={{2,0},{3,1},{0,2},{1,3},{6,4},{7,5},{4,6},{5,7},{10,8},{11,9},{8,1... | collective-permute-start | bytes 1572872 | tf_op jit(solution)/shard_map/ppermute | solution.py:34
  73.6 1.4 copy-start.19
  73.6 20.1 %collective-permute-start.5 = (bf16[2,32,16,256]{3,2,0,1:T(8,128)(2,1)S(1)}, bf16[2,32,16,256]{3,2,0,1:T(8,128)(2,1)S(1)}, u32[]{:S(2)}, u32[]{:S(2)}) collective-permute-start(bf16[2,32,16,256]{3,2,0,1:T(8,128)(2,1)S(1)} %get-tuple-element.55), channel_id=1, source_target_pairs={{1,0},{2,1},{3,2},{0,3},{5,4},{6,5},{7,6},{4,7},{9,8},{10,9},{11,1... | collective-permute-start | bytes 1572872 | tf_op jit(solution)/shard_map/ppermute | solution.py:34
  105.5 1.6 copy-start
  123.1 20.5 %copy-start.22 = (s32[4096]{0:T(1024)S(1)}, s32[4096]{0:T(1024)}, u32[]{:S(2)}) copy-start(s32[4096]{0:T(1024)} %param.17) | copy-start | bytes 49156
  123.1 18.0 %all-to-all-start.2 = ((bf16[4,512,256]{2,1,0:T(8,128)(2,1)}), bf16[4,512,256]{2,1,0:T(8,128)(2,1)S(1)}, u32[]{:S(2)}, u32[]{:S(2)}) async-start(bf16[4,512,256]{2,1,0:T(8,128)(2,1)} %broadcast_in_dim.14), calls=%async_computation.2 | async-start | bytes 2097152 | tf_op jit(solution)/shard_map/all_to_all | solution.py:39
  126.7 183.1 %all-gather.5.cloned.1.call-start = ((), (), s32[]{:S(2)}) async-start(), calls=%async_computation.8 | async-start | bytes 8650752 | tf_op jit(solution)/shard_map/all_gather | solution.py:392
  141.1 10.3 %collective-permute-start.8 = (bf16[2048,256]{1,0:T(8,128)(2,1)S(1)}, bf16[2048,256]{1,0:T(8,128)(2,1)}, u32[]{:S(2)}, u32[]{:S(2)}) collective-permute-start(bf16[2048,256]{1,0:T(8,128)(2,1)S(1)} %bitcast.122), channel_id=1, source_target_pairs={{0,8},{8,0},{1,9},{9,1},{2,10},{10,2},{3,11},{11,3},{4,12},{12,4},... | collective-permute-start | bytes 3145736 | tf_op jit(solution)/shard_map/ppermute | solution.py:30
  164.7 3.2 copy-start.4
  164.7 2.9 collective-permute-start.13
  186.2 5.0 %copy-start.5 = (bf16[128,1024]{1,0:T(8,128)(2,1)S(1)}, bf16[128,1024]{1,0:T(8,128)(2,1)}, u32[]{:S(2)}) copy-start(bf16[128,1024]{1,0:T(8,128)(2,1)} %copy-done.4) | copy-start | bytes 786436
  191.2 9.3 %copy-start.7 = (bf16[2,4,16,4096]{3,2,0,1:T(8,128)(2,1)S(1)}, bf16[2,4,16,4096]{3,2,0,1:T(8,128)(2,1)}, u32[]{:S(2)}) copy-start(bf16[2,4,16,4096]{3,2,0,1:T(8,128)(2,1)} %copy-done.6) | copy-start | bytes 3145732
  199.1 1.4 copy-start.2
  201.2 16.6 %all-to-all-start.4 = ((bf16[4,128,256]{2,1,0:T(8,128)(2,1)}), bf16[4,128,256]{2,1,0:T(8,128)(2,1)S(1)}, u32[]{:S(2)}, u32[]{:S(2)}) async-start(bf16[4,128,256]{2,1,0:T(8,128)(2,1)} %bitcast.35), calls=%async_computation.4 | async-start | bytes 524288 | tf_op jit(solution)/shard_map/all_to_all | solution.py:51
  207.1 18.2 %collective-permute-start.11 = (bf16[2,16,4096]{2,1,0:T(8,128)(2,1)}, bf16[2,16,4096]{2,1,0:T(8,128)(2,1)}, u32[]{:S(2)}, u32[]{:S(2)}) collective-permute-start(bf16[2,16,4096]{2,1,0:T(8,128)(2,1)} %get-tuple-element.50), channel_id=1, source_target_pairs={{1,0},{2,1},{3,2},{0,3},{5,4},{6,5},{7,6},{4,7},{9,8},{10,9},{11,1... | collective-permute-start | bytes 786440 | tf_op jit(solution)/shard_map/ppermute | solution.py:34
  210.0 15.3 %collective-permute-start.10 = (bf16[2,16,4096]{2,1,0:T(8,128)(2,1)}, bf16[2,16,4096]{2,1,0:T(8,128)(2,1)}, u32[]{:S(2)}, u32[]{:S(2)}) collective-permute-start(bf16[2,16,4096]{2,1,0:T(8,128)(2,1)} %get-tuple-element.51), channel_id=1, source_target_pairs={{2,0},{3,1},{0,2},{1,3},{6,4},{7,5},{4,6},{5,7},{10,8},{11,9},{8,1... | collective-permute-start | bytes 786440 | tf_op jit(solution)/shard_map/ppermute | solution.py:34
  210.3 15.0 %collective-permute-start.9 = (bf16[2,16,4096]{2,1,0:T(8,128)(2,1)}, bf16[2,16,4096]{2,1,0:T(8,128)(2,1)}, u32[]{:S(2)}, u32[]{:S(2)}) collective-permute-start(bf16[2,16,4096]{2,1,0:T(8,128)(2,1)} %get-tuple-element.49), channel_id=1, source_target_pairs={{3,0},{0,1},{1,2},{2,3},{7,4},{4,5},{5,6},{6,7},{11,8},{8,9},{9,10... | collective-permute-start | bytes 786440 | tf_op jit(solution)/shard_map/ppermute | solution.py:34
  218.1 2.6 copy-start.3
  220.7 1.2 copy-start.8
  221.2 1.8 collective-permute-start.18
  223.0 8.1 %collective-permute-start.19 = (f32[32,128]{1,0:T(8,128)S(1)}, f32[32,128]{1,0:T(8,128)S(1)}, u32[]{:S(2)}, u32[]{:S(2)}) collective-permute-start(f32[32,128]{1,0:T(8,128)S(1)} %bitcast_add_fusion), channel_id=1, source_target_pairs={{0,4},{4,0},{1,5},{5,1},{2,6},{6,2},{3,7},{7,3},{8,12},{12,8},{9,1... | collective-permute-start | bytes 49160 | tf_op jit(solution)/shard_map/ppermute | solution.py:30
  226.6 33.4 %copy-start.14 = (f32[2,16,4096]{2,1,0:T(8,128)}, f32[2,16,4096]{2,1,0:T(8,128)S(1)}, u32[]{:S(2)}) copy-start(f32[2,16,4096]{2,1,0:T(8,128)S(1)} %fusion.9) | copy-start | bytes 1572868
  231.1 5.3 %collective-permute-start.21 = (f32[32,128]{1,0:T(8,128)S(1)}, f32[32,128]{1,0:T(8,128)S(1)}, u32[]{:S(2)}, u32[]{:S(2)}) collective-permute-start(f32[32,128]{1,0:T(8,128)S(1)} %fusion.50), channel_id=1, source_target_pairs={{0,2},{1,3},{2,0},{3,1},{4,6},{5,7},{6,4},{7,5},{8,10},{9,11},{10,... | collective-permute-start | bytes 49160 | tf_op jit(solution)/shard_map/ppermute | solution.py:57
  234.3 4.9 %collective-permute-start.22 = (f32[32,128]{1,0:T(8,128)S(1)}, f32[32,128]{1,0:T(8,128)S(1)}, u32[]{:S(2)}, u32[]{:S(2)}) collective-permute-start(f32[32,128]{1,0:T(8,128)S(1)} %fusion.50), channel_id=1, source_target_pairs={{0,3},{1,2},{2,1},{3,0},{4,7},{5,6},{6,5},{7,4},{8,11},{9,10},{10,... | collective-permute-start | bytes 49160 | tf_op jit(solution)/shard_map/ppermute | solution.py:57
  234.7 4.5 %collective-permute-start.20 = (f32[32,128]{1,0:T(8,128)S(1)}, f32[32,128]{1,0:T(8,128)S(1)}, u32[]{:S(2)}, u32[]{:S(2)}) collective-permute-start(f32[32,128]{1,0:T(8,128)S(1)} %fusion.50), channel_id=1, source_target_pairs={{0,1},{1,0},{2,3},{3,2},{4,5},{5,4},{6,7},{7,6},{8,9},{9,8},{10,11... | collective-permute-start | bytes 49160 | tf_op jit(solution)/shard_map/ppermute | solution.py:57
  239.2 9.9 %collective-permute-start.24 = (f32[32,128]{1,0:T(8,128)S(1)}, f32[32,128]{1,0:T(8,128)S(1)}, u32[]{:S(2)}, u32[]{:S(2)}) collective-permute-start(f32[32,128]{1,0:T(8,128)S(1)} %add_add_fusion.1), channel_id=1, source_target_pairs={{0,128},{64,192},{128,0},{192,64},{1,129},{65,193},{129,1},{193,65... | collective-permute-start | bytes 49160 | tf_op jit(solution)/shard_map/ppermute | solution.py:57
  239.3 24.3 %collective-permute-start.16 = (bf16[2,16,4096]{2,1,0:T(8,128)(2,1)}, bf16[2,16,4096]{2,1,0:T(8,128)(2,1)S(1)}, u32[]{:S(2)}, u32[]{:S(2)}) collective-permute-start(bf16[2,16,4096]{2,1,0:T(8,128)(2,1)} %bitcast.39), channel_id=1, source_target_pairs={{1,0},{2,1},{3,2},{0,3},{5,4},{6,5},{7,6},{4,7},{9,8},{10,9},{11,1... | collective-permute-start | bytes 786440 | tf_op jit(solution)/shard_map/ppermute | solution.py:34
  241.4 23.0 %collective-permute-start.15 = (bf16[2,16,4096]{2,1,0:T(8,128)(2,1)}, bf16[2,16,4096]{2,1,0:T(8,128)(2,1)S(1)}, u32[]{:S(2)}, u32[]{:S(2)}) collective-permute-start(bf16[2,16,4096]{2,1,0:T(8,128)(2,1)} %bitcast.38), channel_id=1, source_target_pairs={{2,0},{3,1},{0,2},{1,3},{6,4},{7,5},{4,6},{5,7},{10,8},{11,9},{8,1... | collective-permute-start | bytes 786440 | tf_op jit(solution)/shard_map/ppermute | solution.py:34
  241.4 25.6 %collective-permute-start.14 = (bf16[2,16,4096]{2,1,0:T(8,128)(2,1)}, bf16[2,16,4096]{2,1,0:T(8,128)(2,1)}, u32[]{:S(2)}, u32[]{:S(2)}) collective-permute-start(bf16[2,16,4096]{2,1,0:T(8,128)(2,1)} %bitcast.37), channel_id=1, source_target_pairs={{3,0},{0,1},{1,2},{2,3},{7,4},{4,5},{5,6},{6,7},{11,8},{8,9},{9,10... | collective-permute-start | bytes 786440 | tf_op jit(solution)/shard_map/ppermute | solution.py:34
  243.1 15.8 %all-to-all-start.5 = ((bf16[4,128,256]{2,1,0:T(8,128)(2,1)}), bf16[4,128,256]{2,1,0:T(8,128)(2,1)S(1)}, u32[]{:S(2)}, u32[]{:S(2)}) async-start(bf16[4,128,256]{2,1,0:T(8,128)(2,1)} %broadcast_in_dim.15), calls=%async_computation.5 | async-start | bytes 524288 | tf_op jit(solution)/shard_map/all_to_all | solution.py:39
  246.5 5.0 %collective-permute-start.25 = (f32[32,128]{1,0:T(8,128)S(1)}, f32[32,128]{1,0:T(8,128)S(1)}, u32[]{:S(2)}, u32[]{:S(2)}) collective-permute-start(f32[32,128]{1,0:T(8,128)S(1)} %add_add_fusion.1), channel_id=1, source_target_pairs={{0,192},{64,128},{128,64},{192,0},{1,193},{65,129},{129,65},{193,1... | collective-permute-start | bytes 49160 | tf_op jit(solution)/shard_map/ppermute | solution.py:57
  249.1 4.7 %collective-permute-start.23 = (f32[32,128]{1,0:T(8,128)S(1)}, f32[32,128]{1,0:T(8,128)S(1)}, u32[]{:S(2)}, u32[]{:S(2)}) collective-permute-start(f32[32,128]{1,0:T(8,128)S(1)} %add_add_fusion.1), channel_id=1, source_target_pairs={{0,64},{64,0},{128,192},{192,128},{1,65},{65,1},{129,193},{193,129... | collective-permute-start | bytes 49160 | tf_op jit(solution)/shard_map/ppermute | solution.py:57
  251.6 51.2 %collective-permute-start.12 = (bf16[16,4096]{1,0:T(8,128)(2,1)}, bf16[16,4096]{1,0:T(8,128)(2,1)}, u32[]{:S(2)}, u32[]{:S(2)}) collective-permute-start(bf16[16,4096]{1,0:T(8,128)(2,1)} %fusion.26), channel_id=1, source_target_pairs={{0,4},{4,0},{1,5},{5,1},{2,6},{6,2},{3,7},{7,3},{8,12},{12,8},{9,1... | collective-permute-start | bytes 393224 | tf_op jit(solution)/shard_map/ppermute | solution.py:30
  254.4 20.5 %collective-permute-start.27 = (f32[32,128]{1,0:T(8,128)}, f32[32,128]{1,0:T(8,128)}, u32[]{:S(2)}, u32[]{:S(2)}) collective-permute-start(f32[32,128]{1,0:T(8,128)} %add_add_fusion), channel_id=1, source_target_pairs={{0,32},{16,48},{32,0},{48,16},{1,33},{17,49},{33,1},{49,17},{2,34}... | collective-permute-start | bytes 49160 | tf_op jit(solution)/shard_map/ppermute | solution.py:57
  260.0 27.6 %copy-start.10 = (bf16[16,4096]{1,0:T(8,128)(2,1)S(1)}, bf16[16,4096]{1,0:T(8,128)(2,1)}, u32[]{:S(2)}) copy-start(bf16[16,4096]{1,0:T(8,128)(2,1)} %param.9) | copy-start | bytes 393220
  260.0 28.5 %copy-start.12 = (bf16[16,1,128,128]{3,2,1,0:T(8,128)(2,1)S(1)}, bf16[16,1,128,128]{3,2,1,0:T(8,128)(2,1)}, u32[]{:S(2)}) copy-start(bf16[16,1,128,128]{3,2,1,0:T(8,128)(2,1)} %get-tuple-element.44) | copy-start | bytes 1572868
  260.0 14.9 %all-to-all-start.6 = ((bf16[4,512,256]{2,1,0:T(8,128)(2,1)}), bf16[4,512,256]{2,1,0:T(8,128)(2,1)S(1)}, u32[]{:S(2)}, u32[]{:S(2)}) async-start(bf16[4,512,256]{2,1,0:T(8,128)(2,1)} %broadcast_in_dim.17), calls=%async_computation.6 | async-start | bytes 2097152 | tf_op jit(solution)/shard_map/all_to_all | solution.py:39
  263.7 25.2 %copy-start.11 = (bf16[16,1,128,128]{3,2,1,0:T(8,128)(2,1)S(1)}, bf16[16,1,128,128]{3,2,1,0:T(8,128)(2,1)}, u32[]{:S(2)}) copy-start(bf16[16,1,128,128]{3,2,1,0:T(8,128)(2,1)} %get-tuple-element.43) | copy-start | bytes 1572868
  263.7 16.1 %collective-permute-start.28 = (f32[32,128]{1,0:T(8,128)}, f32[32,128]{1,0:T(8,128)}, u32[]{:S(2)}, u32[]{:S(2)}) collective-permute-start(f32[32,128]{1,0:T(8,128)} %add_add_fusion), channel_id=1, source_target_pairs={{0,48},{16,32},{32,16},{48,0},{1,49},{17,33},{33,17},{49,1},{2,50}... | collective-permute-start | bytes 49160 | tf_op jit(solution)/shard_map/ppermute | solution.py:57
  264.4 15.3 %collective-permute-start.26 = (f32[32,128]{1,0:T(8,128)}, f32[32,128]{1,0:T(8,128)}, u32[]{:S(2)}, u32[]{:S(2)}) collective-permute-start(f32[32,128]{1,0:T(8,128)} %add_add_fusion), channel_id=1, source_target_pairs={{0,16},{16,0},{32,48},{48,32},{1,17},{17,1},{33,49},{49,33},{2,18}... | collective-permute-start | bytes 49160 | tf_op jit(solution)/shard_map/ppermute | solution.py:57
  274.9 14.0 %collective-permute-start.29 = (bf16[2048,256]{1,0:T(8,128)(2,1)S(1)}, bf16[2048,256]{1,0:T(8,128)(2,1)S(1)}, u32[]{:S(2)}, u32[]{:S(2)}) collective-permute-start(bf16[2048,256]{1,0:T(8,128)(2,1)S(1)} %bitcast.127), channel_id=1, source_target_pairs={{0,8},{8,0},{1,9},{9,1},{2,10},{10,2},{3,11},{11,3},{4,12},{12,4},... | collective-permute-start | bytes 3145736 | tf_op jit(solution)/shard_map/ppermute | solution.py:30
  274.9 12.7 %collective-permute-start.17 = (bf16[16,4096]{1,0:T(8,128)(2,1)S(1)}, bf16[16,4096]{1,0:T(8,128)(2,1)S(1)}, u32[]{:S(2)}, u32[]{:S(2)}) collective-permute-start(bf16[16,4096]{1,0:T(8,128)(2,1)S(1)} %fusion.27), channel_id=1, source_target_pairs={{0,4},{4,0},{1,5},{5,1},{2,6},{6,2},{3,7},{7,3},{8,12},{12,8},{9,1... | collective-permute-start | bytes 393224 | tf_op jit(solution)/shard_map/ppermute | solution.py:30
  288.5 14.3 %copy-start.15 = (f32[2,16,4096]{2,1,0:T(8,128)S(1)}, f32[2,16,4096]{2,1,0:T(8,128)}, u32[]{:S(2)}) copy-start(f32[2,16,4096]{2,1,0:T(8,128)} %copy-done.14) | copy-start | bytes 1572868
  288.5 14.3 %copy-start.17 = (bf16[16,4096]{1,0:T(8,128)(2,1)S(1)}, bf16[16,4096]{1,0:T(8,128)(2,1)}, u32[]{:S(2)}) copy-start(bf16[16,4096]{1,0:T(8,128)(2,1)} %param.16) | copy-start | bytes 393220
  288.5 14.2 %copy-start.24 = (f32[16]{0:T(128)S(1)}, f32[16]{0:T(128)}, u32[]{:S(2)}) copy-start(f32[16]{0:T(128)} %copy-done.23) | copy-start | bytes 196
  289.3 6.3 %collective-permute-start.32 = (bf16[128,256]{1,0:T(8,128)(2,1)S(1)}, bf16[128,256]{1,0:T(8,128)(2,1)S(1)}, u32[]{:S(2)}, u32[]{:S(2)}) collective-permute-start(bf16[128,256]{1,0:T(8,128)(2,1)S(1)} %fusion.3), channel_id=1, source_target_pairs={{2,0},{3,1},{0,2},{1,3},{6,4},{7,5},{4,6},{5,7},{10,8},{11,9},{8,1... | collective-permute-start | bytes 196616 | tf_op jit(solution)/shard_map/ppermute | solution.py:34
  292.0 4.3 %collective-permute-start.31 = (bf16[128,256]{1,0:T(8,128)(2,1)S(1)}, bf16[128,256]{1,0:T(8,128)(2,1)S(1)}, u32[]{:S(2)}, u32[]{:S(2)}) collective-permute-start(bf16[128,256]{1,0:T(8,128)(2,1)S(1)} %fusion.3), channel_id=1, source_target_pairs={{1,0},{2,1},{3,2},{0,3},{5,4},{6,5},{7,6},{4,7},{9,8},{10,9},{11,1... | collective-permute-start | bytes 196616 | tf_op jit(solution)/shard_map/ppermute | solution.py:34
  293.1 5.5 %collective-permute-start.30 = (bf16[128,256]{1,0:T(8,128)(2,1)S(1)}, bf16[128,256]{1,0:T(8,128)(2,1)S(1)}, u32[]{:S(2)}, u32[]{:S(2)}) collective-permute-start(bf16[128,256]{1,0:T(8,128)(2,1)S(1)} %fusion.3), channel_id=1, source_target_pairs={{3,0},{0,1},{1,2},{2,3},{7,4},{4,5},{5,6},{6,7},{11,8},{8,9},{9,10... | collective-permute-start | bytes 196616 | tf_op jit(solution)/shard_map/ppermute | solution.py:34
  298.6 9.1 %collective-permute-start.33 = (bf16[2,128,256]{2,1,0:T(8,128)(2,1)S(1)}, bf16[2,128,256]{2,1,0:T(8,128)(2,1)S(1)}, u32[]{:S(2)}, u32[]{:S(2)}) collective-permute-start(bf16[2,128,256]{2,1,0:T(8,128)(2,1)S(1)} %pad_maximum_fusion.6), channel_id=1, source_target_pairs={{0,4},{4,0},{1,5},{5,1},{2,6},{6,2},{3,7},{7,3},{8,12},{12,8},{9,1... | collective-permute-start | bytes 393224 | tf_op jit(solution)/shard_map/ppermute | solution.py:30
  307.7 2.1 copy-start.1
  (2 other events, 1.8 us)
Sparse Core Ops, SparseCore 0:
  10.1 95.3 all-gather.2
  188.9 78.9 all-gather.4

commit v2 on v1

--- a/solution.py
+++ b/solution.py
@@ -41,51 +41,45 @@
     )
 
 
-def spread_yz(a):
-    rows, cols = a.shape
-    a = spread(a, "z").reshape(SIZES["z"] * rows, cols)
-    return spread(a, "y").reshape(SIZES["y"] * SIZES["z"] * rows, cols)
-
-
 def collect(a, axis):
     return jnp.sum(lax.all_to_all(a, axis, 0, 0, tiled=True).astype(wide), axis=0)
 
 
-def all_sum(a, axis):
-    if SIZES[axis] == 2:
-        return a + swap(a, axis)
-    far = [lax.ppermute(a, axis, [(i, i ^ k) for i in range(4)]) for k in range(1, 4)]
-    return (a + far[0]) + (far[1] + far[2])
-
-
-def spread_tensor(a):
-    both = jnp.stack([a, swap(a, "h")])
-    return jnp.stack([both] + [shift(both, k) for k in range(1, NX)])
-
-
-def collect_tensor(a):
+def spread_h(a):
+    return jnp.stack([a, swap(a, "h")])
+
+
+def spread_x(a):
+    return [a] + [shift(a, k) for k in range(1, NX)]
+
+
+def sum_pair(a):
+    return a[0].astype(wide) + a[1].astype(wide)
+
+
+def collect_x(a):
     total = a[0].astype(wide)
     for k in range(1, NX):
         total = total + shift(a[k], NX - k).astype(wide)
-    return total[0] + swap(total[1].astype(low), "h").astype(wide)
+    return total[0], total[1].astype(low)
 
 
 def turn(field, cosine, sine):
     return field * cosine + pltpu.roll(field, HALF_DIM, 1) * sine
 
 
+ANY = pl.BlockSpec(memory_space=pl.ANY)
 PARAMS = pltpu.CompilerParams(vmem_limit_bytes=48 * 2**20)
-ANY = pl.BlockSpec(memory_space=pl.ANY)
-
-
-def kv_project_kernel(both, weights, cosine, sine, rows, pend, kv, total):
+
+
+def kv_project_kernel(normed, weights, cosine, sine, kv, total):
     step = pl.program_id(0)
 
     @pl.when(step == 0)
     def _():
         total[...] = jnp.zeros_like(total)
 
-    total[...] += dot(both[...], weights[...], ((1,), (0,)))
+    total[...] += dot(normed[...], weights[...], ((1,), (0,)))
 
     @pl.when(step == pl.num_programs(0) - 1)
     def _():
@@ -93,7 +87,7 @@
         kv[:, HEAD_DIM:] = total[:, HEAD_DIM:].astype(low)
 
 
-def kv_project(both, weights, cosine, sine, rows, pend, step=1024):
+def kv_project(both, weights, cosine, sine, step=1024):
     tok = both.shape[0]
     width, cols = weights.shape
     kv_cols = 2 * HEAD_DIM
@@ -106,14 +100,12 @@
             pl.BlockSpec((step, kv_cols), lambda i: (i, cols // kv_cols - 1)),
             fixed,
             fixed,
-            ANY,
-            ANY,
         ],
         out_specs=pl.BlockSpec((tok, kv_cols), lambda i: (0, 0)),
         out_shape=jax.ShapeDtypeStruct((tok, kv_cols), low),
         scratch_shapes=[pltpu.VMEM((tok, kv_cols), wide)],
         compiler_params=PARAMS,
-    )(both, weights, cosine, sine, rows, pend)
+    )(both, weights, cosine, sine)
 
 
 def project_kernel(normed, grads, weights, cosine, sine, query, grad_heads, total):
@@ -139,7 +131,7 @@
             ].astype(low)
 
 
-def project(both, weights, cosine, sine, cols, step=512):
+def project(both, weights, cosine, sine, cols, step=1024):
     tok = both.shape[0]
     width = weights.shape[0]
     steps = width // step
@@ -162,20 +154,19 @@
     )(both, both, weights, cosine, sine)
 
 
-def hold_kernel(value, other, out):
-    out[...] = value[...]
-
-
-def hold(value, other):
-    return pl.pallas_call(
-        hold_kernel,
-        in_specs=[pl.BlockSpec(memory_space=pltpu.VMEM), ANY],
-        out_shape=jax.ShapeDtypeStruct(value.shape, value.dtype),
-    )(value, other)
-
-
 def attend_kernel(
-    query, grad_heads, near, far, key_place, bounds, cosine, sine, att_gq, near_grad, far_grad, score
+    at_chx,
+    query,
+    grad_heads,
+    near,
+    far,
+    bounds,
+    cosine,
+    sine,
+    att_gq,
+    near_grad,
+    far_grad,
+    score,
 ):
     rows = query.shape[0]
     tok = cosine.shape[0]
@@ -186,14 +177,19 @@
     q, g = query[...], grad_heads[...]
     last, first = bounds[0:1, :], bounds[1:2, :]
 
+    c, h, x = at_chx[0], at_chx[1], at_chx[2]
+    key = lax.broadcasted_iota(jnp.int32, (step, tok), 0)
+    key_x = (x + (key // 32) % NX) % NX
+    key_h = (h + (key // 16) % 2) % 2
+    local = (key // tok) * (2 * tok) + (key_h * NX + key_x) * 16 + key % 16
+
     peak = jnp.full((1, rows), -1e30, wide)
-    for kv, base in ((near, 0), (far, half)):
-
-        def mark(i, peak, kv=kv, base=base):
+    for kv, base, core in ((near, 0, c), (far, half, 1 - c)):
+
+        def mark(i, peak, kv=kv, base=base, core=core):
             at = pl.multiple_of(i * step, step)
             s = dot(kv[pl.ds(at, step), :HEAD_DIM], q, ((1,), (1,))) * scale
-            place = key_place[pl.ds(base + at, step), :]
-            place = jnp.broadcast_to(place, (step, tok))
+            place = local + (2 * at + core * tok)
             bias = jnp.where((place <= last) & (place >= first), 0.0, -1e30)
             s = s + jnp.concatenate([bias] * heads, axis=1)
             score[pl.ds(base + at, step), :] = s
@@ -241,11 +237,13 @@
         ).astype(low)
 
 
-def attend(query, grad_heads, near, far, key_place, bounds, cosine, sine):
+def attend(at_chx, query, grad_heads, near, far, bounds, cosine, sine):
     rows, tok = query.shape[0], cosine.shape[0]
     half = near.shape[0]
+    vmem = pl.BlockSpec(memory_space=pltpu.VMEM)
     return pl.pallas_call(
         attend_kernel,
+        in_specs=[pl.BlockSpec(memory_space=pltpu.SMEM)] + [vmem] * 7,
         out_shape=[
             jax.ShapeDtypeStruct((tok, 2 * rows // tok * HEAD_DIM), low),
             jax.ShapeDtypeStruct(near.shape, low),
@@ -253,16 +251,16 @@
         ],
         scratch_shapes=[pltpu.VMEM((2 * half, rows), wide)],
         compiler_params=PARAMS,
-    )(query, grad_heads, near, far, key_place, bounds, cosine, sine)
-
-
-def back_project_kernel(att_gq, weights, terms, grad):
+    )(at_chx, query, grad_heads, near, far, bounds, cosine, sine)
+
+
+def back_project_kernel(att_gq, weights, waited, terms, grad):
     half = att_gq.shape[1] // 2
     terms[...] = dot(att_gq[:, :half], weights[:, half:], ((1,), (1,))).astype(low)
     grad[...] = dot(att_gq[:, half:], weights[:, :half], ((1,), (1,)))
 
 
-def back_project(att_gq, weights, step=512):
+def back_project(att_gq, weights, waited, step=1024):
     tok = att_gq.shape[0]
     width, cols = weights.shape[0], att_gq.shape[1]
     out = pl.BlockSpec((tok, step), lambda i: (0, i))
@@ -272,6 +270,7 @@
         in_specs=[
             pl.BlockSpec(att_gq.shape, lambda i: (0, 0)),
             pl.BlockSpec((step, cols), lambda i: (i, 0)),
+            ANY,
         ],
         out_specs=[out, out],
         out_shape=[
@@ -279,35 +278,161 @@
             jax.ShapeDtypeStruct((tok, width), wide),
         ],
         compiler_params=PARAMS,
-    )(att_gq, weights)
-
-
-def weight_grad_kernel(rows, att_gq, grad_o, grad_q):
-    half, block = att_gq.shape[1] // 2, rows.shape[1] // 2
+    )(att_gq, weights, waited)
+
+
+def normed_grad_kernel(query_terms, grad_kv, weights, normed, terms, gain):
+    total = query_terms[...] + dot(grad_kv[...], weights[...], ((1,), (1,)))
+    terms[...] = total.astype(low)
+    gain[...] = jnp.sum(total * normed[...].astype(wide), axis=0, keepdims=True)
+
+
+def normed_grad(query_terms, grad_kv, weights, both, step=1024):
+    tok, width = query_terms.shape
+    kv_cols = grad_kv.shape[1]
+    at = weights.shape[1] // kv_cols - 1
+    columns = pl.BlockSpec((tok, step), lambda i: (0, i))
+    return pl.pallas_call(
+        normed_grad_kernel,
+        grid=(width // step,),
+        in_specs=[
+            columns,
+            pl.BlockSpec((tok, kv_cols), lambda i: (0, 0)),
+            pl.BlockSpec((step, kv_cols), lambda i: (i, at)),
+            columns,
+        ],
+        out_specs=[columns, pl.BlockSpec((1, step), lambda i: (0, i))],
+        out_shape=[
+            jax.ShapeDtypeStruct((tok, width), low),
+            jax.ShapeDtypeStruct((1, width), wide),
+        ],
+        compiler_params=PARAMS,
+    )(query_terms, grad_kv, weights, both)
+
+
+def positions(rows, at):
+    return jnp.concatenate([part[j, at] for part in rows for j in range(2)], axis=0)
+
+
+def weight_grad_kernel(*refs):
+    rows, att_gq, grad_o, grad_q = refs[:NX], refs[NX], refs[-2], refs[-1]
+    half, block = att_gq.shape[1] // 2, rows[0].shape[3] // 2
 
     @pl.when(pl.program_id(0) == 0)
     def _():
         grad_o[...] = jnp.zeros_like(grad_o)
         grad_q[...] = jnp.zeros_like(grad_q)
 
-    grad_o[...] += dot(rows[:, :block], att_gq[:, :half], ((0,), (0,)))
-    grad_q[...] += dot(rows[:, block:], att_gq[:, half:], ((0,), (0,)))
-
-
-def weight_grads(rows, att_gq, step=512):
+    own = jnp.concatenate([positions(rows, i) for i in range(rows[0].shape[1])], axis=0)
+    grad_o[...] += dot(own[:, :block], att_gq[:, :half], ((0,), (0,)))
+    grad_q[...] += dot(own[:, block:], att_gq[:, half:], ((0,), (0,)))
+
+
+def weight_grads(rows, att_gq, step=8):
+    two, n_dp, rows_own, both = rows[0].shape
     seq_len, cols = att_gq.shape
-    out = jax.ShapeDtypeStruct((rows.shape[1] // 2, cols // 2), wide)
+    out = jax.ShapeDtypeStruct((both // 2, cols // 2), wide)
+    part = pl.BlockSpec((two, step, rows_own, both), lambda i: (0, i, 0, 0))
     return pl.pallas_call(
         weight_grad_kernel,
-        grid=(seq_len // step,),
-        in_specs=[
-            pl.BlockSpec((step, rows.shape[1]), lambda i: (i, 0)),
-            pl.BlockSpec((step, cols), lambda i: (i, 0)),
-        ],
+        grid=(n_dp // step,),
+        in_specs=[part] * NX
+        + [pl.BlockSpec((seq_len // n_dp * step, cols), lambda i: (i, 0))],
         out_specs=[pl.BlockSpec(out.shape, lambda i: (0, 0))] * 2,
         out_shape=[out, out],
         compiler_params=PARAMS,
-    )(rows, att_gq)
+    )(*rows, att_gq)
+
+
+def kv_weight_grad_kernel(core, *refs):
+    rows, (near, far, out, total, gains) = refs[:NX], refs[NX:]
+    block = rows[0].shape[3] // 2
+    tok = near.shape[1] - gains.shape[1]
+    step = pl.program_id(0)
+
+    @pl.when(step == 0)
+    def _():
+        total[...] = jnp.zeros_like(total)
+        gains[...] = jnp.zeros_like(gains)
+
+    c = core[0]
+    for i in range(near.shape[0]):
+        for at, (grad, of) in enumerate(((near, c), (far, 1 - c))):
+            own = positions(rows, 2 * i + of)[:, block:]
+            total[...] += dot(own, grad[i, :tok], ((0,), (0,)))
+            gains[at] += grad[i, tok:].astype(wide)
+
+    @pl.when(step == pl.num_programs(0) - 1)
+    def _():
+        out[: total.shape[0]] = total[...].astype(low)
+        out[total.shape[0] :] = (gains[0] + gains[1]).astype(low)
+
+
+def kv_weight_grad(core, rows, near, far, tok, step=4):
+    two, n_dp, rows_own, both = rows[0].shape
+    outer, depth, cols = near.shape
+    kv = pl.BlockSpec((step, depth, cols), lambda i, c: (i, 0, 0))
+    part = pl.BlockSpec((two, 2 * step, rows_own, both), lambda i, c: (0, i, 0, 0))
+    out = jax.ShapeDtypeStruct((both // 2 + depth - tok, cols), low)
+    return pl.pallas_call(
+        kv_weight_grad_kernel,
+        grid_spec=pltpu.PrefetchScalarGridSpec(
+            num_scalar_prefetch=1,
+            grid=(outer // step,),
+            in_specs=[part] * NX + [kv, kv],
+            out_specs=pl.BlockSpec(out.shape, lambda i, c: (0, 0)),
+            scratch_shapes=[
+                pltpu.VMEM((both // 2, cols), wide),
+                pltpu.VMEM((2, depth - tok, cols), wide),
+            ],
+        ),
+        out_shape=out,
+        compiler_params=PARAMS,
+    )(core, *rows, near, far)
+
+
+def hold_kernel(first, second, waited, first_out, second_out):
+    first_out[...] = first[...]
+    second_out[...] = second[...]
+
+
+def hold(first, second, waited):
+    vmem = pl.BlockSpec(memory_space=pltpu.VMEM)
+    return pl.pallas_call(
+        hold_kernel,
+        in_specs=[vmem, vmem, ANY],
+        out_shape=[jax.ShapeDtypeStruct(a.shape, a.dtype) for a in (first, second)],
+        compiler_params=PARAMS,
+    )(first, second, waited)
+
+
+def add_kernel(near, far, rows, out, rows_out):
+    out[...] = (near[...].astype(wide) + far[...].astype(wide)).astype(low)
+    rows_out[...] = rows[...]
+
+
+def add(near, far, rows):
+    vmem = pl.BlockSpec(memory_space=pltpu.VMEM)
+    return pl.pallas_call(
+        add_kernel,
+        in_specs=[vmem, vmem, vmem],
+        out_shape=[jax.ShapeDtypeStruct(a.shape, low) for a in (near, rows)],
+        compiler_params=PARAMS,
+    )(near, far, rows)
+
+
+def pair_kernel(sums, waited, out):
+    for i in range(2):
+        out[i] = (sums[2 * i].astype(wide) + sums[2 * i + 1].astype(wide)).astype(low)
+
+
+def pairs(sums, waited):
+    return pl.pallas_call(
+        pair_kernel,
+        in_specs=[pl.BlockSpec(memory_space=pltpu.VMEM), ANY],
+        out_shape=jax.ShapeDtypeStruct((NX // 2,) + sums.shape[1:], low),
+        compiler_params=PARAMS,
+    )(sums, waited)
 
 
 def on_device(
@@ -335,8 +460,12 @@
     inv_rms = lax.rsqrt(jnp.mean(stream_f * stream_f, axis=-1, keepdims=True) + eps)
     unit_rows = stream_f * inv_rms
     normed_own = (unit_rows * gain).astype(low)
-    both = jnp.concatenate([normed_own, grad_out], axis=1)
-    both = spread_tensor(both).reshape(tok, 2 * width)
+    both = spread_h(jnp.concatenate([normed_own, grad_out], axis=1))
+    both = jnp.stack(spread_x(both)).reshape(tok, 2 * width)
+
+    split = [a.reshape(rows_own, n_dp, block) for a in (grad_out, normed_own)]
+    rows = jnp.transpose(jnp.concatenate(split, axis=2), (1, 0, 2))
+    rows = lax.all_to_all(rows, DP, 0, 0, tiled=True)
 
     def index(axis):
         return lax.broadcasted_iota(jnp.int32, (NX, 2, rows_own), axis)
@@ -344,10 +473,6 @@
     local = (((h ^ index(1)) * NX + (x + index(0)) % NX) * rows_own + index(2)).reshape(tok)
     block_first = ((y * SIZES["z"] + z) * 2 + c) * tok
     places = block_first + local
-    rel_c = jnp.arange(2, dtype=jnp.int32)[:, None, None]
-    at_yz = jnp.arange(outer, dtype=jnp.int32)[None, :, None]
-    key_place = ((at_yz * 2 + (c ^ rel_c)) * tok + local[None, None, :]).reshape(seq_len, 1)
-
     def relative(a):
         a = a.reshape((2, NX, rows_own) + a.shape[1:])
         a = jnp.where(h == 0, a, a[::-1])
@@ -367,63 +492,60 @@
         flipped = jnp.concatenate([field[:, HALF_DIM:], field[:, :HALF_DIM]], axis=1)
         return field * cosine + sign * flipped * sine
 
-    split = [a.reshape(rows_own, n_dp, block) for a in (grad_out, normed_own)]
-    rows = jnp.transpose(jnp.concatenate(split, axis=2), (1, 0, 2))
-    rows = spread_tensor(lax.all_to_all(rows, DP, 0, 0, tiled=True))
-    rows = jnp.transpose(rows, (2, 0, 1, 3, 4)).reshape(seq_len, 2 * block)
-    normed_cores = rows[:, block:].reshape(outer, 2, tok, block)
-    rows_near, rows_far = (
-        lax.dynamic_index_in_dim(normed_cores, i, 1, keepdims=False).reshape(-1, block)
-        for i in (c, 1 - c)
-    )
     pend = relative(pending[0])
-
-    kv_own = kv_project(both, weights, cosine, sine, rows, pend)
-    kv_near = spread_yz(kv_own)
+    bounds = jnp.stack([places, first_place])
+    both, rows, pend, bounds, cosine, sine = lax.optimization_barrier(
+        (both, rows, pend, bounds, cosine, sine)
+    )
+    kv_own = kv_project(both, weights, cosine, sine)
+    kv_near = spread(kv_own, "z").reshape(-1, 2 * HEAD_DIM)
+    query, grad_heads = project(both, weights, cosine, sine, 2 * q_width)
+    kv_near = spread(kv_near, "y").reshape(-1, 2 * HEAD_DIM)
     kv_far = swap(kv_near, "c")
-    query, grad_heads = project(both, weights, cosine, sine, 2 * q_width)
-    bounds = jnp.stack([places, first_place])
+    at_chx = jnp.stack([c, h, x]).astype(jnp.int32)
     att_gq, near_piece, far_piece = attend(
-        query, grad_heads, kv_near, kv_far, key_place, bounds, cosine, sine
-    )
-    kv_sum = near_piece.astype(wide) + swap(far_piece, "c").astype(wide)
-    kv_sum = kv_sum.astype(low).reshape(SIZES["y"], -1, 2 * HEAD_DIM)
+        at_chx, query, grad_heads, kv_near, kv_far, bounds, cosine, sine
+    )
+    kv_sum, rows = add(near_piece, swap(far_piece, "c"), rows)
+    kv_sum = kv_sum.reshape(SIZES["y"], -1, 2 * HEAD_DIM)
+    rows = spread_h(rows)
+    terms, query_terms = back_project(att_gq, weights, rows)
     kv_sum = collect(kv_sum, "y").astype(low)
-    att_gq_all = lax.all_gather(hold(att_gq, kv_sum), DP, axis=0, tiled=True)
+    att_gq_all = lax.all_gather(att_gq, DP, axis=0, tiled=True)
     kv_grad = collect(kv_sum.reshape(SIZES["z"], tok, 2 * HEAD_DIM), "z")
     grad_key = rotate(kv_grad[:, :HEAD_DIM], -1.0)
     grad_kv = jnp.concatenate([grad_key, kv_grad[:, HEAD_DIM:]], axis=1).astype(low)
 
-    gkv_near = spread_yz(grad_kv)
-    gkv_far = swap(gkv_near, "c")
-    grad_w_kv = dot(rows_near, gkv_near, ((0,), (0,))) + dot(rows_far, gkv_far, ((0,), (0,)))
-
-    terms, query_terms = back_project(att_gq, weights)
     terms = terms.reshape(NX, 2, rows_own, width).astype(wide) + pend.astype(wide)
-    hidden_out = (stream_f + collect_tensor(terms.astype(low))).astype(low)
-
-    wkv = weights[:, 2 * q_width :]
-    normed_terms = query_terms + dot(grad_kv, wkv, ((1,), (1,)))
-    grad_normed = collect_tensor(normed_terms.astype(low).reshape(NX, 2, rows_own, width))
-    gain_sum = jnp.sum(normed_terms * both[:, :width].astype(wide), axis=0).reshape(n_dp, block)
-    for axis in ("c", "h", "x", "y", "z"):
-        gain_sum = all_sum(gain_sum, axis)
+    hidden_part, hidden_other = collect_x(terms.astype(low))
+
+    normed_terms, gain_terms = normed_grad(query_terms, grad_kv, weights, both)
+    gain_rows = gain_terms.astype(low).reshape(-1, 2 * HEAD_DIM)
+    depth = tok + gain_rows.shape[0]
+    near = spread(jnp.concatenate([grad_kv, gain_rows], axis=0), "z")
+    near = spread(near, "y").reshape(outer, depth, 2 * HEAD_DIM)
+    rows = spread_x(rows)
+    sums = kv_weight_grad(c.astype(jnp.int32)[None], rows, near, swap(near, "c"), tok)
+
+    normed_part, normed_other = collect_x(normed_terms.reshape(NX, 2, rows_own, width))
+    normed_other, hidden_other = hold(normed_other, hidden_other, sums)
+    normed_other = swap(normed_other, "h")
+    grad_normed = normed_part + normed_other.astype(wide)
+
+    hidden_other = swap(hidden_other, "h")
+    hidden_out = (stream_f + (hidden_part + hidden_other.astype(wide))).astype(low)
+
+    sums = spread(sums, "x")
+    grad_o, grad_q = weight_grads(rows, att_gq_all)
+    sums = pairs(sums, grad_o)
+    sums_other = swap(sums, "h")
+    pair, other = sums[:, :block], sums_other[:, :block]
+    gain_sum = sum_pair(sums[:, block:]) + sum_pair(sums_other[:, block:])
     grad_gain = gain_sum.reshape(width) / gain
-
-    grad_o, grad_q = weight_grads(rows, att_gq_all)
-
-    kv_own_w = grad_w_kv.astype(low)
-    kv_blocks = [kv_own_w.astype(wide)] + [shift(kv_own_w, k).astype(wide) for k in range(1, NX)]
-    odd = x % 2 == 1
-    near = kv_blocks[0] + jnp.where(odd, kv_blocks[3], kv_blocks[1])
-    far = kv_blocks[2] + jnp.where(odd, kv_blocks[1], kv_blocks[3])
-    pair = jnp.stack([jnp.where(x < 2, near, far), jnp.where(x < 2, far, near)]).astype(low)
-    other = swap(pair, "h")
-    pair = jnp.concatenate(
-        [jnp.where(h == 0, pair, other), jnp.where(h == 0, other, pair)], axis=0
-    ).astype(wide)
+    first, second = jnp.where(h == 0, pair, other), jnp.where(h == 0, other, pair)
+    heads = [first[0], first[1], second[0], second[1]]
     grad_k, grad_v = (
-        jnp.transpose(pair[:, :, i : i + HEAD_DIM], (1, 0, 2)).reshape(k_weight.shape)
+        jnp.concatenate([a[:, i : i + HEAD_DIM] for a in heads], axis=1).astype(wide)
         for i in (0, HEAD_DIM)
     )
 

time: 327 us -> 296 us (0.905)
  starting transfers between devices: 86 us -> 70.7 us
  other arithmetic: 23.6 us -> 19.7 us
  matrix products: 3.33 us -> 0 us
    all_gather x1, waiting for transfers between devices: 10.2 us -> 35.1 us  [on_device(): lax.all_gather(jnp.concatenate([q_weight, out_weight] + kv_weights, axis=...]
    all_to_all x1 -> x0, blocking collectives: 18.3 us -> none  [collect(): lax.all_to_all(a, axis, 0, 0, tiled=True).astype(wide)]
    all_to_all x1 -> x2, blocking collectives: 11.8 us -> 29.1 us  [spread(): lax.all_to_all(jnp.broadcast_to(a[None], (size,) + a.shape), axis, 0, 0,...]
    ppermute x9 -> x0, starting transfers between devices: 13.1 us -> none  [all_sum(): lax.ppermute(a, axis, [(i, i ^ k) for i in range(4)])]
    all_to_all x3, waiting for transfers between devices: 23.2 us -> 12.6 us  [spread(): lax.all_to_all(jnp.broadcast_to(a[None], (size,) + a.shape), axis, 0, 0,...]
    ppermute x10 -> x8, waiting for transfers between devices: 40.8 us -> 31.8 us  [swap(): return lax.ppermute(a, axis, [(0, 1), (1, 0)])]
    ppermute x10 -> x8, starting transfers between devices: 27.6 us -> 19.6 us  [swap(): return lax.ppermute(a, axis, [(0, 1), (1, 0)])]
    all_to_all x1 -> x2, starting transfers between devices: 5.06 us -> 12.6 us  [collect(): lax.all_to_all(a, axis, 0, 0, tiled=True).astype(wide)]
  transfers between devices with their start and end apart: 41 -> 28, of which waited for: 19 -> 13; matrix products, arithmetic and copies ran while one was open for 11% -> 8% of each run, Pallas kernels for 5% -> 8%
where the time goes in v2:
time: 296 us; the launch traced here: 294 us
  waiting for transfers between devices  102 us (34%)
  starting transfers between devices  70.7 us (24%)
  Pallas kernels  39.7 us (13%)
  blocking collectives  29.1 us (10%)
  other arithmetic  19.7 us (7%)
  local copies, waits for them, and re-layouts  17.6 us (6%)
  between operations  14.7 us (5%)
    all_gather x1, waiting for transfers between devices, on_device(): lax.all_gather(jnp.concatenate([q_weight, out_weight] + kv_weights, axis=...  35.1 us
    ppermute x8, waiting for transfers between devices, swap(): return lax.ppermute(a, axis, [(0, 1), (1, 0)])  31.8 us
    all_to_all x2, blocking collectives, spread(): lax.all_to_all(jnp.broadcast_to(a[None], (size,) + a.shape), axis, 0, 0,...  29.1 us
    ppermute x8, starting transfers between devices, swap(): return lax.ppermute(a, axis, [(0, 1), (1, 0)])  19.6 us
    ppermute x12, starting transfers between devices, shift(): return lax.ppermute(a, 'x', [((i + step) % NX, i) for i in range(NX)])  19 us
    ppermute x12, waiting for transfers between devices, shift(): return lax.ppermute(a, 'x', [((i + step) % NX, i) for i in range(NX)])  15 us
    pallas_call x1, Pallas kernels, attend(): pl.pallas_call(attend_kernel, in_specs=[pl.BlockSpec(memory_space=pltpu.S...  12.9 us
    all_to_all x3, waiting for transfers between devices, spread(): lax.all_to_all(jnp.broadcast_to(a[None], (size,) + a.shape), axis, 0, 0,...  12.6 us
  transfers between devices with their start and end apart: 28, of which 13 were waited for; matrix products, arithmetic and copies ran while one was open for 8% of the time, Pallas kernels for 8%

profile of v2, /device:TPU:32, one launch (start us, length us, event | category | flops | bytes accessed | tf_op | source)
XLA Modules:
  0.0 293.8 jit_solution(8642237835058083365)
XLA Ops:
  7.3 0.9 constant_dynamic-slice_fusion
  8.2 1.7 pad_maximum_fusion.3
  9.9 1.1 fusion.16
  11.0 1.0 fusion.10
  12.0 0.9 fusion.33
  13.0 6.4 %collective-permute-start = (bf16[16,8192]{1,0:T(8,128)(2,1)S(1)}, bf16[16,8192]{1,0:T(8,128)(2,1)S(1)}, u32[]{:S(2)}, u32[]{:S(2)}) collective-permute-start(bf16[16,8192]{1,0:T(8,128)(2,1)S(1)} %get-tuple-element.61), channel_id=1, source_target_pairs={{0,4},{4,0},{1,5},{5,1},{2,6},{6,2},{3,7},{7,3},{8,12},{12,8},{9,1... | collective-permute-start | bytes 786440 | tf_op jit(solution)/shard_map/ppermute | solution.py:30
  20.2 7.0 %all-to-all-start = ((bf16[32,16,256]{2,1,0:T(8,128)(2,1)}), bf16[32,16,256]{2,1,0:T(8,128)(2,1)S(1)}, u32[]{:S(2)}, u32[]{:S(2)}) async-start(bf16[32,16,256]{2,1,0:T(8,128)(2,1)} %maximum_bitcast_fusion), calls=%async_computation | async-start | bytes 524288 | tf_op jit(solution)/shard_map/all_to_all | solution.py:468
  29.4 7.7 %collective-permute-done = bf16[16,8192]{1,0:T(8,128)(2,1)S(1)} collective-permute-done((bf16[16,8192]{1,0:T(8,128)(2,1)S(1)}, bf16[16,8192]{1,0:T(8,128)(2,1)S(1)}, u32[]{:S(2)}, u32[]{:S(2)}) %collective-permute-start) | collective-permute-done | bytes 262176 | tf_op jit(solution)/shard_map/ppermute | solution.py:30
  37.2 1.6 collective-permute-start.3
  38.8 2.7 collective-permute-start.2
  41.5 1.4 collective-permute-start.1
  43.0 1.4 fusion.2
  44.4 8.6 %collective-permute-done.3 = bf16[2,16,8192]{2,1,0:T(8,128)(2,1)S(1)} collective-permute-done((bf16[2,16,8192]{2,1,0:T(8,128)(2,1)S(1)}, bf16[2,16,8192]{2,1,0:T(8,128)(2,1)S(1)}, u32[]{:S(2)}, u32[]{:S(2)}) %collective-permute-start.3) | collective-permute-done | bytes 524320 | tf_op jit(solution)/shard_map/ppermute | solution.py:34
  53.0 5.6 %collective-permute-done.2 = bf16[2,16,8192]{2,1,0:T(8,128)(2,1)S(1)} collective-permute-done((bf16[2,16,8192]{2,1,0:T(8,128)(2,1)S(1)}, bf16[2,16,8192]{2,1,0:T(8,128)(2,1)S(1)}, u32[]{:S(2)}, u32[]{:S(2)}) %collective-permute-start.2) | collective-permute-done | bytes 524320 | tf_op jit(solution)/shard_map/ppermute | solution.py:34
  58.9 35.1 %all-gather.3.cloned.1.call-done.weights = bf16[4096,1280]{1,0:T(8,128)(2,1)} async-done(((bf16[128,1280]{1,0:T(8,128)(2,1)}), bf16[4096,1280]{1,0:T(8,128)(2,1)}) %all-gather.3.cloned.1.call-update) | async-done | bytes 10485776 | tf_op jit(solution)/shard_map/all_gather | solution.py:455
  94.0 3.0 %shard_map.145 = bf16[128,256]{1,0:T(8,128)(2,1)S(1)} custom-call(bf16[128,8192]{1,0:T(8,128)(2,1)S(1)} %bitcast.86, bf16[4096,1280]{1,0:T(8,128)(2,1)} %all-gather.3.cloned.1.call-done.weights, f32[128,128]{1,0:T(8,128)S(1)} %get-tuple-element.29.cosine, f32[128,128]{1,0:T(8,128)S(1)} %get-tuple-element.30.sine), custom_call_target="tpu_custom_call" | custom-call | tf_op jit(solution)/shard_map/pallas_call | solution.py:95
  97.1 11.7 %all_to_all.40 = bf16[4,128,256]{2,1,0:T(8,128)(2,1)S(1)} all-to-all(bf16[4,128,256]{2,1,0:T(8,128)(2,1)S(1)} %broadcast_in_dim.12), channel_id=1, replica_groups=mesh['y'=4,'z'=4,'c'=2,'h'=2,'x'=4] {'z'}, dimensions={0} | all-to-all | bytes 524288 | tf_op jit(solution)/shard_map/all_to_all | solution.py:39
  108.9 17.4 %all_to_all.41 = bf16[4,512,256]{2,1,0:T(8,128)(2,1)S(1)} all-to-all(bf16[4,512,256]{2,1,0:T(8,128)(2,1)S(1)} %broadcast_in_dim.14), channel_id=1, replica_groups=mesh['y'=4,'z'=4,'c'=2,'h'=2,'x'=4] {'y'}, dimensions={0} | all-to-all | bytes 2097152 | tf_op jit(solution)/shard_map/all_to_all | solution.py:39
  126.3 5.2 %shard_map.144 = (bf16[512,128]{1,0:T(8,128)(2,1)S(1)}, bf16[512,128]{1,0:T(8,128)(2,1)S(1)}) custom-call(bf16[128,8192]{1,0:T(8,128)(2,1)S(1)} %bitcast.87, bf16[128,8192]{1,0:T(8,128)(2,1)S(1)} %bitcast.88, bf16[4096,1280]{1,0:T(8,128)(2,1)} %all-gather.3.cloned.1.call-done.weights, f32[128,128]{1,0:T(8,128)S(1)} %get-tuple-element.29.cosine, ...), custom_call_target="tpu_custom_call" | custom-call | tf_op jit(solution)/shard_map/pallas_call | solution.py:140
  131.5 12.9 %shard_map.146 = (bf16[128,1024]{1,0:T(8,128)(2,1)}, bf16[2048,256]{1,0:T(8,128)(2,1)S(1)}, bf16[2048,256]{1,0:T(8,128)(2,1)S(1)}) custom-call(s32[3]{0:T(128)S(1)} %pad_add_fusion.1.at_chx, bf16[512,128]{1,0:T(8,128)(2,1)S(1)} %get-tuple-element.31.query, bf16[512,128]{1,0:T(8,128)(2,1)S(1)} %get-tuple-element.32.grad_heads, ...), custom_call_target="tpu_custom_call" | custom-call | tf_op jit(solution)/shard_map/pallas_call | solution.py:244
  144.4 1.0 copy-done.3
  145.4 1.0 copy-done.7
  147.0 2.5 collective-permute-done.5.far
  149.5 1.2 copy-done.4
  151.0 1.0 copy-done.2
  152.0 3.1 %collective-permute-start.6 = (bf16[32,16,256]{2,1,0:T(8,128)(2,1)S(1)}, bf16[32,16,256]{2,1,0:T(8,128)(2,1)S(1)}, u32[]{:S(2)}, u32[]{:S(2)}) collective-permute-start(bf16[32,16,256]{2,1,0:T(8,128)(2,1)S(1)} %get-tuple-element.38), channel_id=1, source_target_pairs={{0,4},{4,0},{1,5},{5,1},{2,6},{6,2},{3,7},{7,3},{8,12},{12,8},{9,1... | collective-permute-start | bytes 786440 | tf_op jit(solution)/shard_map/ppermute | solution.py:30
  155.0 4.4 %all-to-all-start.3 = ((bf16[4,512,256]{2,1,0:T(8,128)(2,1)}), bf16[4,512,256]{2,1,0:T(8,128)(2,1)}, u32[]{:S(2)}, u32[]{:S(2)}) async-start(bf16[4,512,256]{2,1,0:T(8,128)(2,1)} %bitcast.95), calls=%async_computation.3 | async-start | bytes 2097152 | tf_op jit(solution)/shard_map/all_to_all | solution.py:45
  159.5 13.0 %collective-permute-done.6 = bf16[32,16,256]{2,1,0:T(8,128)(2,1)S(1)} collective-permute-done((bf16[32,16,256]{2,1,0:T(8,128)(2,1)S(1)}, bf16[32,16,256]{2,1,0:T(8,128)(2,1)S(1)}, u32[]{:S(2)}, u32[]{:S(2)}) %collective-permute-start.6) | collective-permute-done | bytes 262176 | tf_op jit(solution)/shard_map/ppermute | solution.py:30
  172.6 6.1 %shard_map.148 = (bf16[128,4096]{1,0:T(8,128)(2,1)S(1)}, f32[128,4096]{1,0:T(8,128)S(1)}) custom-call(bf16[128,1024]{1,0:T(8,128)(2,1)} %get-tuple-element.34.att_gq, bf16[4096,1280]{1,0:T(8,128)(2,1)} %all-gather.3.cloned.1.call-done.weights, bf16[2,32,16,256]{3,2,1,0:T(8,128)(2,1)S(1)} %pad_maximum_fusion.2.waited.refs_0_), custom_call_target="tpu_custom_call" | custom-call | tf_op jit(solution)/shard_map/pallas_call | solution.py:267
  179.0 1.1 slice_bitcast_fusion.4
  180.3 2.9 collective-permute-start.9
  184.7 2.4 collective-permute-start.13
  187.2 1.6 collective-permute-start.14
  188.8 2.2 reduce_sum.50
  190.9 8.1 %all-to-all-start.4 = ((bf16[4,128,256]{2,1,0:T(8,128)(2,1)}), bf16[4,128,256]{2,1,0:T(8,128)(2,1)S(1)}, u32[]{:S(2)}, u32[]{:S(2)}) async-start(bf16[4,128,256]{2,1,0:T(8,128)(2,1)} %bitcast.26), calls=%async_computation.4 | async-start | bytes 524288 | tf_op jit(solution)/shard_map/all_to_all | solution.py:45
  199.8 2.1 fusion.6
  202.0 7.6 %all-to-all-done.4 = bf16[4,128,256]{2,1,0:T(8,128)(2,1)S(1)} async-done(((bf16[4,128,256]{2,1,0:T(8,128)(2,1)}), bf16[4,128,256]{2,1,0:T(8,128)(2,1)S(1)}, u32[]{:S(2)}, u32[]{:S(2)}) %all-to-all-start.4) | async-done | bytes 262176 | tf_op jit(solution)/shard_map/all_to_all | solution.py:45
  209.8 1.6 copy-done.1
  211.5 3.3 %shard_map.149 = (bf16[128,4096]{1,0:T(8,128)(2,1)S(1)}, f32[1,4096]{1,0:T(1,128)S(1)}) custom-call(f32[128,4096]{1,0:T(8,128)S(1)} %copy-done.1, bf16[128,256]{1,0:T(8,128)(2,1)S(1)} %pad_maximum_fusion.8.grad_kv, bf16[4096,1280]{1,0:T(8,128)(2,1)} %all-gather.3.cloned.1.call-done.weights, bf16[128,8192]{1,0:T(8,128)(2,1)S(1)} %bitcast.89), custom_call_target="tpu_custom_call" | custom-call | tf_op jit(solution)/shard_map/pallas_call | solution.py:295
  214.8 1.0 copy-done.5
  216.6 4.0 %all-to-all-start.5 = ((bf16[4,144,256]{2,1,0:T(8,128)(2,1)}), bf16[4,144,256]{2,1,0:T(8,128)(2,1)S(1)}, u32[]{:S(2)}, u32[]{:S(2)}) async-start(bf16[4,144,256]{2,1,0:T(8,128)(2,1)} %broadcast_in_dim.15), calls=%async_computation.5 | async-start | bytes 589824 | tf_op jit(solution)/shard_map/all_to_all | solution.py:39
  220.6 2.1 fusion.35
  222.7 0.8 collective-permute-start.12
  223.5 1.2 collective-permute-start.11
  224.6 1.4 collective-permute-start.10
  226.0 2.1 all-to-all-done.5
  228.1 1.1 broadcast_in_dim.16
  229.3 3.5 %all-to-all-start.6 = ((bf16[4,4,144,256]{3,2,1,0:T(8,128)(2,1)}), bf16[4,4,144,256]{3,2,1,0:T(8,128)(2,1)S(1)}, u32[]{:S(2)}, u32[]{:S(2)}) async-start(bf16[4,4,144,256]{3,2,1,0:T(8,128)(2,1)} %broadcast_in_dim.16), calls=%async_computation.6 | async-start | bytes 2359296 | tf_op jit(solution)/shard_map/all_to_all | solution.py:39
  232.8 1.0 fusion.22.second
  233.8 1.5 collective-permute-start.15
  235.3 10.5 %all-to-all-done.6 = bf16[4,4,144,256]{3,2,1,0:T(8,128)(2,1)S(1)} async-done(((bf16[4,4,144,256]{3,2,1,0:T(8,128)(2,1)}), bf16[4,4,144,256]{3,2,1,0:T(8,128)(2,1)S(1)}, u32[]{:S(2)}, u32[]{:S(2)}) %all-to-all-start.6) | async-done | bytes 1179680 | tf_op jit(solution)/shard_map/all_to_all | solution.py:39
  245.8 1.2 fusion.4
  247.8 0.8 collective-permute-done.16.refs_5_
  248.7 3.0 %shard_map.150.waited = bf16[144,256]{1,0:T(8,128)(2,1)S(1)} custom-call(s32[1]{0:T(128)} %bitcast.core, bf16[2,32,16,256]{3,2,1,0:T(8,128)(2,1)S(1)} %pad_maximum_fusion.2.waited.refs_0_, bf16[2,32,16,256]{3,2,1,0:T(8,128)(2,1)S(1)} %collective-permute-done.13.refs_1_, bf16[2,32,16,256]{3,2,1,0:T(8,128)(2,1)} %collective-permute-done.14.refs_2_, ...), custom_call_target="tpu_custom_call" | custom-call | tf_op jit(solution)/shard_map/pallas_call | solution.py:377
  251.7 4.5 %collective-permute-start.18 = (bf16[16,4096]{1,0:T(8,128)(2,1)S(1)}, bf16[16,4096]{1,0:T(8,128)(2,1)S(1)}, u32[]{:S(2)}, u32[]{:S(2)}) collective-permute-start(bf16[16,4096]{1,0:T(8,128)(2,1)S(1)} %get-tuple-element.46), channel_id=1, source_target_pairs={{0,4},{4,0},{1,5},{5,1},{2,6},{6,2},{3,7},{7,3},{8,12},{12,8},{9,1... | collective-permute-start | bytes 393224 | tf_op jit(solution)/shard_map/ppermute | solution.py:30
  256.2 1.5 collective-permute-start.17
  258.4 4.8 %all-to-all-start.7 = ((bf16[4,144,256]{2,1,0:T(8,128)(2,1)}), bf16[4,144,256]{2,1,0:T(8,128)(2,1)S(1)}, u32[]{:S(2)}, u32[]{:S(2)}) async-start(bf16[4,144,256]{2,1,0:T(8,128)(2,1)} %broadcast_in_dim.17), calls=%async_computation.7 | async-start | bytes 589824 | tf_op jit(solution)/shard_map/all_to_all | solution.py:39
  263.2 4.2 %collective-permute-done.18 = bf16[16,4096]{1,0:T(8,128)(2,1)S(1)} collective-permute-done((bf16[16,4096]{1,0:T(8,128)(2,1)S(1)}, bf16[16,4096]{1,0:T(8,128)(2,1)S(1)}, u32[]{:S(2)}, u32[]{:S(2)}) %collective-permute-start.18) | collective-permute-done | bytes 131104 | tf_op jit(solution)/shard_map/ppermute | solution.py:30
  267.4 1.2 fusion.11
  268.7 5.9 %shard_map.152 = (f32[128,512]{1,0:T(8,128)}, f32[128,512]{1,0:T(8,128)}) custom-call(bf16[2,32,16,256]{3,2,1,0:T(8,128)(2,1)S(1)} %pad_maximum_fusion.2.waited.refs_0_, bf16[2,32,16,256]{3,2,1,0:T(8,128)(2,1)S(1)} %collective-permute-done.13.refs_1_, bf16[2,32,16,256]{3,2,1,0:T(8,128)(2,1)} %collective-permute-done.14.refs_2_, ...), custom_call_target="tpu_custom_call" | custom-call | tf_op jit(solution)/shard_map/pallas_call | solution.py:336
  274.6 0.9 copy-done.6
  275.6 3.6 %collective-permute-start.19 = (bf16[2,144,256]{2,1,0:T(8,128)(2,1)S(1)}, bf16[2,144,256]{2,1,0:T(8,128)(2,1)S(1)}, u32[]{:S(2)}, u32[]{:S(2)}) collective-permute-start(bf16[2,144,256]{2,1,0:T(8,128)(2,1)S(1)} %shard_map.153), channel_id=1, source_target_pairs={{0,4},{4,0},{1,5},{5,1},{2,6},{6,2},{3,7},{7,3},{8,12},{12,8},{9,1... | collective-permute-start | bytes 442376 | tf_op jit(solution)/shard_map/ppermute | solution.py:30
  279.2 2.0 fusion.15
  281.2 3.6 %collective-permute-done.19 = bf16[2,144,256]{2,1,0:T(8,128)(2,1)S(1)} collective-permute-done((bf16[2,144,256]{2,1,0:T(8,128)(2,1)S(1)}, bf16[2,144,256]{2,1,0:T(8,128)(2,1)S(1)}, u32[]{:S(2)}, u32[]{:S(2)}) %collective-permute-start.19) | collective-permute-done | bytes 147488 | tf_op jit(solution)/shard_map/ppermute | solution.py:30
  (126 shorter events, 11.9 us)
Async XLA Ops:
  7.2 12.2 %copy-start.10 = (bf16[16,4096]{1,0:T(8,128)(2,1)S(1)}, bf16[16,4096]{1,0:T(8,128)(2,1)}, u32[]{:S(2)}) copy-start(bf16[16,4096]{1,0:T(8,128)(2,1)} %param.9) | copy-start | bytes 393220
  7.2 12.2 %copy-start.17 = (f32[4096]{0:T(1024)S(1)}, f32[4096]{0:T(1024)}, u32[]{:S(2)}) copy-start(f32[4096]{0:T(1024)} %param.11) | copy-start | bytes 49156
  7.2 12.2 %copy-start.14 = (bf16[16,4096]{1,0:T(8,128)(2,1)S(1)}, bf16[16,4096]{1,0:T(8,128)(2,1)}, u32[]{:S(2)}) copy-start(bf16[16,4096]{1,0:T(8,128)(2,1)} %param.16) | copy-start | bytes 393220
  7.2 20.1 %copy-start.15 = (bf16[1,128,4096]{2,1,0:T(8,128)(2,1)S(1)}, bf16[1,128,4096]{2,1,0:T(8,128)(2,1)}, u32[]{:S(2)}) copy-start(bf16[1,128,4096]{2,1,0:T(8,128)(2,1)} %param.10) | copy-start | bytes 3145732
  7.2 86.8 %all-gather.3.cloned.1.call-start = ((), (), s32[]{:S(2)}) async-start(), calls=%async_computation.8 | async-start | bytes 10813440 | tf_op jit(solution)/shard_map/all_gather | solution.py:455
  11.0 16.4 %copy-start.19 = (f32[16]{0:T(128)}, f32[16]{0:T(128)S(1)}, u32[]{:S(2)}) copy-start(f32[16]{0:T(128)S(1)} %add_rsqrt_fusion) | copy-start | bytes 196
  12.0 15.4 %copy-start.18 = (s32[4096]{0:T(1024)S(1)}, s32[4096]{0:T(1024)}, u32[]{:S(2)}) copy-start(s32[4096]{0:T(1024)} %param.17) | copy-start | bytes 49156
  13.0 24.2 %collective-permute-start = (bf16[16,8192]{1,0:T(8,128)(2,1)S(1)}, bf16[16,8192]{1,0:T(8,128)(2,1)S(1)}, u32[]{:S(2)}, u32[]{:S(2)}) collective-permute-start(bf16[16,8192]{1,0:T(8,128)(2,1)S(1)} %get-tuple-element.61), channel_id=1, source_target_pairs={{0,4},{4,0},{1,5},{5,1},{2,6},{6,2},{3,7},{7,3},{8,12},{12,8},{9,1... | collective-permute-start | bytes 786440 | tf_op jit(solution)/shard_map/ppermute | solution.py:30
  20.2 38.7 %all-to-all-start = ((bf16[32,16,256]{2,1,0:T(8,128)(2,1)}), bf16[32,16,256]{2,1,0:T(8,128)(2,1)S(1)}, u32[]{:S(2)}, u32[]{:S(2)}) async-start(bf16[32,16,256]{2,1,0:T(8,128)(2,1)} %maximum_bitcast_fusion), calls=%async_computation | async-start | bytes 524288 | tf_op jit(solution)/shard_map/all_to_all | solution.py:468
  27.2 241.5 %all-gather.5.cloned.1.call-start = ((), (), s32[]{:S(2)}) async-start(), calls=%async_computation.9 | async-start | bytes 8650752 | tf_op jit(solution)/shard_map/all_gather | solution.py:514
  37.2 15.7 %collective-permute-start.3 = (bf16[2,16,8192]{2,1,0:T(8,128)(2,1)S(1)}, bf16[2,16,8192]{2,1,0:T(8,128)(2,1)S(1)}, u32[]{:S(2)}, u32[]{:S(2)}) collective-permute-start(bf16[2,16,8192]{2,1,0:T(8,128)(2,1)S(1)} %get-tuple-element.57), channel_id=1, source_target_pairs={{3,0},{0,1},{1,2},{2,3},{7,4},{4,5},{5,6},{6,7},{11,8},{8,9},{9,10... | collective-permute-start | bytes 1572872 | tf_op jit(solution)/shard_map/ppermute | solution.py:34
  38.8 19.8 %collective-permute-start.2 = (bf16[2,16,8192]{2,1,0:T(8,128)(2,1)S(1)}, bf16[2,16,8192]{2,1,0:T(8,128)(2,1)S(1)}, u32[]{:S(2)}, u32[]{:S(2)}) collective-permute-start(bf16[2,16,8192]{2,1,0:T(8,128)(2,1)S(1)} %get-tuple-element.57), channel_id=1, source_target_pairs={{2,0},{3,1},{0,2},{1,3},{6,4},{7,5},{4,6},{5,7},{10,8},{11,9},{8,1... | collective-permute-start | bytes 1572872 | tf_op jit(solution)/shard_map/ppermute | solution.py:34
  41.5 17.1 %collective-permute-start.1 = (bf16[2,16,8192]{2,1,0:T(8,128)(2,1)S(1)}, bf16[2,16,8192]{2,1,0:T(8,128)(2,1)S(1)}, u32[]{:S(2)}, u32[]{:S(2)}) collective-permute-start(bf16[2,16,8192]{2,1,0:T(8,128)(2,1)S(1)} %get-tuple-element.57), channel_id=1, source_target_pairs={{1,0},{2,1},{3,2},{0,3},{5,4},{6,5},{7,6},{4,7},{9,8},{10,9},{11,1... | collective-permute-start | bytes 1572872 | tf_op jit(solution)/shard_map/ppermute | solution.py:34
  126.3 5.2 %collective-permute-start.4 = (bf16[2048,256]{1,0:T(8,128)(2,1)S(1)}, bf16[2048,256]{1,0:T(8,128)(2,1)S(1)}, u32[]{:S(2)}, u32[]{:S(2)}) collective-permute-start(bf16[2048,256]{1,0:T(8,128)(2,1)S(1)} %bitcast.92), channel_id=1, source_target_pairs={{0,8},{8,0},{1,9},{9,1},{2,10},{10,2},{3,11},{11,3},{4,12},{12,4},... | collective-permute-start | bytes 3145736 | tf_op jit(solution)/shard_map/ppermute | solution.py:30
  144.4 1.0 copy-start.3
  145.4 1.0 copy-start.7
  146.4 3.1 %collective-permute-start.5 = (bf16[2048,256]{1,0:T(8,128)(2,1)}, bf16[2048,256]{1,0:T(8,128)(2,1)S(1)}, u32[]{:S(2)}, u32[]{:S(2)}) collective-permute-start(bf16[2048,256]{1,0:T(8,128)(2,1)} %copy-done.7), channel_id=1, source_target_pairs={{0,8},{8,0},{1,9},{9,1},{2,10},{10,2},{3,11},{11,3},{4,12},{12,4},... | collective-permute-start | bytes 3145736 | tf_op jit(solution)/shard_map/ppermute | solution.py:30
  149.5 1.2 copy-start.4
  151.0 1.0 copy-start.2
  152.0 20.6 %collective-permute-start.6 = (bf16[32,16,256]{2,1,0:T(8,128)(2,1)S(1)}, bf16[32,16,256]{2,1,0:T(8,128)(2,1)S(1)}, u32[]{:S(2)}, u32[]{:S(2)}) collective-permute-start(bf16[32,16,256]{2,1,0:T(8,128)(2,1)S(1)} %get-tuple-element.38), channel_id=1, source_target_pairs={{0,4},{4,0},{1,5},{5,1},{2,6},{6,2},{3,7},{7,3},{8,12},{12,8},{9,1... | collective-permute-start | bytes 786440 | tf_op jit(solution)/shard_map/ppermute | solution.py:30
  155.0 33.7 %all-to-all-start.3 = ((bf16[4,512,256]{2,1,0:T(8,128)(2,1)}), bf16[4,512,256]{2,1,0:T(8,128)(2,1)}, u32[]{:S(2)}, u32[]{:S(2)}) async-start(bf16[4,512,256]{2,1,0:T(8,128)(2,1)} %bitcast.95), calls=%async_computation.3 | async-start | bytes 2097152 | tf_op jit(solution)/shard_map/all_to_all | solution.py:45
  172.6 6.2 %copy-start.8 = (bf16[4,2,16,4096]{3,2,1,0:T(8,128)(2,1)S(1)}, bf16[4,2,16,4096]{3,2,1,0:T(8,128)(2,1)}, u32[]{:S(2)}) copy-start(bf16[4,2,16,4096]{3,2,1,0:T(8,128)(2,1)} %fusion.2) | copy-start | bytes 3145732
  178.7 1.6 copy-start
  179.0 5.7 %copy-start.9 = (bf16[4,2,16,4096]{3,2,1,0:T(8,128)(2,1)}, bf16[4,2,16,4096]{3,2,1,0:T(8,128)(2,1)S(1)}, u32[]{:S(2)}) copy-start(bf16[4,2,16,4096]{3,2,1,0:T(8,128)(2,1)S(1)} %fusion) | copy-start | bytes 3145732
  180.3 18.7 %collective-permute-start.9 = (bf16[2,16,4096]{2,1,0:T(8,128)(2,1)}, bf16[2,16,4096]{2,1,0:T(8,128)(2,1)}, u32[]{:S(2)}, u32[]{:S(2)}) collective-permute-start(bf16[2,16,4096]{2,1,0:T(8,128)(2,1)} %get-tuple-element.54), channel_id=1, source_target_pairs={{1,0},{2,1},{3,2},{0,3},{5,4},{6,5},{7,6},{4,7},{9,8},{10,9},{11,1... | collective-permute-start | bytes 786440 | tf_op jit(solution)/shard_map/ppermute | solution.py:34
  183.2 15.9 %collective-permute-start.8 = (bf16[2,16,4096]{2,1,0:T(8,128)(2,1)}, bf16[2,16,4096]{2,1,0:T(8,128)(2,1)}, u32[]{:S(2)}, u32[]{:S(2)}) collective-permute-start(bf16[2,16,4096]{2,1,0:T(8,128)(2,1)} %get-tuple-element.55), channel_id=1, source_target_pairs={{2,0},{3,1},{0,2},{1,3},{6,4},{7,5},{4,6},{5,7},{10,8},{11,9},{8,1... | collective-permute-start | bytes 786440 | tf_op jit(solution)/shard_map/ppermute | solution.py:34
  183.9 15.9 %collective-permute-start.7 = (bf16[2,16,4096]{2,1,0:T(8,128)(2,1)}, bf16[2,16,4096]{2,1,0:T(8,128)(2,1)}, u32[]{:S(2)}, u32[]{:S(2)}) collective-permute-start(bf16[2,16,4096]{2,1,0:T(8,128)(2,1)} %get-tuple-element.53), channel_id=1, source_target_pairs={{3,0},{0,1},{1,2},{2,3},{7,4},{4,5},{5,6},{6,7},{11,8},{8,9},{9,10... | collective-permute-start | bytes 786440 | tf_op jit(solution)/shard_map/ppermute | solution.py:34
  184.7 62.4 %collective-permute-start.13 = (bf16[2,32,16,256]{3,2,1,0:T(8,128)(2,1)S(1)}, bf16[2,32,16,256]{3,2,1,0:T(8,128)(2,1)S(1)}, u32[]{:S(2)}, u32[]{:S(2)}) collective-permute-start(bf16[2,32,16,256]{3,2,1,0:T(8,128)(2,1)S(1)} %pad_maximum_fusion.2.waited.refs_0_), channel_id=1, source_target_pairs={{1,0},{2,1},{3,2},{0,3},{5,4},{6,5},{7,6},{4,7},{9,8},{10,9},{11,1... | collective-permute-start | bytes 1572872 | tf_op jit(solution)/shard_map/ppermute | solution.py:34
  187.2 59.9 %collective-permute-start.14 = (bf16[2,32,16,256]{3,2,1,0:T(8,128)(2,1)S(1)}, bf16[2,32,16,256]{3,2,1,0:T(8,128)(2,1)}, u32[]{:S(2)}, u32[]{:S(2)}) collective-permute-start(bf16[2,32,16,256]{3,2,1,0:T(8,128)(2,1)S(1)} %pad_maximum_fusion.2.waited.refs_0_), channel_id=1, source_target_pairs={{2,0},{3,1},{0,2},{1,3},{6,4},{7,5},{4,6},{5,7},{10,8},{11,9},{8,1... | collective-permute-start | bytes 1572872 | tf_op jit(solution)/shard_map/ppermute | solution.py:34
  190.9 18.6 %all-to-all-start.4 = ((bf16[4,128,256]{2,1,0:T(8,128)(2,1)}), bf16[4,128,256]{2,1,0:T(8,128)(2,1)S(1)}, u32[]{:S(2)}, u32[]{:S(2)}) async-start(bf16[4,128,256]{2,1,0:T(8,128)(2,1)} %bitcast.26), calls=%async_computation.4 | async-start | bytes 524288 | tf_op jit(solution)/shard_map/all_to_all | solution.py:45
  209.8 1.6 copy-start.1
  214.8 1.0 copy-start.5
  216.6 11.5 %all-to-all-start.5 = ((bf16[4,144,256]{2,1,0:T(8,128)(2,1)}), bf16[4,144,256]{2,1,0:T(8,128)(2,1)S(1)}, u32[]{:S(2)}, u32[]{:S(2)}) async-start(bf16[4,144,256]{2,1,0:T(8,128)(2,1)} %broadcast_in_dim.15), calls=%async_computation.5 | async-start | bytes 589824 | tf_op jit(solution)/shard_map/all_to_all | solution.py:39
  222.7 11.1 %collective-permute-start.12 = (bf16[2,16,4096]{2,1,0:T(8,128)(2,1)S(1)}, bf16[2,16,4096]{2,1,0:T(8,128)(2,1)}, u32[]{:S(2)}, u32[]{:S(2)}) collective-permute-start(bf16[2,16,4096]{2,1,0:T(8,128)(2,1)S(1)} %bitcast.105), channel_id=1, source_target_pairs={{1,0},{2,1},{3,2},{0,3},{5,4},{6,5},{7,6},{4,7},{9,8},{10,9},{11,1... | collective-permute-start | bytes 786440 | tf_op jit(solution)/shard_map/ppermute | solution.py:34
  223.5 11.8 %collective-permute-start.11 = (bf16[2,16,4096]{2,1,0:T(8,128)(2,1)}, bf16[2,16,4096]{2,1,0:T(8,128)(2,1)}, u32[]{:S(2)}, u32[]{:S(2)}) collective-permute-start(bf16[2,16,4096]{2,1,0:T(8,128)(2,1)} %bitcast.29), channel_id=1, source_target_pairs={{2,0},{3,1},{0,2},{1,3},{6,4},{7,5},{4,6},{5,7},{10,8},{11,9},{8,1... | collective-permute-start | bytes 786440 | tf_op jit(solution)/shard_map/ppermute | solution.py:34
  224.6 21.2 %collective-permute-start.10 = (bf16[2,16,4096]{2,1,0:T(8,128)(2,1)}, bf16[2,16,4096]{2,1,0:T(8,128)(2,1)}, u32[]{:S(2)}, u32[]{:S(2)}) collective-permute-start(bf16[2,16,4096]{2,1,0:T(8,128)(2,1)} %bitcast.28), channel_id=1, source_target_pairs={{3,0},{0,1},{1,2},{2,3},{7,4},{4,5},{5,6},{6,7},{11,8},{8,9},{9,10... | collective-permute-start | bytes 786440 | tf_op jit(solution)/shard_map/ppermute | solution.py:34
  229.3 16.5 %all-to-all-start.6 = ((bf16[4,4,144,256]{3,2,1,0:T(8,128)(2,1)}), bf16[4,4,144,256]{3,2,1,0:T(8,128)(2,1)S(1)}, u32[]{:S(2)}, u32[]{:S(2)}) async-start(bf16[4,4,144,256]{3,2,1,0:T(8,128)(2,1)} %broadcast_in_dim.16), calls=%async_computation.6 | async-start | bytes 2359296 | tf_op jit(solution)/shard_map/all_to_all | solution.py:39
  233.8 13.4 %collective-permute-start.15 = (bf16[2,32,16,256]{3,2,1,0:T(8,128)(2,1)S(1)}, bf16[2,32,16,256]{3,2,1,0:T(8,128)(2,1)S(1)}, u32[]{:S(2)}, u32[]{:S(2)}) collective-permute-start(bf16[2,32,16,256]{3,2,1,0:T(8,128)(2,1)S(1)} %pad_maximum_fusion.2.waited.refs_0_), channel_id=1, source_target_pairs={{3,0},{0,1},{1,2},{2,3},{7,4},{4,5},{5,6},{6,7},{11,8},{8,9},{9,10... | collective-permute-start | bytes 1572872 | tf_op jit(solution)/shard_map/ppermute | solution.py:34
  245.8 2.8 collective-permute-start.16
  247.0 0.8 copy-start.12
  247.1 20.3 %copy-start.11 = (bf16[16,4096]{1,0:T(8,128)(2,1)S(1)}, bf16[16,4096]{1,0:T(8,128)(2,1)}, u32[]{:S(2)}) copy-start(bf16[16,4096]{1,0:T(8,128)(2,1)} %param.9) | copy-start | bytes 393220
  247.1 20.3 %copy-start.20 = (f32[16]{0:T(128)S(1)}, f32[16]{0:T(128)}, u32[]{:S(2)}) copy-start(f32[16]{0:T(128)} %copy-done.19) | copy-start | bytes 196
  251.7 15.8 %collective-permute-start.18 = (bf16[16,4096]{1,0:T(8,128)(2,1)S(1)}, bf16[16,4096]{1,0:T(8,128)(2,1)S(1)}, u32[]{:S(2)}, u32[]{:S(2)}) collective-permute-start(bf16[16,4096]{1,0:T(8,128)(2,1)S(1)} %get-tuple-element.46), channel_id=1, source_target_pairs={{0,4},{4,0},{1,5},{5,1},{2,6},{6,2},{3,7},{7,3},{8,12},{12,8},{9,1... | collective-permute-start | bytes 393224 | tf_op jit(solution)/shard_map/ppermute | solution.py:30
  256.2 23.0 %collective-permute-start.17 = (bf16[16,4096]{1,0:T(8,128)(2,1)S(1)}, bf16[16,4096]{1,0:T(8,128)(2,1)}, u32[]{:S(2)}, u32[]{:S(2)}) collective-permute-start(bf16[16,4096]{1,0:T(8,128)(2,1)S(1)} %get-tuple-element.45), channel_id=1, source_target_pairs={{0,4},{4,0},{1,5},{5,1},{2,6},{6,2},{3,7},{7,3},{8,12},{12,8},{9,1... | collective-permute-start | bytes 393224 | tf_op jit(solution)/shard_map/ppermute | solution.py:30
  258.4 16.2 %all-to-all-start.7 = ((bf16[4,144,256]{2,1,0:T(8,128)(2,1)}), bf16[4,144,256]{2,1,0:T(8,128)(2,1)S(1)}, u32[]{:S(2)}, u32[]{:S(2)}) async-start(bf16[4,144,256]{2,1,0:T(8,128)(2,1)} %broadcast_in_dim.17), calls=%async_computation.7 | async-start | bytes 589824 | tf_op jit(solution)/shard_map/all_to_all | solution.py:39
  267.4 7.2 %copy-start.16 = (bf16[16,4096]{1,0:T(8,128)(2,1)}, bf16[16,4096]{1,0:T(8,128)(2,1)S(1)}, u32[]{:S(2)}) copy-start(bf16[16,4096]{1,0:T(8,128)(2,1)S(1)} %collective-permute-done.18) | copy-start | bytes 393220
  268.7 10.5 %copy-start.13 = (f32[2,16,4096]{2,1,0:T(8,128)S(1)}, f32[2,16,4096]{2,1,0:T(8,128)}, u32[]{:S(2)}) copy-start(f32[2,16,4096]{2,1,0:T(8,128)} %copy-done.12) | copy-start | bytes 1572868
  268.7 10.5 %copy-start.21 = (f32[16]{0:T(128)S(1)}, f32[16]{0:T(128)}, u32[]{:S(2)}) copy-start(f32[16]{0:T(128)} %copy-done.19) | copy-start | bytes 196
  274.6 1.0 copy-start.6
  275.6 9.1 %collective-permute-start.19 = (bf16[2,144,256]{2,1,0:T(8,128)(2,1)S(1)}, bf16[2,144,256]{2,1,0:T(8,128)(2,1)S(1)}, u32[]{:S(2)}, u32[]{:S(2)}) collective-permute-start(bf16[2,144,256]{2,1,0:T(8,128)(2,1)S(1)} %shard_map.153), channel_id=1, source_target_pairs={{0,4},{4,0},{1,5},{5,1},{2,6},{6,2},{3,7},{7,3},{8,12},{12,8},{9,1... | collective-permute-start | bytes 442376 | tf_op jit(solution)/shard_map/ppermute | solution.py:30
Sparse Core Ops, SparseCore 0:
  10.1 83.9 all-gather.2
  146.5 83.7 all-gather.4

commit v3 on v2

--- a/solution.py
+++ b/solution.py
@@ -406,19 +406,17 @@
     )(first, second, waited)
 
 
-def add_kernel(near, far, rows, out, rows_out):
-    out[...] = (near[...].astype(wide) + far[...].astype(wide)).astype(low)
-    rows_out[...] = rows[...]
-
-
-def add(near, far, rows):
-    vmem = pl.BlockSpec(memory_space=pltpu.VMEM)
-    return pl.pallas_call(
-        add_kernel,
-        in_specs=[vmem, vmem, vmem],
-        out_shape=[jax.ShapeDtypeStruct(a.shape, low) for a in (near, rows)],
-        compiler_params=PARAMS,
-    )(near, far, rows)
+def wait_kernel(value, waited, out):
+    out[...] = value[...]
+
+
+def wait(value, waited):
+    return pl.pallas_call(
+        wait_kernel,
+        in_specs=[pl.BlockSpec(memory_space=pltpu.VMEM), ANY],
+        out_shape=jax.ShapeDtypeStruct(value.shape, value.dtype),
+        compiler_params=PARAMS,
+    )(value, waited)
 
 
 def pair_kernel(sums, waited, out):
@@ -453,8 +451,13 @@
         lax.dynamic_slice_in_dim(w, kv_first, HEAD_DIM, 1) for w in (k_weight, v_weight)
     ]
     weights = lax.all_gather(
-        jnp.concatenate([q_weight, out_weight] + kv_weights, axis=1), DP, axis=0, tiled=True
-    )
+        jnp.concatenate([q_weight, out_weight], axis=1), DP, axis=0, tiled=True
+    )
+    near = spread(jnp.concatenate(kv_weights, axis=1), "z").reshape(-1, 2 * HEAD_DIM)
+    near = spread(near, "y").reshape(outer, 1, block, 2 * HEAD_DIM)
+    far = swap(near, "c")
+    natural = [jnp.where(c == 0, near, far), jnp.where(c == 0, far, near)]
+    wkv = jnp.concatenate(natural, axis=1).reshape(width, 2 * HEAD_DIM)
 
     stream_f = stream_in.astype(wide)
     inv_rms = lax.rsqrt(jnp.mean(stream_f * stream_f, axis=-1, keepdims=True) + eps)
@@ -465,7 +468,6 @@
 
     split = [a.reshape(rows_own, n_dp, block) for a in (grad_out, normed_own)]
     rows = jnp.transpose(jnp.concatenate(split, axis=2), (1, 0, 2))
-    rows = lax.all_to_all(rows, DP, 0, 0, tiled=True)
 
     def index(axis):
         return lax.broadcasted_iota(jnp.int32, (NX, 2, rows_own), axis)
@@ -494,24 +496,26 @@
 
     pend = relative(pending[0])
     bounds = jnp.stack([places, first_place])
-    both, rows, pend, bounds, cosine, sine = lax.optimization_barrier(
-        (both, rows, pend, bounds, cosine, sine)
-    )
-    kv_own = kv_project(both, weights, cosine, sine)
+    both, pend, bounds, cosine, sine = lax.optimization_barrier(
+        (both, pend, bounds, cosine, sine)
+    )
+    kv_own = kv_project(both, wkv, cosine, sine)
     kv_near = spread(kv_own, "z").reshape(-1, 2 * HEAD_DIM)
     query, grad_heads = project(both, weights, cosine, sine, 2 * q_width)
     kv_near = spread(kv_near, "y").reshape(-1, 2 * HEAD_DIM)
     kv_far = swap(kv_near, "c")
+    rows = lax.all_to_all(wait(rows, kv_near), DP, 0, 0, tiled=True)
     at_chx = jnp.stack([c, h, x]).astype(jnp.int32)
     att_gq, near_piece, far_piece = attend(
         at_chx, query, grad_heads, kv_near, kv_far, bounds, cosine, sine
     )
-    kv_sum, rows = add(near_piece, swap(far_piece, "c"), rows)
-    kv_sum = kv_sum.reshape(SIZES["y"], -1, 2 * HEAD_DIM)
+    att_gq_all = lax.all_gather(wait(att_gq, rows), DP, axis=0, tiled=True)
+    kv_sum = near_piece.astype(wide) + swap(far_piece, "c").astype(wide)
+    kv_sum = kv_sum.astype(low).reshape(SIZES["y"], -1, 2 * HEAD_DIM)
+    rows = wait(rows, kv_sum)
     rows = spread_h(rows)
     terms, query_terms = back_project(att_gq, weights, rows)
     kv_sum = collect(kv_sum, "y").astype(low)
-    att_gq_all = lax.all_gather(att_gq, DP, axis=0, tiled=True)
     kv_grad = collect(kv_sum.reshape(SIZES["z"], tok, 2 * HEAD_DIM), "z")
     grad_key = rotate(kv_grad[:, :HEAD_DIM], -1.0)
     grad_kv = jnp.concatenate([grad_key, kv_grad[:, HEAD_DIM:]], axis=1).astype(low)
@@ -519,7 +523,7 @@
     terms = terms.reshape(NX, 2, rows_own, width).astype(wide) + pend.astype(wide)
     hidden_part, hidden_other = collect_x(terms.astype(low))
 
-    normed_terms, gain_terms = normed_grad(query_terms, grad_kv, weights, both)
+    normed_terms, gain_terms = normed_grad(query_terms, grad_kv, wkv, both)
     gain_rows = gain_terms.astype(low).reshape(-1, 2 * HEAD_DIM)
     depth = tok + gain_rows.shape[0]
     near = spread(jnp.concatenate([grad_kv, gain_rows], axis=0), "z")

time: 296 us -> 287 us (0.970)
  waiting for transfers between devices: 102 us -> 89.2 us
  blocking collectives: 29.1 us -> 33.7 us
  other arithmetic: 19.7 us -> 24.2 us
    all_gather x2, waiting for transfers between devices: 35.2 us -> 0.02 us  [the longest x1 0.02 us: on_device(): att_gq_all = lax.all_gather(wait(att_gq, rows), DP, axis=0, tiled=True)]
    all_to_all x3 -> x5, waiting for transfers between devices: 12.6 us -> 42.5 us  [spread(): lax.all_to_all(jnp.broadcast_to(a[None], (size,) + a.shape), axis, 0, 0,...]
    all_to_all x3 -> x5, starting transfers between devices: 12.3 us -> 20 us  [spread(): lax.all_to_all(jnp.broadcast_to(a[None], (size,) + a.shape), axis, 0, 0,...]
    ppermute x12, waiting for transfers between devices: 15 us -> 9.59 us  [shift(): return lax.ppermute(a, 'x', [((i + step) % NX, i) for i in range(NX)])]
    all_to_all x2, blocking collectives: 29.1 us -> 33.7 us  [spread(): lax.all_to_all(jnp.broadcast_to(a[None], (size,) + a.shape), axis, 0, 0,...]
    ppermute x8 -> x9, starting transfers between devices: 19.6 us -> 16 us  [swap(): return lax.ppermute(a, axis, [(0, 1), (1, 0)])]
    another operation x2, other arithmetic: 0.33 us -> 3.61 us  [on_device(): both = jnp.stack(spread_x(both)).reshape(tok, 2 * width)]
    unnamed x45 -> x49, local copies, waits for them, and re-layouts: 8.73 us -> 5.87 us
  transfers between devices with their start and end apart: 28 -> 31, of which waited for: 13 -> 12; matrix products, arithmetic and copies ran while one was open for 8% -> 11% of each run, Pallas kernels for 8% -> 13%
where the time goes in v3:
time: 287 us; the launch traced here: 286 us
  waiting for transfers between devices  89.2 us (31%)
  starting transfers between devices  69 us (24%)
  Pallas kernels  38.2 us (13%)
  blocking collectives  33.7 us (12%)
  other arithmetic  24.2 us (8%)
  local copies, waits for them, and re-layouts  16.5 us (6%)
  between operations  14.7 us (5%)
    all_to_all x5, waiting for transfers between devices, spread(): lax.all_to_all(jnp.broadcast_to(a[None], (size,) + a.shape), axis, 0, 0,...  42.5 us
    all_to_all x2, blocking collectives, spread(): lax.all_to_all(jnp.broadcast_to(a[None], (size,) + a.shape), axis, 0, 0,...  33.7 us
    ppermute x9, waiting for transfers between devices, swap(): return lax.ppermute(a, axis, [(0, 1), (1, 0)])  30.7 us
    all_to_all x5, starting transfers between devices, spread(): lax.all_to_all(jnp.broadcast_to(a[None], (size,) + a.shape), axis, 0, 0,...  20 us
    ppermute x12, starting transfers between devices, shift(): return lax.ppermute(a, 'x', [((i + step) % NX, i) for i in range(NX)])  18.3 us
    ppermute x9, starting transfers between devices, swap(): return lax.ppermute(a, axis, [(0, 1), (1, 0)])  16 us
    pallas_call x1, Pallas kernels, attend(): pl.pallas_call(attend_kernel, in_specs=[pl.BlockSpec(memory_space=pltpu.S...  12.9 us
    all_to_all x2, starting transfers between devices, collect(): lax.all_to_all(a, axis, 0, 0, tiled=True).astype(wide)  10.3 us
  transfers between devices with their start and end apart: 31, of which 12 were waited for; matrix products, arithmetic and copies ran while one was open for 11% of the time, Pallas kernels for 13%

profile of v3, /device:TPU:32, one launch (start us, length us, event | category | flops | bytes accessed | tf_op | source)
XLA Modules:
  0.0 285.6 jit_solution(893241631022714608)
XLA Ops:
  7.2 1.8 pad_maximum_fusion.5
  9.0 1.1 fusion.16
  10.1 1.0 fusion.10
  11.1 1.6 fusion.33
  12.8 6.3 %collective-permute-start = (bf16[16,8192]{1,0:T(8,128)(2,1)}, bf16[16,8192]{1,0:T(8,128)(2,1)}, u32[]{:S(2)}, u32[]{:S(2)}) collective-permute-start(bf16[16,8192]{1,0:T(8,128)(2,1)} %get-tuple-element.57), channel_id=1, source_target_pairs={{0,4},{4,0},{1,5},{5,1},{2,6},{6,2},{3,7},{7,3},{8,12},{12,8},{9,1... | collective-permute-start | bytes 786440 | tf_op jit(solution)/shard_map/ppermute | solution.py:30
  20.6 4.4 %all-to-all-start = ((bf16[4,128,256]{2,1,0:T(8,128)(2,1)}), bf16[4,128,256]{2,1,0:T(8,128)(2,1)S(1)}, u32[]{:S(2)}, u32[]{:S(2)}) async-start(bf16[4,128,256]{2,1,0:T(8,128)(2,1)} %broadcast_in_dim.18), calls=%async_computation | async-start | bytes 524288 | tf_op jit(solution)/shard_map/all_to_all | solution.py:39
  27.1 14.5 %all-to-all-done = bf16[4,128,256]{2,1,0:T(8,128)(2,1)S(1)} async-done(((bf16[4,128,256]{2,1,0:T(8,128)(2,1)}), bf16[4,128,256]{2,1,0:T(8,128)(2,1)S(1)}, u32[]{:S(2)}, u32[]{:S(2)}) %all-to-all-start) | async-done | bytes 262176 | tf_op jit(solution)/shard_map/all_to_all | solution.py:39
  41.6 1.1 broadcast_in_dim.20
  42.7 4.5 %all-to-all-start.1 = ((bf16[4,512,256]{2,1,0:T(8,128)(2,1)}), bf16[4,512,256]{2,1,0:T(8,128)(2,1)S(1)}, u32[]{:S(2)}, u32[]{:S(2)}) async-start(bf16[4,512,256]{2,1,0:T(8,128)(2,1)} %broadcast_in_dim.20), calls=%async_computation.1 | async-start | bytes 2097152 | tf_op jit(solution)/shard_map/all_to_all | solution.py:39
  47.1 1.8 fusion.34
  49.0 1.5 collective-permute-start.3
  50.5 2.8 collective-permute-start.2
  53.2 1.4 collective-permute-start.1
  54.6 1.4 fusion.2
  56.0 13.1 %all-to-all-done.1 = bf16[4,512,256]{2,1,0:T(8,128)(2,1)S(1)} async-done(((bf16[4,512,256]{2,1,0:T(8,128)(2,1)}), bf16[4,512,256]{2,1,0:T(8,128)(2,1)S(1)}, u32[]{:S(2)}, u32[]{:S(2)}) %all-to-all-start.1) | async-done | bytes 1048608 | tf_op jit(solution)/shard_map/all_to_all | solution.py:39
  69.1 6.7 %collective-permute-done.2 = bf16[2,16,8192]{2,1,0:T(8,128)(2,1)} collective-permute-done((bf16[2,16,8192]{2,1,0:T(8,128)(2,1)S(1)}, bf16[2,16,8192]{2,1,0:T(8,128)(2,1)}, u32[]{:S(2)}, u32[]{:S(2)}) %collective-permute-start.2) | collective-permute-done | bytes 524320 | tf_op jit(solution)/shard_map/ppermute | solution.py:34
  75.8 1.8 pad_maximum_fusion
  78.0 1.2 shard_map.145
  79.6 14.9 %all_to_all.50 = bf16[4,128,256]{2,1,0:T(8,128)(2,1)S(1)} all-to-all(bf16[4,128,256]{2,1,0:T(8,128)(2,1)S(1)} %broadcast_in_dim.21), channel_id=1, replica_groups=mesh['y'=4,'z'=4,'c'=2,'h'=2,'x'=4] {'z'}, dimensions={0} | all-to-all | bytes 524288 | tf_op jit(solution)/shard_map/all_to_all | solution.py:39
  94.6 18.8 %all_to_all.51 = bf16[4,512,256]{2,1,0:T(8,128)(2,1)S(1)} all-to-all(bf16[4,512,256]{2,1,0:T(8,128)(2,1)S(1)} %broadcast_in_dim.23), channel_id=1, replica_groups=mesh['y'=4,'z'=4,'c'=2,'h'=2,'x'=4] {'y'}, dimensions={0} | all-to-all | bytes 2097152 | tf_op jit(solution)/shard_map/all_to_all | solution.py:39
  114.3 4.4 %all-to-all-start.4 = ((bf16[32,16,256]{2,1,0:T(8,128)(2,1)}), bf16[32,16,256]{2,1,0:T(8,128)(2,1)S(1)}, u32[]{:S(2)}, u32[]{:S(2)}) async-start(bf16[32,16,256]{2,1,0:T(8,128)(2,1)} %copy-done.6), calls=%async_computation.4 | async-start | bytes 524288 | tf_op jit(solution)/shard_map/all_to_all | solution.py:507
  118.8 5.1 %shard_map.144 = (bf16[512,128]{1,0:T(8,128)(2,1)S(1)}, bf16[512,128]{1,0:T(8,128)(2,1)S(1)}) custom-call(bf16[128,8192]{1,0:T(8,128)(2,1)S(1)} %bitcast.90, bf16[128,8192]{1,0:T(8,128)(2,1)S(1)} %bitcast.91, bf16[4096,1024]{1,0:T(8,128)(2,1)} %all-gather.3.cloned.1.call-done.weights, f32[128,128]{1,0:T(8,128)S(1)} %get-tuple-element.26.cosine, ...), custom_call_target="tpu_custom_call" | custom-call | tf_op jit(solution)/shard_map/pallas_call | solution.py:140
  124.0 12.9 %shard_map.146 = (bf16[128,1024]{1,0:T(8,128)(2,1)S(1)}, bf16[2048,256]{1,0:T(8,128)(2,1)S(1)}, bf16[2048,256]{1,0:T(8,128)(2,1)S(1)}) custom-call(s32[3]{0:T(128)S(1)} %pad_add_fusion.1.at_chx, bf16[512,128]{1,0:T(8,128)(2,1)S(1)} %get-tuple-element.28.query, bf16[512,128]{1,0:T(8,128)(2,1)S(1)} %get-tuple-element.29.grad_heads, ...), custom_call_target="tpu_custom_call" | custom-call | tf_op jit(solution)/shard_map/pallas_call | solution.py:244
  137.0 1.0 copy-done.8
  139.1 2.7 collective-permute-done.6
  141.9 1.3 add_convert_fusion
  144.1 4.2 %all-to-all-start.5 = ((bf16[4,512,256]{2,1,0:T(8,128)(2,1)}), bf16[4,512,256]{2,1,0:T(8,128)(2,1)}, u32[]{:S(2)}, u32[]{:S(2)}) async-start(bf16[4,512,256]{2,1,0:T(8,128)(2,1)} %bitcast.20.waited), calls=%async_computation.5 | async-start | bytes 2097152 | tf_op jit(solution)/shard_map/all_to_all | solution.py:45
  148.4 16.9 %collective-permute-done.7 = bf16[32,16,256]{2,1,0:T(8,128)(2,1)S(1)} collective-permute-done((bf16[32,16,256]{2,1,0:T(8,128)(2,1)S(1)}, bf16[32,16,256]{2,1,0:T(8,128)(2,1)S(1)}, u32[]{:S(2)}, u32[]{:S(2)}) %collective-permute-start.7) | collective-permute-done | bytes 262176 | tf_op jit(solution)/shard_map/ppermute | solution.py:30
  165.3 6.1 %shard_map.149 = (bf16[128,4096]{1,0:T(8,128)(2,1)S(1)}, f32[128,4096]{1,0:T(8,128)S(1)}) custom-call(bf16[128,1024]{1,0:T(8,128)(2,1)S(1)} %get-tuple-element.31.att_gq.value, bf16[4096,1024]{1,0:T(8,128)(2,1)} %all-gather.3.cloned.1.call-done.weights, bf16[2,32,16,256]{3,2,1,0:T(8,128)(2,1)S(1)} %pad_maximum_fusion.3.waited.refs_0_), custom_call_target="tpu_custom_call" | custom-call | tf_op jit(solution)/shard_map/pallas_call | solution.py:267
  171.7 1.1 slice_bitcast_fusion.4
  173.0 2.5 collective-permute-start.10
  175.5 1.2 collective-permute-start.9
  176.7 3.2 %collective-permute-start.14 = (bf16[2,32,16,256]{3,2,1,0:T(8,128)(2,1)S(1)}, bf16[2,32,16,256]{3,2,1,0:T(8,128)(2,1)S(1)}, u32[]{:S(2)}, u32[]{:S(2)}) collective-permute-start(bf16[2,32,16,256]{3,2,1,0:T(8,128)(2,1)S(1)} %pad_maximum_fusion.3.waited.refs_0_), channel_id=1, source_target_pairs={{1,0},{2,1},{3,2},{0,3},{5,4},{6,5},{7,6},{4,7},{9,8},{10,9},{11,1... | collective-permute-start | bytes 1572872 | tf_op jit(solution)/shard_map/ppermute | solution.py:34
  179.9 1.1 collective-permute-start.15
  181.0 2.1 reduce_sum.50
  183.2 6.0 %all-to-all-start.6 = ((bf16[4,128,256]{2,1,0:T(8,128)(2,1)}), bf16[4,128,256]{2,1,0:T(8,128)(2,1)S(1)}, u32[]{:S(2)}, u32[]{:S(2)}) async-start(bf16[4,128,256]{2,1,0:T(8,128)(2,1)} %bitcast.29), calls=%async_computation.6 | async-start | bytes 524288 | tf_op jit(solution)/shard_map/all_to_all | solution.py:45
  189.2 2.9 %collective-permute-done.8 = bf16[2,16,4096]{2,1,0:T(8,128)(2,1)} collective-permute-done((bf16[2,16,4096]{2,1,0:T(8,128)(2,1)}, bf16[2,16,4096]{2,1,0:T(8,128)(2,1)}, u32[]{:S(2)}, u32[]{:S(2)}) %collective-permute-start.8) | collective-permute-done | bytes 262176 | tf_op jit(solution)/shard_map/ppermute | solution.py:34
  192.1 2.1 fusion.6
  194.2 6.4 %all-to-all-done.6 = bf16[4,128,256]{2,1,0:T(8,128)(2,1)S(1)} async-done(((bf16[4,128,256]{2,1,0:T(8,128)(2,1)}), bf16[4,128,256]{2,1,0:T(8,128)(2,1)S(1)}, u32[]{:S(2)}, u32[]{:S(2)}) %all-to-all-start.6) | async-done | bytes 262176 | tf_op jit(solution)/shard_map/all_to_all | solution.py:45
  200.9 1.6 copy-done.4
  202.5 3.1 %shard_map.150 = (bf16[128,4096]{1,0:T(8,128)(2,1)S(1)}, f32[1,4096]{1,0:T(1,128)S(1)}) custom-call(f32[128,4096]{1,0:T(8,128)S(1)} %copy-done.4, bf16[128,256]{1,0:T(8,128)(2,1)S(1)} %pad_maximum_fusion.10.grad_kv, bf16[4096,256]{1,0:T(8,128)(2,1)S(1)} %bitcast.94, bf16[128,8192]{1,0:T(8,128)(2,1)} %bitcast.92), custom_call_target="tpu_custom_call" | custom-call | tf_op jit(solution)/shard_map/pallas_call | solution.py:295
  205.6 0.9 copy-done.5
  207.4 3.4 %all-to-all-start.7 = ((bf16[4,144,256]{2,1,0:T(8,128)(2,1)}), bf16[4,144,256]{2,1,0:T(8,128)(2,1)S(1)}, u32[]{:S(2)}, u32[]{:S(2)}) async-start(bf16[4,144,256]{2,1,0:T(8,128)(2,1)} %broadcast_in_dim.24), calls=%async_computation.7 | async-start | bytes 589824 | tf_op jit(solution)/shard_map/all_to_all | solution.py:39
  210.8 2.2 fusion.35
  213.8 1.1 collective-permute-start.12
  214.9 1.4 collective-permute-start.11
  216.3 2.4 all-to-all-done.7
  218.7 1.1 broadcast_in_dim.25
  219.8 3.5 %all-to-all-start.8 = ((bf16[4,4,144,256]{3,2,1,0:T(8,128)(2,1)}), bf16[4,4,144,256]{3,2,1,0:T(8,128)(2,1)S(1)}, u32[]{:S(2)}, u32[]{:S(2)}) async-start(bf16[4,4,144,256]{3,2,1,0:T(8,128)(2,1)} %broadcast_in_dim.25), calls=%async_computation.8 | async-start | bytes 2359296 | tf_op jit(solution)/shard_map/all_to_all | solution.py:39
  223.3 1.0 fusion.22.second
  224.3 1.2 collective-permute-start.16
  225.6 12.5 %all-to-all-done.8 = bf16[4,4,144,256]{3,2,1,0:T(8,128)(2,1)S(1)} async-done(((bf16[4,4,144,256]{3,2,1,0:T(8,128)(2,1)}), bf16[4,4,144,256]{3,2,1,0:T(8,128)(2,1)S(1)}, u32[]{:S(2)}, u32[]{:S(2)}) %all-to-all-start.8) | async-done | bytes 1179680 | tf_op jit(solution)/shard_map/all_to_all | solution.py:39
  238.1 1.3 fusion.4
  239.5 1.4 collective-permute-done.17.refs_5_
  240.9 3.0 %shard_map.151.waited = bf16[144,256]{1,0:T(8,128)(2,1)S(1)} custom-call(s32[1]{0:T(128)} %bitcast.core, bf16[2,32,16,256]{3,2,1,0:T(8,128)(2,1)S(1)} %pad_maximum_fusion.3.waited.refs_0_, bf16[2,32,16,256]{3,2,1,0:T(8,128)(2,1)S(1)} %collective-permute-done.14.refs_1_, bf16[2,32,16,256]{3,2,1,0:T(8,128)(2,1)} %collective-permute-done.15.refs_2_, ...), custom_call_target="tpu_custom_call" | custom-call | tf_op jit(solution)/shard_map/pallas_call | solution.py:377
  243.9 3.4 %collective-permute-start.19 = (bf16[16,4096]{1,0:T(8,128)(2,1)S(1)}, bf16[16,4096]{1,0:T(8,128)(2,1)S(1)}, u32[]{:S(2)}, u32[]{:S(2)}) collective-permute-start(bf16[16,4096]{1,0:T(8,128)(2,1)S(1)} %get-tuple-element.40), channel_id=1, source_target_pairs={{0,4},{4,0},{1,5},{5,1},{2,6},{6,2},{3,7},{7,3},{8,12},{12,8},{9,1... | collective-permute-start | bytes 393224 | tf_op jit(solution)/shard_map/ppermute | solution.py:30
  247.3 2.6 collective-permute-start.18
  250.7 4.2 %all-to-all-start.9 = ((bf16[4,144,256]{2,1,0:T(8,128)(2,1)}), bf16[4,144,256]{2,1,0:T(8,128)(2,1)S(1)}, u32[]{:S(2)}, u32[]{:S(2)}) async-start(bf16[4,144,256]{2,1,0:T(8,128)(2,1)} %broadcast_in_dim.26), calls=%async_computation.9 | async-start | bytes 589824 | tf_op jit(solution)/shard_map/all_to_all | solution.py:39
  254.9 4.5 %collective-permute-done.19 = bf16[16,4096]{1,0:T(8,128)(2,1)S(1)} collective-permute-done((bf16[16,4096]{1,0:T(8,128)(2,1)S(1)}, bf16[16,4096]{1,0:T(8,128)(2,1)S(1)}, u32[]{:S(2)}, u32[]{:S(2)}) %collective-permute-start.19) | collective-permute-done | bytes 131104 | tf_op jit(solution)/shard_map/ppermute | solution.py:30
  260.3 5.9 %shard_map.154 = (f32[128,512]{1,0:T(8,128)}, f32[128,512]{1,0:T(8,128)}) custom-call(bf16[2,32,16,256]{3,2,1,0:T(8,128)(2,1)S(1)} %pad_maximum_fusion.3.waited.refs_0_, bf16[2,32,16,256]{3,2,1,0:T(8,128)(2,1)S(1)} %collective-permute-done.14.refs_1_, bf16[2,32,16,256]{3,2,1,0:T(8,128)(2,1)} %collective-permute-done.15.refs_2_, ...), custom_call_target="tpu_custom_call" | custom-call | tf_op jit(solution)/shard_map/pallas_call | solution.py:336
  266.2 0.9 copy-done.7
  267.2 2.4 collective-permute-start.20
  269.6 1.7 fusion.15
  271.4 5.2 %collective-permute-done.20 = bf16[2,144,256]{2,1,0:T(8,128)(2,1)S(1)} collective-permute-done((bf16[2,144,256]{2,1,0:T(8,128)(2,1)S(1)}, bf16[2,144,256]{2,1,0:T(8,128)(2,1)S(1)}, u32[]{:S(2)}, u32[]{:S(2)}) %collective-permute-start.20) | collective-permute-done | bytes 147488 | tf_op jit(solution)/shard_map/ppermute | solution.py:30
  (144 shorter events, 13.9 us)
Async XLA Ops:
  7.2 17.8 %copy-start.16 = (bf16[1,128,4096]{2,1,0:T(8,128)(2,1)S(1)}, bf16[1,128,4096]{2,1,0:T(8,128)(2,1)}, u32[]{:S(2)}) copy-start(bf16[1,128,4096]{2,1,0:T(8,128)(2,1)} %param.10) | copy-start | bytes 3145732
  7.2 111.7 %all-gather.3.cloned.1.call-start = ((), (), s32[]{:S(2)}) async-start(), calls=%async_computation.10 | async-start | bytes 8650752 | tf_op jit(solution)/shard_map/all_gather | solution.py:453
  10.1 103.3 %copy-start.22 = (f32[16]{0:T(128)}, f32[16]{0:T(128)S(1)}, u32[]{:S(2)}) copy-start(f32[16]{0:T(128)S(1)} %add_rsqrt_fusion) | copy-start | bytes 196
  11.1 14.0 %copy-start.21 = (s32[4096]{0:T(1024)S(1)}, s32[4096]{0:T(1024)}, u32[]{:S(2)}) copy-start(s32[4096]{0:T(1024)} %param.17) | copy-start | bytes 49156
  12.8 34.4 %collective-permute-start = (bf16[16,8192]{1,0:T(8,128)(2,1)}, bf16[16,8192]{1,0:T(8,128)(2,1)}, u32[]{:S(2)}, u32[]{:S(2)}) collective-permute-start(bf16[16,8192]{1,0:T(8,128)(2,1)} %get-tuple-element.57), channel_id=1, source_target_pairs={{0,4},{4,0},{1,5},{5,1},{2,6},{6,2},{3,7},{7,3},{8,12},{12,8},{9,1... | collective-permute-start | bytes 786440 | tf_op jit(solution)/shard_map/ppermute | solution.py:30
  20.6 21.0 %all-to-all-start = ((bf16[4,128,256]{2,1,0:T(8,128)(2,1)}), bf16[4,128,256]{2,1,0:T(8,128)(2,1)S(1)}, u32[]{:S(2)}, u32[]{:S(2)}) async-start(bf16[4,128,256]{2,1,0:T(8,128)(2,1)} %broadcast_in_dim.18), calls=%async_computation | async-start | bytes 524288 | tf_op jit(solution)/shard_map/all_to_all | solution.py:39
  42.7 26.4 %all-to-all-start.1 = ((bf16[4,512,256]{2,1,0:T(8,128)(2,1)}), bf16[4,512,256]{2,1,0:T(8,128)(2,1)S(1)}, u32[]{:S(2)}, u32[]{:S(2)}) async-start(bf16[4,512,256]{2,1,0:T(8,128)(2,1)} %broadcast_in_dim.20), calls=%async_computation.1 | async-start | bytes 2097152 | tf_op jit(solution)/shard_map/all_to_all | solution.py:39
  49.0 20.2 %collective-permute-start.3 = (bf16[2,16,8192]{2,1,0:T(8,128)(2,1)S(1)}, bf16[2,16,8192]{2,1,0:T(8,128)(2,1)}, u32[]{:S(2)}, u32[]{:S(2)}) collective-permute-start(bf16[2,16,8192]{2,1,0:T(8,128)(2,1)S(1)} %get-tuple-element.53), channel_id=1, source_target_pairs={{3,0},{0,1},{1,2},{2,3},{7,4},{4,5},{5,6},{6,7},{11,8},{8,9},{9,10... | collective-permute-start | bytes 1572872 | tf_op jit(solution)/shard_map/ppermute | solution.py:34
  50.5 25.3 %collective-permute-start.2 = (bf16[2,16,8192]{2,1,0:T(8,128)(2,1)S(1)}, bf16[2,16,8192]{2,1,0:T(8,128)(2,1)}, u32[]{:S(2)}, u32[]{:S(2)}) collective-permute-start(bf16[2,16,8192]{2,1,0:T(8,128)(2,1)S(1)} %get-tuple-element.53), channel_id=1, source_target_pairs={{2,0},{3,1},{0,2},{1,3},{6,4},{7,5},{4,6},{5,7},{10,8},{11,9},{8,1... | collective-permute-start | bytes 1572872 | tf_op jit(solution)/shard_map/ppermute | solution.py:34
  53.2 22.6 %collective-permute-start.1 = (bf16[2,16,8192]{2,1,0:T(8,128)(2,1)S(1)}, bf16[2,16,8192]{2,1,0:T(8,128)(2,1)}, u32[]{:S(2)}, u32[]{:S(2)}) collective-permute-start(bf16[2,16,8192]{2,1,0:T(8,128)(2,1)S(1)} %get-tuple-element.53), channel_id=1, source_target_pairs={{1,0},{2,1},{3,2},{0,3},{5,4},{6,5},{7,6},{4,7},{9,8},{10,9},{11,1... | collective-permute-start | bytes 1572872 | tf_op jit(solution)/shard_map/ppermute | solution.py:34
  69.1 8.5 %collective-permute-start.4 = (bf16[16,1,128,256]{3,2,1,0:T(8,128)(2,1)S(1)}, bf16[16,1,128,256]{3,2,1,0:T(8,128)(2,1)S(1)}, u32[]{:S(2)}, u32[]{:S(2)}) collective-permute-start(bf16[16,1,128,256]{3,2,1,0:T(8,128)(2,1)S(1)} %bitcast.102), channel_id=1, source_target_pairs={{0,8},{8,0},{1,9},{9,1},{2,10},{10,2},{3,11},{11,3},{4,12},{12,4},... | collective-permute-start | bytes 3145736 | tf_op jit(solution)/shard_map/ppermute | solution.py:30
  77.6 41.2 %copy-start = (bf16[4,2,16,8192]{3,2,1,0:T(8,128)(2,1)}, bf16[4,2,16,8192]{3,2,1,0:T(8,128)(2,1)S(1)}, u32[]{:S(2)}) copy-start(bf16[4,2,16,8192]{3,2,1,0:T(8,128)(2,1)S(1)} %pad_maximum_fusion) | copy-start | bytes 6291460
  78.0 1.6 copy-start.1
  79.6 33.8 %copy-start.11 = (bf16[16,4096]{1,0:T(8,128)(2,1)S(1)}, bf16[16,4096]{1,0:T(8,128)(2,1)}, u32[]{:S(2)}) copy-start(bf16[16,4096]{1,0:T(8,128)(2,1)} %param.9) | copy-start | bytes 393220
  79.6 33.8 %copy-start.14 = (bf16[16,4096]{1,0:T(8,128)(2,1)S(1)}, bf16[16,4096]{1,0:T(8,128)(2,1)}, u32[]{:S(2)}) copy-start(bf16[16,4096]{1,0:T(8,128)(2,1)} %param.16) | copy-start | bytes 393220
  79.6 33.8 %copy-start.17 = (f32[4096]{0:T(1024)S(1)}, f32[4096]{0:T(1024)}, u32[]{:S(2)}) copy-start(f32[4096]{0:T(1024)} %param.11) | copy-start | bytes 49156
  113.4 10.6 %collective-permute-start.5 = (bf16[2048,256]{1,0:T(8,128)(2,1)S(1)}, bf16[2048,256]{1,0:T(8,128)(2,1)}, u32[]{:S(2)}, u32[]{:S(2)}) collective-permute-start(bf16[2048,256]{1,0:T(8,128)(2,1)S(1)} %bitcast.95), channel_id=1, source_target_pairs={{0,8},{8,0},{1,9},{9,1},{2,10},{10,2},{3,11},{11,3},{4,12},{12,4},... | collective-permute-start | bytes 3145736 | tf_op jit(solution)/shard_map/ppermute | solution.py:30
  113.6 0.7 copy-start.6
  114.3 23.7 %all-to-all-start.4 = ((bf16[32,16,256]{2,1,0:T(8,128)(2,1)}), bf16[32,16,256]{2,1,0:T(8,128)(2,1)S(1)}, u32[]{:S(2)}, u32[]{:S(2)}) async-start(bf16[32,16,256]{2,1,0:T(8,128)(2,1)} %copy-done.6), calls=%async_computation.4 | async-start | bytes 524288 | tf_op jit(solution)/shard_map/all_to_all | solution.py:507
  118.7 141.6 %all-gather.5.cloned.1.call-start = ((), (), s32[]{:S(2)}) async-start(), calls=%async_computation.11 | async-start | bytes 8650752 | tf_op jit(solution)/shard_map/all_gather | solution.py:512
  137.0 1.0 copy-start.8
  138.7 3.1 %collective-permute-start.6 = (bf16[2048,256]{1,0:T(8,128)(2,1)}, bf16[2048,256]{1,0:T(8,128)(2,1)S(1)}, u32[]{:S(2)}, u32[]{:S(2)}) collective-permute-start(bf16[2048,256]{1,0:T(8,128)(2,1)} %copy-done.8), channel_id=1, source_target_pairs={{0,8},{8,0},{1,9},{9,1},{2,10},{10,2},{3,11},{11,3},{4,12},{12,4},... | collective-permute-start | bytes 3145736 | tf_op jit(solution)/shard_map/ppermute | solution.py:30
  143.2 22.0 %collective-permute-start.7 = (bf16[32,16,256]{2,1,0:T(8,128)(2,1)S(1)}, bf16[32,16,256]{2,1,0:T(8,128)(2,1)S(1)}, u32[]{:S(2)}, u32[]{:S(2)}) collective-permute-start(bf16[32,16,256]{2,1,0:T(8,128)(2,1)S(1)} %shard_map.148), channel_id=1, source_target_pairs={{0,4},{4,0},{1,5},{5,1},{2,6},{6,2},{3,7},{7,3},{8,12},{12,8},{9,1... | collective-permute-start | bytes 786440 | tf_op jit(solution)/shard_map/ppermute | solution.py:30
  144.1 36.9 %all-to-all-start.5 = ((bf16[4,512,256]{2,1,0:T(8,128)(2,1)}), bf16[4,512,256]{2,1,0:T(8,128)(2,1)}, u32[]{:S(2)}, u32[]{:S(2)}) async-start(bf16[4,512,256]{2,1,0:T(8,128)(2,1)} %bitcast.20.waited), calls=%async_computation.5 | async-start | bytes 2097152 | tf_op jit(solution)/shard_map/all_to_all | solution.py:45
  165.3 6.1 %copy-start.9 = (bf16[4,2,16,4096]{3,2,1,0:T(8,128)(2,1)S(1)}, bf16[4,2,16,4096]{3,2,1,0:T(8,128)(2,1)}, u32[]{:S(2)}) copy-start(bf16[4,2,16,4096]{3,2,1,0:T(8,128)(2,1)} %fusion.2) | copy-start | bytes 3145732
  171.4 1.6 copy-start.3
  171.7 5.1 %copy-start.10 = (bf16[4,2,16,4096]{3,2,1,0:T(8,128)(2,1)}, bf16[4,2,16,4096]{3,2,1,0:T(8,128)(2,1)S(1)}, u32[]{:S(2)}) copy-start(bf16[4,2,16,4096]{3,2,1,0:T(8,128)(2,1)S(1)} %fusion) | copy-start | bytes 3145732
  173.0 16.2 %collective-permute-start.10 = (bf16[2,16,4096]{2,1,0:T(8,128)(2,1)}, bf16[2,16,4096]{2,1,0:T(8,128)(2,1)}, u32[]{:S(2)}, u32[]{:S(2)}) collective-permute-start(bf16[2,16,4096]{2,1,0:T(8,128)(2,1)} %get-tuple-element.50), channel_id=1, source_target_pairs={{1,0},{2,1},{3,2},{0,3},{5,4},{6,5},{7,6},{4,7},{9,8},{10,9},{11,1... | collective-permute-start | bytes 786440 | tf_op jit(solution)/shard_map/ppermute | solution.py:34
  175.5 13.7 %collective-permute-start.9 = (bf16[2,16,4096]{2,1,0:T(8,128)(2,1)}, bf16[2,16,4096]{2,1,0:T(8,128)(2,1)}, u32[]{:S(2)}, u32[]{:S(2)}) collective-permute-start(bf16[2,16,4096]{2,1,0:T(8,128)(2,1)} %get-tuple-element.51), channel_id=1, source_target_pairs={{2,0},{3,1},{0,2},{1,3},{6,4},{7,5},{4,6},{5,7},{10,8},{11,9},{8,1... | collective-permute-start | bytes 786440 | tf_op jit(solution)/shard_map/ppermute | solution.py:34
  176.7 24.2 %copy-start.2 = (bf16[16,2,128,256]{3,2,1,0:T(8,128)(2,1)S(1)}, bf16[16,2,128,256]{3,2,1,0:T(8,128)(2,1)}, u32[]{:S(2)}) copy-start(bf16[16,2,128,256]{3,2,1,0:T(8,128)(2,1)} %copy-done.1) | copy-start | bytes 6291460
  176.7 15.4 %collective-permute-start.8 = (bf16[2,16,4096]{2,1,0:T(8,128)(2,1)}, bf16[2,16,4096]{2,1,0:T(8,128)(2,1)}, u32[]{:S(2)}, u32[]{:S(2)}) collective-permute-start(bf16[2,16,4096]{2,1,0:T(8,128)(2,1)} %get-tuple-element.49), channel_id=1, source_target_pairs={{3,0},{0,1},{1,2},{2,3},{7,4},{4,5},{5,6},{6,7},{11,8},{8,9},{9,10... | collective-permute-start | bytes 786440 | tf_op jit(solution)/shard_map/ppermute | solution.py:34
  176.7 62.7 %collective-permute-start.14 = (bf16[2,32,16,256]{3,2,1,0:T(8,128)(2,1)S(1)}, bf16[2,32,16,256]{3,2,1,0:T(8,128)(2,1)S(1)}, u32[]{:S(2)}, u32[]{:S(2)}) collective-permute-start(bf16[2,32,16,256]{3,2,1,0:T(8,128)(2,1)S(1)} %pad_maximum_fusion.3.waited.refs_0_), channel_id=1, source_target_pairs={{1,0},{2,1},{3,2},{0,3},{5,4},{6,5},{7,6},{4,7},{9,8},{10,9},{11,1... | collective-permute-start | bytes 1572872 | tf_op jit(solution)/shard_map/ppermute | solution.py:34
  179.9 59.6 %collective-permute-start.15 = (bf16[2,32,16,256]{3,2,1,0:T(8,128)(2,1)S(1)}, bf16[2,32,16,256]{3,2,1,0:T(8,128)(2,1)}, u32[]{:S(2)}, u32[]{:S(2)}) collective-permute-start(bf16[2,32,16,256]{3,2,1,0:T(8,128)(2,1)S(1)} %pad_maximum_fusion.3.waited.refs_0_), channel_id=1, source_target_pairs={{2,0},{3,1},{0,2},{1,3},{6,4},{7,5},{4,6},{5,7},{10,8},{11,9},{8,1... | collective-permute-start | bytes 1572872 | tf_op jit(solution)/shard_map/ppermute | solution.py:34
  183.2 17.4 %all-to-all-start.6 = ((bf16[4,128,256]{2,1,0:T(8,128)(2,1)}), bf16[4,128,256]{2,1,0:T(8,128)(2,1)S(1)}, u32[]{:S(2)}, u32[]{:S(2)}) async-start(bf16[4,128,256]{2,1,0:T(8,128)(2,1)} %bitcast.29), calls=%async_computation.6 | async-start | bytes 524288 | tf_op jit(solution)/shard_map/all_to_all | solution.py:45
  200.9 1.6 copy-start.4
  205.6 1.0 copy-start.5
  207.4 11.3 %all-to-all-start.7 = ((bf16[4,144,256]{2,1,0:T(8,128)(2,1)}), bf16[4,144,256]{2,1,0:T(8,128)(2,1)S(1)}, u32[]{:S(2)}, u32[]{:S(2)}) async-start(bf16[4,144,256]{2,1,0:T(8,128)(2,1)} %broadcast_in_dim.24), calls=%async_computation.7 | async-start | bytes 589824 | tf_op jit(solution)/shard_map/all_to_all | solution.py:39
  213.0 11.3 %collective-permute-start.13 = (bf16[2,16,4096]{2,1,0:T(8,128)(2,1)}, bf16[2,16,4096]{2,1,0:T(8,128)(2,1)S(1)}, u32[]{:S(2)}, u32[]{:S(2)}) collective-permute-start(bf16[2,16,4096]{2,1,0:T(8,128)(2,1)} %bitcast.33), channel_id=1, source_target_pairs={{1,0},{2,1},{3,2},{0,3},{5,4},{6,5},{7,6},{4,7},{9,8},{10,9},{11,1... | collective-permute-start | bytes 786440 | tf_op jit(solution)/shard_map/ppermute | solution.py:34
  213.8 11.8 %collective-permute-start.12 = (bf16[2,16,4096]{2,1,0:T(8,128)(2,1)}, bf16[2,16,4096]{2,1,0:T(8,128)(2,1)S(1)}, u32[]{:S(2)}, u32[]{:S(2)}) collective-permute-start(bf16[2,16,4096]{2,1,0:T(8,128)(2,1)} %bitcast.32), channel_id=1, source_target_pairs={{2,0},{3,1},{0,2},{1,3},{6,4},{7,5},{4,6},{5,7},{10,8},{11,9},{8,1... | collective-permute-start | bytes 786440 | tf_op jit(solution)/shard_map/ppermute | solution.py:34
  214.9 23.2 %collective-permute-start.11 = (bf16[2,16,4096]{2,1,0:T(8,128)(2,1)}, bf16[2,16,4096]{2,1,0:T(8,128)(2,1)}, u32[]{:S(2)}, u32[]{:S(2)}) collective-permute-start(bf16[2,16,4096]{2,1,0:T(8,128)(2,1)} %bitcast.31), channel_id=1, source_target_pairs={{3,0},{0,1},{1,2},{2,3},{7,4},{4,5},{5,6},{6,7},{11,8},{8,9},{9,10... | collective-permute-start | bytes 786440 | tf_op jit(solution)/shard_map/ppermute | solution.py:34
  219.8 18.3 %all-to-all-start.8 = ((bf16[4,4,144,256]{3,2,1,0:T(8,128)(2,1)}), bf16[4,4,144,256]{3,2,1,0:T(8,128)(2,1)S(1)}, u32[]{:S(2)}, u32[]{:S(2)}) async-start(bf16[4,4,144,256]{3,2,1,0:T(8,128)(2,1)} %broadcast_in_dim.25), calls=%async_computation.8 | async-start | bytes 2359296 | tf_op jit(solution)/shard_map/all_to_all | solution.py:39
  224.3 13.8 %copy-start.19 = (bf16[2,16,4096]{2,1,0:T(8,128)(2,1)}, bf16[2,16,4096]{2,1,0:T(8,128)(2,1)S(1)}, u32[]{:S(2)}) copy-start(bf16[2,16,4096]{2,1,0:T(8,128)(2,1)S(1)} %collective-permute-done.13) | copy-start | bytes 786436
  224.3 15.2 %collective-permute-start.16 = (bf16[2,32,16,256]{3,2,1,0:T(8,128)(2,1)S(1)}, bf16[2,32,16,256]{3,2,1,0:T(8,128)(2,1)S(1)}, u32[]{:S(2)}, u32[]{:S(2)}) collective-permute-start(bf16[2,32,16,256]{3,2,1,0:T(8,128)(2,1)S(1)} %pad_maximum_fusion.3.waited.refs_0_), channel_id=1, source_target_pairs={{3,0},{0,1},{1,2},{2,3},{7,4},{4,5},{5,6},{6,7},{11,8},{8,9},{9,10... | collective-permute-start | bytes 1572872 | tf_op jit(solution)/shard_map/ppermute | solution.py:34
  225.6 12.5 %copy-start.20 = (bf16[2,16,4096]{2,1,0:T(8,128)(2,1)}, bf16[2,16,4096]{2,1,0:T(8,128)(2,1)S(1)}, u32[]{:S(2)}) copy-start(bf16[2,16,4096]{2,1,0:T(8,128)(2,1)S(1)} %collective-permute-done.12) | copy-start | bytes 786436
  238.1 2.8 collective-permute-start.17
  239.4 19.9 %copy-start.12 = (bf16[16,4096]{1,0:T(8,128)(2,1)S(1)}, bf16[16,4096]{1,0:T(8,128)(2,1)}, u32[]{:S(2)}) copy-start(bf16[16,4096]{1,0:T(8,128)(2,1)} %param.9) | copy-start | bytes 393220
  239.4 19.9 %copy-start.18 = (f32[4096]{0:T(1024)S(1)}, f32[4096]{0:T(1024)}, u32[]{:S(2)}) copy-start(f32[4096]{0:T(1024)} %param.11) | copy-start | bytes 49156
  243.9 15.4 %collective-permute-start.19 = (bf16[16,4096]{1,0:T(8,128)(2,1)S(1)}, bf16[16,4096]{1,0:T(8,128)(2,1)S(1)}, u32[]{:S(2)}, u32[]{:S(2)}) collective-permute-start(bf16[16,4096]{1,0:T(8,128)(2,1)S(1)} %get-tuple-element.40), channel_id=1, source_target_pairs={{0,4},{4,0},{1,5},{5,1},{2,6},{6,2},{3,7},{7,3},{8,12},{12,8},{9,1... | collective-permute-start | bytes 393224 | tf_op jit(solution)/shard_map/ppermute | solution.py:30
  247.3 22.3 %collective-permute-start.18 = (bf16[16,4096]{1,0:T(8,128)(2,1)S(1)}, bf16[16,4096]{1,0:T(8,128)(2,1)}, u32[]{:S(2)}, u32[]{:S(2)}) collective-permute-start(bf16[16,4096]{1,0:T(8,128)(2,1)S(1)} %get-tuple-element.39), channel_id=1, source_target_pairs={{0,4},{4,0},{1,5},{5,1},{2,6},{6,2},{3,7},{7,3},{8,12},{12,8},{9,1... | collective-permute-start | bytes 393224 | tf_op jit(solution)/shard_map/ppermute | solution.py:30
  250.7 15.6 %all-to-all-start.9 = ((bf16[4,144,256]{2,1,0:T(8,128)(2,1)}), bf16[4,144,256]{2,1,0:T(8,128)(2,1)S(1)}, u32[]{:S(2)}, u32[]{:S(2)}) async-start(bf16[4,144,256]{2,1,0:T(8,128)(2,1)} %broadcast_in_dim.26), calls=%async_computation.9 | async-start | bytes 589824 | tf_op jit(solution)/shard_map/all_to_all | solution.py:39
  260.2 9.4 %copy-start.13 = (f32[2,16,4096]{2,1,0:T(8,128)S(1)}, f32[2,16,4096]{2,1,0:T(8,128)}, u32[]{:S(2)}) copy-start(f32[2,16,4096]{2,1,0:T(8,128)} %fusion.6) | copy-start | bytes 1572868
  260.2 9.4 %copy-start.15 = (bf16[16,4096]{1,0:T(8,128)(2,1)S(1)}, bf16[16,4096]{1,0:T(8,128)(2,1)}, u32[]{:S(2)}) copy-start(bf16[16,4096]{1,0:T(8,128)(2,1)} %param.16) | copy-start | bytes 393220
  260.3 9.4 %copy-start.23 = (f32[16]{0:T(128)S(1)}, f32[16]{0:T(128)}, u32[]{:S(2)}) copy-start(f32[16]{0:T(128)} %copy-done.22) | copy-start | bytes 196
  266.2 1.0 copy-start.7
  267.2 9.4 %collective-permute-start.20 = (bf16[2,144,256]{2,1,0:T(8,128)(2,1)S(1)}, bf16[2,144,256]{2,1,0:T(8,128)(2,1)S(1)}, u32[]{:S(2)}, u32[]{:S(2)}) collective-permute-start(bf16[2,144,256]{2,1,0:T(8,128)(2,1)S(1)} %shard_map.155), channel_id=1, source_target_pairs={{0,4},{4,0},{1,5},{5,1},{2,6},{6,2},{3,7},{7,3},{8,12},{12,8},{9,1... | collective-permute-start | bytes 442376 | tf_op jit(solution)/shard_map/ppermute | solution.py:30
Sparse Core Ops, SparseCore 0:
  10.4 92.2 all-gather.2
  138.8 82.8 all-gather.4

commit v4 on v3

--- a/solution.py
+++ b/solution.py
@@ -257,7 +257,7 @@
 def back_project_kernel(att_gq, weights, waited, terms, grad):
     half = att_gq.shape[1] // 2
     terms[...] = dot(att_gq[:, :half], weights[:, half:], ((1,), (1,))).astype(low)
-    grad[...] = dot(att_gq[:, half:], weights[:, :half], ((1,), (1,)))
+    grad[...] = dot(att_gq[:, half:], weights[:, :half], ((1,), (1,))).astype(low)
 
 
 def back_project(att_gq, weights, waited, step=1024):
@@ -275,14 +275,14 @@
         out_specs=[out, out],
         out_shape=[
             jax.ShapeDtypeStruct((tok, width), low),
-            jax.ShapeDtypeStruct((tok, width), wide),
+            jax.ShapeDtypeStruct((tok, width), low),
         ],
         compiler_params=PARAMS,
     )(att_gq, weights, waited)
 
 
 def normed_grad_kernel(query_terms, grad_kv, weights, normed, terms, gain):
-    total = query_terms[...] + dot(grad_kv[...], weights[...], ((1,), (1,)))
+    total = query_terms[...].astype(wide) + dot(grad_kv[...], weights[...], ((1,), (1,)))
     terms[...] = total.astype(low)
     gain[...] = jnp.sum(total * normed[...].astype(wide), axis=0, keepdims=True)
 
@@ -345,7 +345,7 @@
 
 
 def kv_weight_grad_kernel(core, *refs):
-    rows, (near, far, out, total, gains) = refs[:NX], refs[NX:]
+    rows, (near, far, _, out, total, gains) = refs[:NX], refs[NX:]
     block = rows[0].shape[3] // 2
     tok = near.shape[1] - gains.shape[1]
     step = pl.program_id(0)
@@ -368,7 +368,7 @@
         out[total.shape[0] :] = (gains[0] + gains[1]).astype(low)
 
 
-def kv_weight_grad(core, rows, near, far, tok, step=4):
+def kv_weight_grad(core, rows, near, far, waited, tok, step=4):
     two, n_dp, rows_own, both = rows[0].shape
     outer, depth, cols = near.shape
     kv = pl.BlockSpec((step, depth, cols), lambda i, c: (i, 0, 0))
@@ -379,7 +379,7 @@
         grid_spec=pltpu.PrefetchScalarGridSpec(
             num_scalar_prefetch=1,
             grid=(outer // step,),
-            in_specs=[part] * NX + [kv, kv],
+            in_specs=[part] * NX + [kv, kv, ANY],
             out_specs=pl.BlockSpec(out.shape, lambda i, c: (0, 0)),
             scratch_shapes=[
                 pltpu.VMEM((both // 2, cols), wide),
@@ -388,22 +388,7 @@
         ),
         out_shape=out,
         compiler_params=PARAMS,
-    )(core, *rows, near, far)
-
-
-def hold_kernel(first, second, waited, first_out, second_out):
-    first_out[...] = first[...]
-    second_out[...] = second[...]
-
-
-def hold(first, second, waited):
-    vmem = pl.BlockSpec(memory_space=pltpu.VMEM)
-    return pl.pallas_call(
-        hold_kernel,
-        in_specs=[vmem, vmem, ANY],
-        out_shape=[jax.ShapeDtypeStruct(a.shape, a.dtype) for a in (first, second)],
-        compiler_params=PARAMS,
-    )(first, second, waited)
+    )(core, *rows, near, far, waited)
 
 
 def wait_kernel(value, waited, out):
@@ -529,14 +514,14 @@
     near = spread(jnp.concatenate([grad_kv, gain_rows], axis=0), "z")
     near = spread(near, "y").reshape(outer, depth, 2 * HEAD_DIM)
     rows = spread_x(rows)
-    sums = kv_weight_grad(c.astype(jnp.int32)[None], rows, near, swap(near, "c"), tok)
+    hidden_other = swap(hidden_other, "h")
+    sums = kv_weight_grad(
+        c.astype(jnp.int32)[None], rows, near, swap(near, "c"), hidden_other, tok
+    )
 
     normed_part, normed_other = collect_x(normed_terms.reshape(NX, 2, rows_own, width))
-    normed_other, hidden_other = hold(normed_other, hidden_other, sums)
-    normed_other = swap(normed_other, "h")
+    normed_other = swap(wait(normed_other, sums), "h")
     grad_normed = normed_part + normed_other.astype(wide)
-
-    hidden_other = swap(hidden_other, "h")
     hidden_out = (stream_f + (hidden_part + hidden_other.astype(wide))).astype(low)
 
     sums = spread(sums, "x")

time: 287 us -> 285 us (level)
  no operation moved by 1% of the time
where the time goes in v4:
time: 285 us; the launch traced here: 283 us
  waiting for transfers between devices  88.4 us (31%)
  starting transfers between devices  69.2 us (24%)
  Pallas kernels  38.1 us (13%)
  blocking collectives  33.3 us (12%)
  other arithmetic  23.3 us (8%)
  local copies, waits for them, and re-layouts  16.5 us (6%)
  between operations  14.7 us (5%)
    all_to_all x5, waiting for transfers between devices, spread(): lax.all_to_all(jnp.broadcast_to(a[None], (size,) + a.shape), axis, 0, 0,...  39.7 us
    all_to_all x2, blocking collectives, spread(): lax.all_to_all(jnp.broadcast_to(a[None], (size,) + a.shape), axis, 0, 0,...  33.3 us
    ppermute x9, waiting for transfers between devices, swap(): return lax.ppermute(a, axis, [(0, 1), (1, 0)])  32.5 us
    all_to_all x5, starting transfers between devices, spread(): lax.all_to_all(jnp.broadcast_to(a[None], (size,) + a.shape), axis, 0, 0,...  19.4 us
    ppermute x12, starting transfers between devices, shift(): return lax.ppermute(a, 'x', [((i + step) % NX, i) for i in range(NX)])  18.7 us
    ppermute x9, starting transfers between devices, swap(): return lax.ppermute(a, axis, [(0, 1), (1, 0)])  16.4 us
    pallas_call x1, Pallas kernels, attend(): pl.pallas_call(attend_kernel, in_specs=[pl.BlockSpec(memory_space=pltpu.S...  12.9 us
    ppermute x12, waiting for transfers between devices, shift(): return lax.ppermute(a, 'x', [((i + step) % NX, i) for i in range(NX)])  9.92 us
  transfers between devices with their start and end apart: 31, of which 12 were waited for; matrix products, arithmetic and copies ran while one was open for 11% of the time, Pallas kernels for 13%

profile of v4, /device:TPU:32, one launch (start us, length us, event | category | flops | bytes accessed | tf_op | source)
XLA Modules:
  0.0 283.4 jit_solution(5645867734848742063)
XLA Ops:
  7.2 1.8 pad_maximum_fusion.5
  9.0 1.1 fusion.16
  10.1 1.0 fusion.10
  11.1 1.6 fusion.33
  12.8 6.3 %collective-permute-start = (bf16[16,8192]{1,0:T(8,128)(2,1)}, bf16[16,8192]{1,0:T(8,128)(2,1)}, u32[]{:S(2)}, u32[]{:S(2)}) collective-permute-start(bf16[16,8192]{1,0:T(8,128)(2,1)} %get-tuple-element.53), channel_id=1, source_target_pairs={{0,4},{4,0},{1,5},{5,1},{2,6},{6,2},{3,7},{7,3},{8,12},{12,8},{9,1... | collective-permute-start | bytes 786440 | tf_op jit(solution)/shard_map/ppermute | solution.py:30
  20.6 4.4 %all-to-all-start = ((bf16[4,128,256]{2,1,0:T(8,128)(2,1)}), bf16[4,128,256]{2,1,0:T(8,128)(2,1)S(1)}, u32[]{:S(2)}, u32[]{:S(2)}) async-start(bf16[4,128,256]{2,1,0:T(8,128)(2,1)} %broadcast_in_dim.18), calls=%async_computation | async-start | bytes 524288 | tf_op jit(solution)/shard_map/all_to_all | solution.py:39
  27.1 14.5 %all-to-all-done = bf16[4,128,256]{2,1,0:T(8,128)(2,1)S(1)} async-done(((bf16[4,128,256]{2,1,0:T(8,128)(2,1)}), bf16[4,128,256]{2,1,0:T(8,128)(2,1)S(1)}, u32[]{:S(2)}, u32[]{:S(2)}) %all-to-all-start) | async-done | bytes 262176 | tf_op jit(solution)/shard_map/all_to_all | solution.py:39
  41.6 1.1 broadcast_in_dim.20
  42.7 4.5 %all-to-all-start.1 = ((bf16[4,512,256]{2,1,0:T(8,128)(2,1)}), bf16[4,512,256]{2,1,0:T(8,128)(2,1)S(1)}, u32[]{:S(2)}, u32[]{:S(2)}) async-start(bf16[4,512,256]{2,1,0:T(8,128)(2,1)} %broadcast_in_dim.20), calls=%async_computation.1 | async-start | bytes 2097152 | tf_op jit(solution)/shard_map/all_to_all | solution.py:39
  47.2 1.8 fusion.34
  49.0 1.5 collective-permute-start.3
  50.5 2.8 collective-permute-start.2
  53.3 1.4 collective-permute-start.1
  54.7 1.4 fusion.2
  56.0 13.1 %all-to-all-done.1 = bf16[4,512,256]{2,1,0:T(8,128)(2,1)S(1)} async-done(((bf16[4,512,256]{2,1,0:T(8,128)(2,1)}), bf16[4,512,256]{2,1,0:T(8,128)(2,1)S(1)}, u32[]{:S(2)}, u32[]{:S(2)}) %all-to-all-start.1) | async-done | bytes 1048608 | tf_op jit(solution)/shard_map/all_to_all | solution.py:39
  69.2 6.7 %collective-permute-done.2 = bf16[2,16,8192]{2,1,0:T(8,128)(2,1)} collective-permute-done((bf16[2,16,8192]{2,1,0:T(8,128)(2,1)S(1)}, bf16[2,16,8192]{2,1,0:T(8,128)(2,1)}, u32[]{:S(2)}, u32[]{:S(2)}) %collective-permute-start.2) | collective-permute-done | bytes 524320 | tf_op jit(solution)/shard_map/ppermute | solution.py:34
  75.8 1.8 pad_maximum_fusion
  78.0 1.2 shard_map.145
  79.6 14.9 %all_to_all.50 = bf16[4,128,256]{2,1,0:T(8,128)(2,1)S(1)} all-to-all(bf16[4,128,256]{2,1,0:T(8,128)(2,1)S(1)} %broadcast_in_dim.21), channel_id=1, replica_groups=mesh['y'=4,'z'=4,'c'=2,'h'=2,'x'=4] {'z'}, dimensions={0} | all-to-all | bytes 524288 | tf_op jit(solution)/shard_map/all_to_all | solution.py:39
  94.6 18.4 %all_to_all.51 = bf16[4,512,256]{2,1,0:T(8,128)(2,1)S(1)} all-to-all(bf16[4,512,256]{2,1,0:T(8,128)(2,1)S(1)} %broadcast_in_dim.23), channel_id=1, replica_groups=mesh['y'=4,'z'=4,'c'=2,'h'=2,'x'=4] {'y'}, dimensions={0} | all-to-all | bytes 2097152 | tf_op jit(solution)/shard_map/all_to_all | solution.py:39
  113.9 4.8 %all-to-all-start.4 = ((bf16[32,16,256]{2,1,0:T(8,128)(2,1)}), bf16[32,16,256]{2,1,0:T(8,128)(2,1)S(1)}, u32[]{:S(2)}, u32[]{:S(2)}) async-start(bf16[32,16,256]{2,1,0:T(8,128)(2,1)} %copy-done.4), calls=%async_computation.4 | async-start | bytes 524288 | tf_op jit(solution)/shard_map/all_to_all | solution.py:492
  118.8 5.1 %shard_map.144 = (bf16[512,128]{1,0:T(8,128)(2,1)S(1)}, bf16[512,128]{1,0:T(8,128)(2,1)S(1)}) custom-call(bf16[128,8192]{1,0:T(8,128)(2,1)S(1)} %bitcast.90, bf16[128,8192]{1,0:T(8,128)(2,1)S(1)} %bitcast.91, bf16[4096,1024]{1,0:T(8,128)(2,1)} %all-gather.3.cloned.1.call-done.weights, f32[128,128]{1,0:T(8,128)S(1)} %get-tuple-element.24.cosine, ...), custom_call_target="tpu_custom_call" | custom-call | tf_op jit(solution)/shard_map/pallas_call | solution.py:140
  124.0 12.9 %shard_map.146 = (bf16[128,1024]{1,0:T(8,128)(2,1)S(1)}, bf16[2048,256]{1,0:T(8,128)(2,1)S(1)}, bf16[2048,256]{1,0:T(8,128)(2,1)S(1)}) custom-call(s32[3]{0:T(128)S(1)} %pad_add_fusion.1.at_chx, bf16[512,128]{1,0:T(8,128)(2,1)S(1)} %get-tuple-element.26.query, bf16[512,128]{1,0:T(8,128)(2,1)S(1)} %get-tuple-element.27.grad_heads, ...), custom_call_target="tpu_custom_call" | custom-call | tf_op jit(solution)/shard_map/pallas_call | solution.py:244
  137.0 1.0 copy-done.8
  139.1 2.7 collective-permute-done.6
  141.9 1.3 add_convert_fusion
  143.2 0.9 collective-permute-start.7
  144.1 4.2 %all-to-all-start.5 = ((bf16[4,512,256]{2,1,0:T(8,128)(2,1)}), bf16[4,512,256]{2,1,0:T(8,128)(2,1)}, u32[]{:S(2)}, u32[]{:S(2)}) async-start(bf16[4,512,256]{2,1,0:T(8,128)(2,1)} %bitcast.20.waited), calls=%async_computation.5 | async-start | bytes 2097152 | tf_op jit(solution)/shard_map/all_to_all | solution.py:45
  148.4 16.8 %collective-permute-done.7 = bf16[32,16,256]{2,1,0:T(8,128)(2,1)S(1)} collective-permute-done((bf16[32,16,256]{2,1,0:T(8,128)(2,1)S(1)}, bf16[32,16,256]{2,1,0:T(8,128)(2,1)S(1)}, u32[]{:S(2)}, u32[]{:S(2)}) %collective-permute-start.7) | collective-permute-done | bytes 262176 | tf_op jit(solution)/shard_map/ppermute | solution.py:30
  165.3 6.0 %shard_map.149 = (bf16[128,4096]{1,0:T(8,128)(2,1)S(1)}, bf16[128,4096]{1,0:T(8,128)(2,1)S(1)}) custom-call(bf16[128,1024]{1,0:T(8,128)(2,1)S(1)} %get-tuple-element.29.att_gq.value, bf16[4096,1024]{1,0:T(8,128)(2,1)} %all-gather.3.cloned.1.call-done.weights, bf16[2,32,16,256]{3,2,1,0:T(8,128)(2,1)S(1)} %pad_maximum_fusion.3.waited.refs_0_), custom_call_target="tpu_custom_call" | custom-call | tf_op jit(solution)/shard_map/pallas_call | solution.py:267
  171.6 1.0 slice_bitcast_fusion.4
  172.6 2.8 %collective-permute-start.10 = (bf16[2,16,4096]{2,1,0:T(8,128)(2,1)}, bf16[2,16,4096]{2,1,0:T(8,128)(2,1)}, u32[]{:S(2)}, u32[]{:S(2)}) collective-permute-start(bf16[2,16,4096]{2,1,0:T(8,128)(2,1)} %get-tuple-element.46), channel_id=1, source_target_pairs={{1,0},{2,1},{3,2},{0,3},{5,4},{6,5},{7,6},{4,7},{9,8},{10,9},{11,1... | collective-permute-start | bytes 786440 | tf_op jit(solution)/shard_map/ppermute | solution.py:34
  176.3 3.0 %collective-permute-start.15 = (bf16[2,32,16,256]{3,2,1,0:T(8,128)(2,1)S(1)}, bf16[2,32,16,256]{3,2,1,0:T(8,128)(2,1)S(1)}, u32[]{:S(2)}, u32[]{:S(2)}) collective-permute-start(bf16[2,32,16,256]{3,2,1,0:T(8,128)(2,1)S(1)} %pad_maximum_fusion.3.waited.refs_0_), channel_id=1, source_target_pairs={{1,0},{2,1},{3,2},{0,3},{5,4},{6,5},{7,6},{4,7},{9,8},{10,9},{11,1... | collective-permute-start | bytes 1572872 | tf_op jit(solution)/shard_map/ppermute | solution.py:34
  179.4 1.6 collective-permute-start.16
  181.0 2.1 reduce_sum.50
  183.1 5.6 %all-to-all-start.6 = ((bf16[4,128,256]{2,1,0:T(8,128)(2,1)}), bf16[4,128,256]{2,1,0:T(8,128)(2,1)S(1)}, u32[]{:S(2)}, u32[]{:S(2)}) async-start(bf16[4,128,256]{2,1,0:T(8,128)(2,1)} %bitcast.30), calls=%async_computation.6 | async-start | bytes 524288 | tf_op jit(solution)/shard_map/all_to_all | solution.py:45
  188.8 3.2 %collective-permute-done.8 = bf16[2,16,4096]{2,1,0:T(8,128)(2,1)} collective-permute-done((bf16[2,16,4096]{2,1,0:T(8,128)(2,1)}, bf16[2,16,4096]{2,1,0:T(8,128)(2,1)}, u32[]{:S(2)}, u32[]{:S(2)}) %collective-permute-start.8) | collective-permute-done | bytes 262176 | tf_op jit(solution)/shard_map/ppermute | solution.py:34
  192.0 2.1 fusion.6
  194.1 6.2 %all-to-all-done.6 = bf16[4,128,256]{2,1,0:T(8,128)(2,1)S(1)} async-done(((bf16[4,128,256]{2,1,0:T(8,128)(2,1)}), bf16[4,128,256]{2,1,0:T(8,128)(2,1)S(1)}, u32[]{:S(2)}, u32[]{:S(2)}) %all-to-all-start.6) | async-done | bytes 262176 | tf_op jit(solution)/shard_map/all_to_all | solution.py:45
  200.6 1.2 copy-done.6
  201.8 3.0 %shard_map.150 = (bf16[128,4096]{1,0:T(8,128)(2,1)S(1)}, f32[1,4096]{1,0:T(1,128)S(1)}) custom-call(bf16[128,4096]{1,0:T(8,128)(2,1)S(1)} %copy-done.6, bf16[128,256]{1,0:T(8,128)(2,1)S(1)} %pad_maximum_fusion.10.grad_kv, bf16[4096,256]{1,0:T(8,128)(2,1)S(1)} %bitcast.94, bf16[128,8192]{1,0:T(8,128)(2,1)} %bitcast.92), custom_call_target="tpu_custom_call" | custom-call | tf_op jit(solution)/shard_map/pallas_call | solution.py:295
  204.9 0.9 copy-done.3
  206.6 3.4 %all-to-all-start.7 = ((bf16[4,144,256]{2,1,0:T(8,128)(2,1)}), bf16[4,144,256]{2,1,0:T(8,128)(2,1)S(1)}, u32[]{:S(2)}, u32[]{:S(2)}) async-start(bf16[4,144,256]{2,1,0:T(8,128)(2,1)} %broadcast_in_dim.24), calls=%async_computation.7 | async-start | bytes 589824 | tf_op jit(solution)/shard_map/all_to_all | solution.py:39
  210.1 2.2 fusion.35
  212.9 1.3 collective-permute-start.13
  214.3 1.4 collective-permute-start.12
  215.7 2.8 all-to-all-done.7
  218.5 1.1 broadcast_in_dim.25
  219.6 3.5 %all-to-all-start.8 = ((bf16[4,4,144,256]{3,2,1,0:T(8,128)(2,1)}), bf16[4,4,144,256]{3,2,1,0:T(8,128)(2,1)S(1)}, u32[]{:S(2)}, u32[]{:S(2)}) async-start(bf16[4,4,144,256]{3,2,1,0:T(8,128)(2,1)} %broadcast_in_dim.25), calls=%async_computation.8 | async-start | bytes 2359296 | tf_op jit(solution)/shard_map/all_to_all | solution.py:39
  223.2 1.6 fusion.21
  224.8 1.1 collective-permute-start.17
  225.9 2.6 collective-permute-start.11
  228.5 9.3 %all-to-all-done.8 = bf16[4,4,144,256]{3,2,1,0:T(8,128)(2,1)S(1)} async-done(((bf16[4,4,144,256]{3,2,1,0:T(8,128)(2,1)}), bf16[4,4,144,256]{3,2,1,0:T(8,128)(2,1)S(1)}, u32[]{:S(2)}, u32[]{:S(2)}) %all-to-all-start.8) | async-done | bytes 1179680 | tf_op jit(solution)/shard_map/all_to_all | solution.py:39
  237.8 1.3 fusion.4
  239.2 1.4 collective-permute-done.18.refs_5_
  240.6 3.0 %shard_map.151.waited = bf16[144,256]{1,0:T(8,128)(2,1)S(1)} custom-call(s32[1]{0:T(128)} %bitcast.core, bf16[2,32,16,256]{3,2,1,0:T(8,128)(2,1)S(1)} %pad_maximum_fusion.3.waited.refs_0_, bf16[2,32,16,256]{3,2,1,0:T(8,128)(2,1)S(1)} %collective-permute-done.15.refs_1_, bf16[2,32,16,256]{3,2,1,0:T(8,128)(2,1)} %collective-permute-done.16.refs_2_, ...), custom_call_target="tpu_custom_call" | custom-call | tf_op jit(solution)/shard_map/pallas_call | solution.py:377
  243.6 3.6 %collective-permute-start.19 = (bf16[16,4096]{1,0:T(8,128)(2,1)S(1)}, bf16[16,4096]{1,0:T(8,128)(2,1)S(1)}, u32[]{:S(2)}, u32[]{:S(2)}) collective-permute-start(bf16[16,4096]{1,0:T(8,128)(2,1)S(1)} %shard_map.152), channel_id=1, source_target_pairs={{0,4},{4,0},{1,5},{5,1},{2,6},{6,2},{3,7},{7,3},{8,12},{12,8},{9,1... | collective-permute-start | bytes 393224 | tf_op jit(solution)/shard_map/ppermute | solution.py:30
  247.9 3.6 %all-to-all-start.9 = ((bf16[4,144,256]{2,1,0:T(8,128)(2,1)}), bf16[4,144,256]{2,1,0:T(8,128)(2,1)S(1)}, u32[]{:S(2)}, u32[]{:S(2)}) async-start(bf16[4,144,256]{2,1,0:T(8,128)(2,1)} %broadcast_in_dim.26), calls=%async_computation.9 | async-start | bytes 589824 | tf_op jit(solution)/shard_map/all_to_all | solution.py:39
  251.5 4.5 %collective-permute-done.19 = bf16[16,4096]{1,0:T(8,128)(2,1)S(1)} collective-permute-done((bf16[16,4096]{1,0:T(8,128)(2,1)S(1)}, bf16[16,4096]{1,0:T(8,128)(2,1)S(1)}, u32[]{:S(2)}, u32[]{:S(2)}) %collective-permute-start.19) | collective-permute-done | bytes 131104 | tf_op jit(solution)/shard_map/ppermute | solution.py:30
  256.0 0.8 fusion.11
  256.9 5.9 %shard_map.154 = (f32[128,512]{1,0:T(8,128)}, f32[128,512]{1,0:T(8,128)}) custom-call(bf16[2,32,16,256]{3,2,1,0:T(8,128)(2,1)S(1)} %pad_maximum_fusion.3.waited.refs_0_, bf16[2,32,16,256]{3,2,1,0:T(8,128)(2,1)S(1)} %collective-permute-done.15.refs_1_, bf16[2,32,16,256]{3,2,1,0:T(8,128)(2,1)} %collective-permute-done.16.refs_2_, ...), custom_call_target="tpu_custom_call" | custom-call | tf_op jit(solution)/shard_map/pallas_call | solution.py:336
  262.8 0.9 copy-done.7
  263.8 2.7 collective-permute-start.20
  267.3 7.0 %collective-permute-done.20 = bf16[2,144,256]{2,1,0:T(8,128)(2,1)S(1)} collective-permute-done((bf16[2,144,256]{2,1,0:T(8,128)(2,1)S(1)}, bf16[2,144,256]{2,1,0:T(8,128)(2,1)S(1)}, u32[]{:S(2)}, u32[]{:S(2)}) %collective-permute-start.20) | collective-permute-done | bytes 147488 | tf_op jit(solution)/shard_map/ppermute | solution.py:30
  (144 shorter events, 13.5 us)
Async XLA Ops:
  7.2 17.8 %copy-start.16 = (bf16[1,128,4096]{2,1,0:T(8,128)(2,1)S(1)}, bf16[1,128,4096]{2,1,0:T(8,128)(2,1)}, u32[]{:S(2)}) copy-start(bf16[1,128,4096]{2,1,0:T(8,128)(2,1)} %param.10) | copy-start | bytes 3145732
  7.2 111.7 %all-gather.3.cloned.1.call-start = ((), (), s32[]{:S(2)}) async-start(), calls=%async_computation.10 | async-start | bytes 8650752 | tf_op jit(solution)/shard_map/all_gather | solution.py:438
  10.1 102.9 %copy-start.22 = (f32[16]{0:T(128)}, f32[16]{0:T(128)S(1)}, u32[]{:S(2)}) copy-start(f32[16]{0:T(128)S(1)} %add_rsqrt_fusion) | copy-start | bytes 196
  11.1 14.0 %copy-start.21 = (s32[4096]{0:T(1024)S(1)}, s32[4096]{0:T(1024)}, u32[]{:S(2)}) copy-start(s32[4096]{0:T(1024)} %param.17) | copy-start | bytes 49156
  12.8 34.4 %collective-permute-start = (bf16[16,8192]{1,0:T(8,128)(2,1)}, bf16[16,8192]{1,0:T(8,128)(2,1)}, u32[]{:S(2)}, u32[]{:S(2)}) collective-permute-start(bf16[16,8192]{1,0:T(8,128)(2,1)} %get-tuple-element.53), channel_id=1, source_target_pairs={{0,4},{4,0},{1,5},{5,1},{2,6},{6,2},{3,7},{7,3},{8,12},{12,8},{9,1... | collective-permute-start | bytes 786440 | tf_op jit(solution)/shard_map/ppermute | solution.py:30
  20.6 21.0 %all-to-all-start = ((bf16[4,128,256]{2,1,0:T(8,128)(2,1)}), bf16[4,128,256]{2,1,0:T(8,128)(2,1)S(1)}, u32[]{:S(2)}, u32[]{:S(2)}) async-start(bf16[4,128,256]{2,1,0:T(8,128)(2,1)} %broadcast_in_dim.18), calls=%async_computation | async-start | bytes 524288 | tf_op jit(solution)/shard_map/all_to_all | solution.py:39
  42.7 26.4 %all-to-all-start.1 = ((bf16[4,512,256]{2,1,0:T(8,128)(2,1)}), bf16[4,512,256]{2,1,0:T(8,128)(2,1)S(1)}, u32[]{:S(2)}, u32[]{:S(2)}) async-start(bf16[4,512,256]{2,1,0:T(8,128)(2,1)} %broadcast_in_dim.20), calls=%async_computation.1 | async-start | bytes 2097152 | tf_op jit(solution)/shard_map/all_to_all | solution.py:39
  49.0 20.2 %collective-permute-start.3 = (bf16[2,16,8192]{2,1,0:T(8,128)(2,1)S(1)}, bf16[2,16,8192]{2,1,0:T(8,128)(2,1)}, u32[]{:S(2)}, u32[]{:S(2)}) collective-permute-start(bf16[2,16,8192]{2,1,0:T(8,128)(2,1)S(1)} %get-tuple-element.49), channel_id=1, source_target_pairs={{3,0},{0,1},{1,2},{2,3},{7,4},{4,5},{5,6},{6,7},{11,8},{8,9},{9,10... | collective-permute-start | bytes 1572872 | tf_op jit(solution)/shard_map/ppermute | solution.py:34
  50.5 25.3 %collective-permute-start.2 = (bf16[2,16,8192]{2,1,0:T(8,128)(2,1)S(1)}, bf16[2,16,8192]{2,1,0:T(8,128)(2,1)}, u32[]{:S(2)}, u32[]{:S(2)}) collective-permute-start(bf16[2,16,8192]{2,1,0:T(8,128)(2,1)S(1)} %get-tuple-element.49), channel_id=1, source_target_pairs={{2,0},{3,1},{0,2},{1,3},{6,4},{7,5},{4,6},{5,7},{10,8},{11,9},{8,1... | collective-permute-start | bytes 1572872 | tf_op jit(solution)/shard_map/ppermute | solution.py:34
  53.3 22.6 %collective-permute-start.1 = (bf16[2,16,8192]{2,1,0:T(8,128)(2,1)S(1)}, bf16[2,16,8192]{2,1,0:T(8,128)(2,1)}, u32[]{:S(2)}, u32[]{:S(2)}) collective-permute-start(bf16[2,16,8192]{2,1,0:T(8,128)(2,1)S(1)} %get-tuple-element.49), channel_id=1, source_target_pairs={{1,0},{2,1},{3,2},{0,3},{5,4},{6,5},{7,6},{4,7},{9,8},{10,9},{11,1... | collective-permute-start | bytes 1572872 | tf_op jit(solution)/shard_map/ppermute | solution.py:34
  69.1 8.5 %collective-permute-start.4 = (bf16[16,1,128,256]{3,2,1,0:T(8,128)(2,1)S(1)}, bf16[16,1,128,256]{3,2,1,0:T(8,128)(2,1)S(1)}, u32[]{:S(2)}, u32[]{:S(2)}) collective-permute-start(bf16[16,1,128,256]{3,2,1,0:T(8,128)(2,1)S(1)} %bitcast.102), channel_id=1, source_target_pairs={{0,8},{8,0},{1,9},{9,1},{2,10},{10,2},{3,11},{11,3},{4,12},{12,4},... | collective-permute-start | bytes 3145736 | tf_op jit(solution)/shard_map/ppermute | solution.py:30
  77.6 41.2 %copy-start = (bf16[4,2,16,8192]{3,2,1,0:T(8,128)(2,1)}, bf16[4,2,16,8192]{3,2,1,0:T(8,128)(2,1)S(1)}, u32[]{:S(2)}) copy-start(bf16[4,2,16,8192]{3,2,1,0:T(8,128)(2,1)S(1)} %pad_maximum_fusion) | copy-start | bytes 6291460
  78.0 1.6 copy-start.1
  79.6 33.4 %copy-start.11 = (bf16[16,4096]{1,0:T(8,128)(2,1)S(1)}, bf16[16,4096]{1,0:T(8,128)(2,1)}, u32[]{:S(2)}) copy-start(bf16[16,4096]{1,0:T(8,128)(2,1)} %param.9) | copy-start | bytes 393220
  79.6 33.4 %copy-start.14 = (bf16[16,4096]{1,0:T(8,128)(2,1)S(1)}, bf16[16,4096]{1,0:T(8,128)(2,1)}, u32[]{:S(2)}) copy-start(bf16[16,4096]{1,0:T(8,128)(2,1)} %param.16) | copy-start | bytes 393220
  79.6 33.4 %copy-start.17 = (f32[4096]{0:T(1024)S(1)}, f32[4096]{0:T(1024)}, u32[]{:S(2)}) copy-start(f32[4096]{0:T(1024)} %param.11) | copy-start | bytes 49156
  113.0 11.0 %collective-permute-start.5 = (bf16[2048,256]{1,0:T(8,128)(2,1)S(1)}, bf16[2048,256]{1,0:T(8,128)(2,1)}, u32[]{:S(2)}, u32[]{:S(2)}) collective-permute-start(bf16[2048,256]{1,0:T(8,128)(2,1)S(1)} %bitcast.95), channel_id=1, source_target_pairs={{0,8},{8,0},{1,9},{9,1},{2,10},{10,2},{3,11},{11,3},{4,12},{12,4},... | collective-permute-start | bytes 3145736 | tf_op jit(solution)/shard_map/ppermute | solution.py:30
  113.2 0.7 copy-start.4
  113.9 24.1 %all-to-all-start.4 = ((bf16[32,16,256]{2,1,0:T(8,128)(2,1)}), bf16[32,16,256]{2,1,0:T(8,128)(2,1)S(1)}, u32[]{:S(2)}, u32[]{:S(2)}) async-start(bf16[32,16,256]{2,1,0:T(8,128)(2,1)} %copy-done.4), calls=%async_computation.4 | async-start | bytes 524288 | tf_op jit(solution)/shard_map/all_to_all | solution.py:492
  118.7 138.2 %all-gather.5.cloned.1.call-start = ((), (), s32[]{:S(2)}) async-start(), calls=%async_computation.11 | async-start | bytes 8650752 | tf_op jit(solution)/shard_map/all_gather | solution.py:497
  137.0 1.0 copy-start.8
  138.7 3.1 %collective-permute-start.6 = (bf16[2048,256]{1,0:T(8,128)(2,1)}, bf16[2048,256]{1,0:T(8,128)(2,1)S(1)}, u32[]{:S(2)}, u32[]{:S(2)}) collective-permute-start(bf16[2048,256]{1,0:T(8,128)(2,1)} %copy-done.8), channel_id=1, source_target_pairs={{0,8},{8,0},{1,9},{9,1},{2,10},{10,2},{3,11},{11,3},{4,12},{12,4},... | collective-permute-start | bytes 3145736 | tf_op jit(solution)/shard_map/ppermute | solution.py:30
  143.2 22.0 %collective-permute-start.7 = (bf16[32,16,256]{2,1,0:T(8,128)(2,1)S(1)}, bf16[32,16,256]{2,1,0:T(8,128)(2,1)S(1)}, u32[]{:S(2)}, u32[]{:S(2)}) collective-permute-start(bf16[32,16,256]{2,1,0:T(8,128)(2,1)S(1)} %shard_map.148), channel_id=1, source_target_pairs={{0,4},{4,0},{1,5},{5,1},{2,6},{6,2},{3,7},{7,3},{8,12},{12,8},{9,1... | collective-permute-start | bytes 786440 | tf_op jit(solution)/shard_map/ppermute | solution.py:30
  144.1 36.9 %all-to-all-start.5 = ((bf16[4,512,256]{2,1,0:T(8,128)(2,1)}), bf16[4,512,256]{2,1,0:T(8,128)(2,1)}, u32[]{:S(2)}, u32[]{:S(2)}) async-start(bf16[4,512,256]{2,1,0:T(8,128)(2,1)} %bitcast.20.waited), calls=%async_computation.5 | async-start | bytes 2097152 | tf_op jit(solution)/shard_map/all_to_all | solution.py:45
  165.3 6.1 %copy-start.9 = (bf16[4,2,16,4096]{3,2,1,0:T(8,128)(2,1)S(1)}, bf16[4,2,16,4096]{3,2,1,0:T(8,128)(2,1)}, u32[]{:S(2)}) copy-start(bf16[4,2,16,4096]{3,2,1,0:T(8,128)(2,1)} %fusion.2) | copy-start | bytes 3145732
  171.3 1.3 copy-start.5
  171.6 4.7 %copy-start.10 = (bf16[4,2,16,4096]{3,2,1,0:T(8,128)(2,1)}, bf16[4,2,16,4096]{3,2,1,0:T(8,128)(2,1)S(1)}, u32[]{:S(2)}) copy-start(bf16[4,2,16,4096]{3,2,1,0:T(8,128)(2,1)S(1)} %fusion) | copy-start | bytes 3145732
  172.6 16.2 %collective-permute-start.10 = (bf16[2,16,4096]{2,1,0:T(8,128)(2,1)}, bf16[2,16,4096]{2,1,0:T(8,128)(2,1)}, u32[]{:S(2)}, u32[]{:S(2)}) collective-permute-start(bf16[2,16,4096]{2,1,0:T(8,128)(2,1)} %get-tuple-element.46), channel_id=1, source_target_pairs={{1,0},{2,1},{3,2},{0,3},{5,4},{6,5},{7,6},{4,7},{9,8},{10,9},{11,1... | collective-permute-start | bytes 786440 | tf_op jit(solution)/shard_map/ppermute | solution.py:34
  175.4 13.3 %collective-permute-start.9 = (bf16[2,16,4096]{2,1,0:T(8,128)(2,1)}, bf16[2,16,4096]{2,1,0:T(8,128)(2,1)}, u32[]{:S(2)}, u32[]{:S(2)}) collective-permute-start(bf16[2,16,4096]{2,1,0:T(8,128)(2,1)} %get-tuple-element.47), channel_id=1, source_target_pairs={{2,0},{3,1},{0,2},{1,3},{6,4},{7,5},{4,6},{5,7},{10,8},{11,9},{8,1... | collective-permute-start | bytes 786440 | tf_op jit(solution)/shard_map/ppermute | solution.py:34
  176.1 24.4 %copy-start.2 = (bf16[16,2,128,256]{3,2,1,0:T(8,128)(2,1)S(1)}, bf16[16,2,128,256]{3,2,1,0:T(8,128)(2,1)}, u32[]{:S(2)}) copy-start(bf16[16,2,128,256]{3,2,1,0:T(8,128)(2,1)} %copy-done.1) | copy-start | bytes 6291460
  176.1 15.9 %collective-permute-start.8 = (bf16[2,16,4096]{2,1,0:T(8,128)(2,1)}, bf16[2,16,4096]{2,1,0:T(8,128)(2,1)}, u32[]{:S(2)}, u32[]{:S(2)}) collective-permute-start(bf16[2,16,4096]{2,1,0:T(8,128)(2,1)} %get-tuple-element.45), channel_id=1, source_target_pairs={{3,0},{0,1},{1,2},{2,3},{7,4},{4,5},{5,6},{6,7},{11,8},{8,9},{9,10... | collective-permute-start | bytes 786440 | tf_op jit(solution)/shard_map/ppermute | solution.py:34
  176.3 62.9 %collective-permute-start.15 = (bf16[2,32,16,256]{3,2,1,0:T(8,128)(2,1)S(1)}, bf16[2,32,16,256]{3,2,1,0:T(8,128)(2,1)S(1)}, u32[]{:S(2)}, u32[]{:S(2)}) collective-permute-start(bf16[2,32,16,256]{3,2,1,0:T(8,128)(2,1)S(1)} %pad_maximum_fusion.3.waited.refs_0_), channel_id=1, source_target_pairs={{1,0},{2,1},{3,2},{0,3},{5,4},{6,5},{7,6},{4,7},{9,8},{10,9},{11,1... | collective-permute-start | bytes 1572872 | tf_op jit(solution)/shard_map/ppermute | solution.py:34
  179.4 59.8 %collective-permute-start.16 = (bf16[2,32,16,256]{3,2,1,0:T(8,128)(2,1)S(1)}, bf16[2,32,16,256]{3,2,1,0:T(8,128)(2,1)}, u32[]{:S(2)}, u32[]{:S(2)}) collective-permute-start(bf16[2,32,16,256]{3,2,1,0:T(8,128)(2,1)S(1)} %pad_maximum_fusion.3.waited.refs_0_), channel_id=1, source_target_pairs={{2,0},{3,1},{0,2},{1,3},{6,4},{7,5},{4,6},{5,7},{10,8},{11,9},{8,1... | collective-permute-start | bytes 1572872 | tf_op jit(solution)/shard_map/ppermute | solution.py:34
  183.1 17.2 %all-to-all-start.6 = ((bf16[4,128,256]{2,1,0:T(8,128)(2,1)}), bf16[4,128,256]{2,1,0:T(8,128)(2,1)S(1)}, u32[]{:S(2)}, u32[]{:S(2)}) async-start(bf16[4,128,256]{2,1,0:T(8,128)(2,1)} %bitcast.30), calls=%async_computation.6 | async-start | bytes 524288 | tf_op jit(solution)/shard_map/all_to_all | solution.py:45
  200.6 1.2 copy-start.6
  204.8 1.0 copy-start.3
  206.6 11.9 %all-to-all-start.7 = ((bf16[4,144,256]{2,1,0:T(8,128)(2,1)}), bf16[4,144,256]{2,1,0:T(8,128)(2,1)S(1)}, u32[]{:S(2)}, u32[]{:S(2)}) async-start(bf16[4,144,256]{2,1,0:T(8,128)(2,1)} %broadcast_in_dim.24), calls=%async_computation.7 | async-start | bytes 589824 | tf_op jit(solution)/shard_map/all_to_all | solution.py:39
  212.3 12.5 %collective-permute-start.14 = (bf16[2,16,4096]{2,1,0:T(8,128)(2,1)}, bf16[2,16,4096]{2,1,0:T(8,128)(2,1)}, u32[]{:S(2)}, u32[]{:S(2)}) collective-permute-start(bf16[2,16,4096]{2,1,0:T(8,128)(2,1)} %bitcast.34), channel_id=1, source_target_pairs={{1,0},{2,1},{3,2},{0,3},{5,4},{6,5},{7,6},{4,7},{9,8},{10,9},{11,1... | collective-permute-start | bytes 786440 | tf_op jit(solution)/shard_map/ppermute | solution.py:34
  212.9 13.0 %collective-permute-start.13 = (bf16[2,16,4096]{2,1,0:T(8,128)(2,1)}, bf16[2,16,4096]{2,1,0:T(8,128)(2,1)S(1)}, u32[]{:S(2)}, u32[]{:S(2)}) collective-permute-start(bf16[2,16,4096]{2,1,0:T(8,128)(2,1)} %bitcast.33), channel_id=1, source_target_pairs={{2,0},{3,1},{0,2},{1,3},{6,4},{7,5},{4,6},{5,7},{10,8},{11,9},{8,1... | collective-permute-start | bytes 786440 | tf_op jit(solution)/shard_map/ppermute | solution.py:34
  214.3 14.2 %collective-permute-start.12 = (bf16[2,16,4096]{2,1,0:T(8,128)(2,1)}, bf16[2,16,4096]{2,1,0:T(8,128)(2,1)S(1)}, u32[]{:S(2)}, u32[]{:S(2)}) collective-permute-start(bf16[2,16,4096]{2,1,0:T(8,128)(2,1)} %bitcast.32), channel_id=1, source_target_pairs={{3,0},{0,1},{1,2},{2,3},{7,4},{4,5},{5,6},{6,7},{11,8},{8,9},{9,10... | collective-permute-start | bytes 786440 | tf_op jit(solution)/shard_map/ppermute | solution.py:34
  219.6 18.2 %all-to-all-start.8 = ((bf16[4,4,144,256]{3,2,1,0:T(8,128)(2,1)}), bf16[4,4,144,256]{3,2,1,0:T(8,128)(2,1)S(1)}, u32[]{:S(2)}, u32[]{:S(2)}) async-start(bf16[4,4,144,256]{3,2,1,0:T(8,128)(2,1)} %broadcast_in_dim.25), calls=%async_computation.8 | async-start | bytes 2359296 | tf_op jit(solution)/shard_map/all_to_all | solution.py:39
  224.8 14.4 %collective-permute-start.17 = (bf16[2,32,16,256]{3,2,1,0:T(8,128)(2,1)S(1)}, bf16[2,32,16,256]{3,2,1,0:T(8,128)(2,1)S(1)}, u32[]{:S(2)}, u32[]{:S(2)}) collective-permute-start(bf16[2,32,16,256]{3,2,1,0:T(8,128)(2,1)S(1)} %pad_maximum_fusion.3.waited.refs_0_), channel_id=1, source_target_pairs={{3,0},{0,1},{1,2},{2,3},{7,4},{4,5},{5,6},{6,7},{11,8},{8,9},{9,10... | collective-permute-start | bytes 1572872 | tf_op jit(solution)/shard_map/ppermute | solution.py:34
  225.9 11.9 %copy-start.19 = (bf16[2,16,4096]{2,1,0:T(8,128)(2,1)}, bf16[2,16,4096]{2,1,0:T(8,128)(2,1)S(1)}, u32[]{:S(2)}) copy-start(bf16[2,16,4096]{2,1,0:T(8,128)(2,1)S(1)} %collective-permute-done.13) | copy-start | bytes 786436
  225.9 13.2 %collective-permute-start.11 = (bf16[16,4096]{1,0:T(8,128)(2,1)}, bf16[16,4096]{1,0:T(8,128)(2,1)S(1)}, u32[]{:S(2)}, u32[]{:S(2)}) collective-permute-start(bf16[16,4096]{1,0:T(8,128)(2,1)} %fusion.21), channel_id=1, source_target_pairs={{0,4},{4,0},{1,5},{5,1},{2,6},{6,2},{3,7},{7,3},{8,12},{12,8},{9,1... | collective-permute-start | bytes 393224 | tf_op jit(solution)/shard_map/ppermute | solution.py:30
  228.5 9.3 %copy-start.20 = (bf16[2,16,4096]{2,1,0:T(8,128)(2,1)}, bf16[2,16,4096]{2,1,0:T(8,128)(2,1)S(1)}, u32[]{:S(2)}) copy-start(bf16[2,16,4096]{2,1,0:T(8,128)(2,1)S(1)} %collective-permute-done.12) | copy-start | bytes 786436
  237.8 2.8 %collective-permute-start.18 = (bf16[16,144,256]{2,1,0:T(8,128)(2,1)S(1)}, bf16[16,144,256]{2,1,0:T(8,128)(2,1)S(1)}, u32[]{:S(2)}, u32[]{:S(2)}) collective-permute-start(bf16[16,144,256]{2,1,0:T(8,128)(2,1)S(1)} %bitcast.98), channel_id=1, source_target_pairs={{0,8},{8,0},{1,9},{9,1},{2,10},{10,2},{3,11},{11,3},{4,12},{12,4},... | collective-permute-start | bytes 3538952 | tf_op jit(solution)/shard_map/ppermute | solution.py:30
  239.1 16.8 %copy-start.12 = (bf16[16,4096]{1,0:T(8,128)(2,1)S(1)}, bf16[16,4096]{1,0:T(8,128)(2,1)}, u32[]{:S(2)}) copy-start(bf16[16,4096]{1,0:T(8,128)(2,1)} %param.9) | copy-start | bytes 393220
  239.2 16.8 %copy-start.18 = (f32[4096]{0:T(1024)S(1)}, f32[4096]{0:T(1024)}, u32[]{:S(2)}) copy-start(f32[4096]{0:T(1024)} %param.11) | copy-start | bytes 49156
  243.6 12.3 %collective-permute-start.19 = (bf16[16,4096]{1,0:T(8,128)(2,1)S(1)}, bf16[16,4096]{1,0:T(8,128)(2,1)S(1)}, u32[]{:S(2)}, u32[]{:S(2)}) collective-permute-start(bf16[16,4096]{1,0:T(8,128)(2,1)S(1)} %shard_map.152), channel_id=1, source_target_pairs={{0,4},{4,0},{1,5},{5,1},{2,6},{6,2},{3,7},{7,3},{8,12},{12,8},{9,1... | collective-permute-start | bytes 393224 | tf_op jit(solution)/shard_map/ppermute | solution.py:30
  247.9 14.9 %all-to-all-start.9 = ((bf16[4,144,256]{2,1,0:T(8,128)(2,1)}), bf16[4,144,256]{2,1,0:T(8,128)(2,1)S(1)}, u32[]{:S(2)}, u32[]{:S(2)}) async-start(bf16[4,144,256]{2,1,0:T(8,128)(2,1)} %broadcast_in_dim.26), calls=%async_computation.9 | async-start | bytes 589824 | tf_op jit(solution)/shard_map/all_to_all | solution.py:39
  256.8 9.6 %copy-start.13 = (f32[2,16,4096]{2,1,0:T(8,128)S(1)}, f32[2,16,4096]{2,1,0:T(8,128)}, u32[]{:S(2)}) copy-start(f32[2,16,4096]{2,1,0:T(8,128)} %fusion.6) | copy-start | bytes 1572868
  256.8 9.6 %copy-start.15 = (bf16[16,4096]{1,0:T(8,128)(2,1)S(1)}, bf16[16,4096]{1,0:T(8,128)(2,1)}, u32[]{:S(2)}) copy-start(bf16[16,4096]{1,0:T(8,128)(2,1)} %param.16) | copy-start | bytes 393220
  256.9 9.6 %copy-start.23 = (f32[16]{0:T(128)S(1)}, f32[16]{0:T(128)}, u32[]{:S(2)}) copy-start(f32[16]{0:T(128)} %copy-done.22) | copy-start | bytes 196
  262.8 1.0 copy-start.7
  263.8 10.5 %collective-permute-start.20 = (bf16[2,144,256]{2,1,0:T(8,128)(2,1)S(1)}, bf16[2,144,256]{2,1,0:T(8,128)(2,1)S(1)}, u32[]{:S(2)}, u32[]{:S(2)}) collective-permute-start(bf16[2,144,256]{2,1,0:T(8,128)(2,1)S(1)} %shard_map.155), channel_id=1, source_target_pairs={{0,4},{4,0},{1,5},{5,1},{2,6},{6,2},{3,7},{7,3},{8,12},{12,8},{9,1... | collective-permute-start | bytes 442376 | tf_op jit(solution)/shard_map/ppermute | solution.py:30
Sparse Core Ops, SparseCore 0:
  10.4 92.2 all-gather.2
  138.8 83.2 all-gather.4

commit v5 on v4

--- a/solution.py
+++ b/solution.py
@@ -195,7 +195,7 @@
             score[pl.ds(base + at, step), :] = s
             return jnp.maximum(peak, jnp.max(s, axis=0, keepdims=True))
 
-        peak = lax.fori_loop(0, half // step, mark, peak)
+        peak = lax.fori_loop(0, half // step, mark, peak, unroll=True)
 
     carry = (jnp.zeros((1, rows), wide), jnp.zeros((HEAD_DIM, rows), wide))
     for kv, base in ((near, 0), (far, half)):
@@ -208,7 +208,7 @@
             out = out + dot(kv[pl.ds(at, step), HEAD_DIM:], e.astype(low), ((0,), (0,)))
             return norm + jnp.sum(e, axis=0, keepdims=True), out
 
-        carry = lax.fori_loop(0, half // step, weigh, carry)
+        carry = lax.fori_loop(0, half // step, weigh, carry, unroll=True)
     norm, out = carry
     inverse = 1.0 / norm
     out = (out * inverse).astype(low).astype(wide)
@@ -226,7 +226,7 @@
             grad[pl.ds(at, step), HEAD_DIM:] = dot(p.astype(low), g, ((1,), (0,))).astype(low)
             return grad_query + dot(kv[pl.ds(at, step), :HEAD_DIM], gs, ((0,), (0,)))
 
-        grad_query = lax.fori_loop(0, half // step, back, grad_query)
+        grad_query = lax.fori_loop(0, half // step, back, grad_query, unroll=True)
 
     for i in range(heads):
         at, cols = slice(i * tok, (i + 1) * tok), slice(i * HEAD_DIM, (i + 1) * HEAD_DIM)
@@ -356,11 +356,14 @@
         gains[...] = jnp.zeros_like(gains)
 
     c = core[0]
-    for i in range(near.shape[0]):
-        for at, (grad, of) in enumerate(((near, c), (far, 1 - c))):
-            own = positions(rows, 2 * i + of)[:, block:]
-            total[...] += dot(own, grad[i, :tok], ((0,), (0,)))
+    own, grads = [], []
+    for at, (grad, of) in enumerate(((near, c), (far, 1 - c))):
+        for i in range(near.shape[0]):
+            own.append(positions(rows, 2 * i + of)[:, block:])
+            grads.append(grad[i, :tok])
             gains[at] += grad[i, tok:].astype(wide)
+    own, grads = jnp.concatenate(own, axis=0), jnp.concatenate(grads, axis=0)
+    total[...] += dot(own, grads, ((0,), (0,)))
 
     @pl.when(step == pl.num_programs(0) - 1)
     def _():

time: 285 us -> 281 us (0.986)
  Pallas kernels: 38.1 us -> 34.2 us
    pallas_call x1, Pallas kernels: 12.9 us -> 9.17 us  [attend(): pl.pallas_call(attend_kernel, in_specs=[pl.BlockSpec(memory_space=pltpu.S...]
  transfers between devices with their start and end apart: 31 -> 31, of which waited for: 12 -> 12; matrix products, arithmetic and copies ran while one was open for 11% -> 11% of each run, Pallas kernels for 13% -> 12%
where the time goes in v5:
time: 281 us; the launch traced here: 280 us
  waiting for transfers between devices  88.8 us (32%)
  starting transfers between devices  69 us (25%)
  Pallas kernels  34.2 us (12%)
  blocking collectives  33.3 us (12%)
  other arithmetic  23.3 us (8%)
  local copies, waits for them, and re-layouts  16.5 us (6%)
  between operations  14.7 us (5%)
    all_to_all x5, waiting for transfers between devices, spread(): lax.all_to_all(jnp.broadcast_to(a[None], (size,) + a.shape), axis, 0, 0,...  40.2 us
    all_to_all x2, blocking collectives, spread(): lax.all_to_all(jnp.broadcast_to(a[None], (size,) + a.shape), axis, 0, 0,...  33.3 us
    ppermute x9, waiting for transfers between devices, swap(): return lax.ppermute(a, axis, [(0, 1), (1, 0)])  32.3 us
    all_to_all x5, starting transfers between devices, spread(): lax.all_to_all(jnp.broadcast_to(a[None], (size,) + a.shape), axis, 0, 0,...  19.5 us
    ppermute x12, starting transfers between devices, shift(): return lax.ppermute(a, 'x', [((i + step) % NX, i) for i in range(NX)])  17.7 us
    ppermute x9, starting transfers between devices, swap(): return lax.ppermute(a, axis, [(0, 1), (1, 0)])  16.8 us
    all_to_all x2, starting transfers between devices, collect(): lax.all_to_all(a, axis, 0, 0, tiled=True).astype(wide)  9.92 us
    ppermute x12, waiting for transfers between devices, shift(): return lax.ppermute(a, 'x', [((i + step) % NX, i) for i in range(NX)])  9.85 us
  transfers between devices with their start and end apart: 31, of which 12 were waited for; matrix products, arithmetic and copies ran while one was open for 11% of the time, Pallas kernels for 12%

profile of v5, /device:TPU:32, one launch (start us, length us, event | category | flops | bytes accessed | tf_op | source)
XLA Modules:
  0.0 279.7 jit_solution(12650263886760862209)
XLA Ops:
  7.2 1.8 pad_maximum_fusion.5
  9.0 1.1 fusion.16
  10.1 1.0 fusion.10
  11.1 1.6 fusion.33
  12.8 6.3 %collective-permute-start = (bf16[16,8192]{1,0:T(8,128)(2,1)}, bf16[16,8192]{1,0:T(8,128)(2,1)}, u32[]{:S(2)}, u32[]{:S(2)}) collective-permute-start(bf16[16,8192]{1,0:T(8,128)(2,1)} %get-tuple-element.53), channel_id=1, source_target_pairs={{0,4},{4,0},{1,5},{5,1},{2,6},{6,2},{3,7},{7,3},{8,12},{12,8},{9,1... | collective-permute-start | bytes 786440 | tf_op jit(solution)/shard_map/ppermute | solution.py:30
  20.6 4.4 %all-to-all-start = ((bf16[4,128,256]{2,1,0:T(8,128)(2,1)}), bf16[4,128,256]{2,1,0:T(8,128)(2,1)S(1)}, u32[]{:S(2)}, u32[]{:S(2)}) async-start(bf16[4,128,256]{2,1,0:T(8,128)(2,1)} %broadcast_in_dim.18), calls=%async_computation | async-start | bytes 524288 | tf_op jit(solution)/shard_map/all_to_all | solution.py:39
  27.1 14.5 %all-to-all-done = bf16[4,128,256]{2,1,0:T(8,128)(2,1)S(1)} async-done(((bf16[4,128,256]{2,1,0:T(8,128)(2,1)}), bf16[4,128,256]{2,1,0:T(8,128)(2,1)S(1)}, u32[]{:S(2)}, u32[]{:S(2)}) %all-to-all-start) | async-done | bytes 262176 | tf_op jit(solution)/shard_map/all_to_all | solution.py:39
  41.6 1.1 broadcast_in_dim.20
  42.7 4.5 %all-to-all-start.1 = ((bf16[4,512,256]{2,1,0:T(8,128)(2,1)}), bf16[4,512,256]{2,1,0:T(8,128)(2,1)S(1)}, u32[]{:S(2)}, u32[]{:S(2)}) async-start(bf16[4,512,256]{2,1,0:T(8,128)(2,1)} %broadcast_in_dim.20), calls=%async_computation.1 | async-start | bytes 2097152 | tf_op jit(solution)/shard_map/all_to_all | solution.py:39
  47.2 1.8 fusion.34
  49.0 1.5 collective-permute-start.3
  50.5 2.8 collective-permute-start.2
  53.3 1.4 collective-permute-start.1
  54.7 1.4 fusion.2
  56.0 13.1 %all-to-all-done.1 = bf16[4,512,256]{2,1,0:T(8,128)(2,1)S(1)} async-done(((bf16[4,512,256]{2,1,0:T(8,128)(2,1)}), bf16[4,512,256]{2,1,0:T(8,128)(2,1)S(1)}, u32[]{:S(2)}, u32[]{:S(2)}) %all-to-all-start.1) | async-done | bytes 1048608 | tf_op jit(solution)/shard_map/all_to_all | solution.py:39
  69.2 6.7 %collective-permute-done.2 = bf16[2,16,8192]{2,1,0:T(8,128)(2,1)} collective-permute-done((bf16[2,16,8192]{2,1,0:T(8,128)(2,1)S(1)}, bf16[2,16,8192]{2,1,0:T(8,128)(2,1)}, u32[]{:S(2)}, u32[]{:S(2)}) %collective-permute-start.2) | collective-permute-done | bytes 524320 | tf_op jit(solution)/shard_map/ppermute | solution.py:34
  75.8 1.8 pad_maximum_fusion
  78.0 1.2 shard_map.145
  79.6 14.9 %all_to_all.50 = bf16[4,128,256]{2,1,0:T(8,128)(2,1)S(1)} all-to-all(bf16[4,128,256]{2,1,0:T(8,128)(2,1)S(1)} %broadcast_in_dim.21), channel_id=1, replica_groups=mesh['y'=4,'z'=4,'c'=2,'h'=2,'x'=4] {'z'}, dimensions={0} | all-to-all | bytes 524288 | tf_op jit(solution)/shard_map/all_to_all | solution.py:39
  94.6 18.4 %all_to_all.51 = bf16[4,512,256]{2,1,0:T(8,128)(2,1)S(1)} all-to-all(bf16[4,512,256]{2,1,0:T(8,128)(2,1)S(1)} %broadcast_in_dim.23), channel_id=1, replica_groups=mesh['y'=4,'z'=4,'c'=2,'h'=2,'x'=4] {'y'}, dimensions={0} | all-to-all | bytes 2097152 | tf_op jit(solution)/shard_map/all_to_all | solution.py:39
  113.9 4.8 %all-to-all-start.4 = ((bf16[32,16,256]{2,1,0:T(8,128)(2,1)}), bf16[32,16,256]{2,1,0:T(8,128)(2,1)S(1)}, u32[]{:S(2)}, u32[]{:S(2)}) async-start(bf16[32,16,256]{2,1,0:T(8,128)(2,1)} %copy-done.4), calls=%async_computation.4 | async-start | bytes 524288 | tf_op jit(solution)/shard_map/all_to_all | solution.py:495
  119.0 5.2 %shard_map.144 = (bf16[512,128]{1,0:T(8,128)(2,1)S(1)}, bf16[512,128]{1,0:T(8,128)(2,1)S(1)}) custom-call(bf16[128,8192]{1,0:T(8,128)(2,1)S(1)} %bitcast.90, bf16[128,8192]{1,0:T(8,128)(2,1)S(1)} %bitcast.91, bf16[4096,1024]{1,0:T(8,128)(2,1)} %all-gather.3.cloned.1.call-done.weights, f32[128,128]{1,0:T(8,128)S(1)} %get-tuple-element.24.cosine, ...), custom_call_target="tpu_custom_call" | custom-call | tf_op jit(solution)/shard_map/pallas_call | solution.py:140
  124.2 9.2 %shard_map.146 = (bf16[128,1024]{1,0:T(8,128)(2,1)S(1)}, bf16[2048,256]{1,0:T(8,128)(2,1)S(1)}, bf16[2048,256]{1,0:T(8,128)(2,1)S(1)}) custom-call(s32[3]{0:T(128)S(1)} %pad_add_fusion.1.at_chx, bf16[512,128]{1,0:T(8,128)(2,1)S(1)} %get-tuple-element.26.query, bf16[512,128]{1,0:T(8,128)(2,1)S(1)} %get-tuple-element.27.grad_heads, ...), custom_call_target="tpu_custom_call" | custom-call | tf_op jit(solution)/shard_map/pallas_call | solution.py:244
  133.4 1.0 copy-done.8
  135.4 2.7 collective-permute-done.6
  138.1 1.3 add_convert_fusion
  139.4 0.9 collective-permute-start.7
  140.4 4.2 %all-to-all-start.5 = ((bf16[4,512,256]{2,1,0:T(8,128)(2,1)}), bf16[4,512,256]{2,1,0:T(8,128)(2,1)}, u32[]{:S(2)}, u32[]{:S(2)}) async-start(bf16[4,512,256]{2,1,0:T(8,128)(2,1)} %bitcast.20.waited), calls=%async_computation.5 | async-start | bytes 2097152 | tf_op jit(solution)/shard_map/all_to_all | solution.py:45
  144.6 16.8 %collective-permute-done.7 = bf16[32,16,256]{2,1,0:T(8,128)(2,1)S(1)} collective-permute-done((bf16[32,16,256]{2,1,0:T(8,128)(2,1)S(1)}, bf16[32,16,256]{2,1,0:T(8,128)(2,1)S(1)}, u32[]{:S(2)}, u32[]{:S(2)}) %collective-permute-start.7) | collective-permute-done | bytes 262176 | tf_op jit(solution)/shard_map/ppermute | solution.py:30
  161.5 6.0 %shard_map.149 = (bf16[128,4096]{1,0:T(8,128)(2,1)S(1)}, bf16[128,4096]{1,0:T(8,128)(2,1)S(1)}) custom-call(bf16[128,1024]{1,0:T(8,128)(2,1)S(1)} %get-tuple-element.29.att_gq.value, bf16[4096,1024]{1,0:T(8,128)(2,1)} %all-gather.3.cloned.1.call-done.weights, bf16[2,32,16,256]{3,2,1,0:T(8,128)(2,1)S(1)} %pad_maximum_fusion.3.waited.refs_0_), custom_call_target="tpu_custom_call" | custom-call | tf_op jit(solution)/shard_map/pallas_call | solution.py:267
  167.8 1.0 slice_bitcast_fusion.4
  168.8 2.8 collective-permute-start.10
  172.5 3.1 %collective-permute-start.15 = (bf16[2,32,16,256]{3,2,1,0:T(8,128)(2,1)S(1)}, bf16[2,32,16,256]{3,2,1,0:T(8,128)(2,1)S(1)}, u32[]{:S(2)}, u32[]{:S(2)}) collective-permute-start(bf16[2,32,16,256]{3,2,1,0:T(8,128)(2,1)S(1)} %pad_maximum_fusion.3.waited.refs_0_), channel_id=1, source_target_pairs={{1,0},{2,1},{3,2},{0,3},{5,4},{6,5},{7,6},{4,7},{9,8},{10,9},{11,1... | collective-permute-start | bytes 1572872 | tf_op jit(solution)/shard_map/ppermute | solution.py:34
  175.6 1.6 collective-permute-start.16
  177.2 2.1 reduce_sum.50
  179.4 5.7 %all-to-all-start.6 = ((bf16[4,128,256]{2,1,0:T(8,128)(2,1)}), bf16[4,128,256]{2,1,0:T(8,128)(2,1)S(1)}, u32[]{:S(2)}, u32[]{:S(2)}) async-start(bf16[4,128,256]{2,1,0:T(8,128)(2,1)} %bitcast.30), calls=%async_computation.6 | async-start | bytes 524288 | tf_op jit(solution)/shard_map/all_to_all | solution.py:45
  185.0 3.2 %collective-permute-done.8 = bf16[2,16,4096]{2,1,0:T(8,128)(2,1)} collective-permute-done((bf16[2,16,4096]{2,1,0:T(8,128)(2,1)}, bf16[2,16,4096]{2,1,0:T(8,128)(2,1)}, u32[]{:S(2)}, u32[]{:S(2)}) %collective-permute-start.8) | collective-permute-done | bytes 262176 | tf_op jit(solution)/shard_map/ppermute | solution.py:34
  188.2 2.1 fusion.6
  190.3 6.3 %all-to-all-done.6 = bf16[4,128,256]{2,1,0:T(8,128)(2,1)S(1)} async-done(((bf16[4,128,256]{2,1,0:T(8,128)(2,1)}), bf16[4,128,256]{2,1,0:T(8,128)(2,1)S(1)}, u32[]{:S(2)}, u32[]{:S(2)}) %all-to-all-start.6) | async-done | bytes 262176 | tf_op jit(solution)/shard_map/all_to_all | solution.py:45
  196.9 1.2 copy-done.6
  198.1 3.0 %shard_map.150 = (bf16[128,4096]{1,0:T(8,128)(2,1)S(1)}, f32[1,4096]{1,0:T(1,128)S(1)}) custom-call(bf16[128,4096]{1,0:T(8,128)(2,1)S(1)} %copy-done.6, bf16[128,256]{1,0:T(8,128)(2,1)S(1)} %pad_maximum_fusion.10.grad_kv, bf16[4096,256]{1,0:T(8,128)(2,1)S(1)} %bitcast.94, bf16[128,8192]{1,0:T(8,128)(2,1)} %bitcast.92), custom_call_target="tpu_custom_call" | custom-call | tf_op jit(solution)/shard_map/pallas_call | solution.py:295
  201.1 0.9 copy-done.3
  202.9 3.4 %all-to-all-start.7 = ((bf16[4,144,256]{2,1,0:T(8,128)(2,1)}), bf16[4,144,256]{2,1,0:T(8,128)(2,1)S(1)}, u32[]{:S(2)}, u32[]{:S(2)}) async-start(bf16[4,144,256]{2,1,0:T(8,128)(2,1)} %broadcast_in_dim.24), calls=%async_computation.7 | async-start | bytes 589824 | tf_op jit(solution)/shard_map/all_to_all | solution.py:39
  206.3 2.2 fusion.35
  209.2 1.3 collective-permute-start.13
  210.5 1.4 collective-permute-start.12
  211.9 3.3 %all-to-all-done.7 = bf16[4,144,256]{2,1,0:T(8,128)(2,1)S(1)} async-done(((bf16[4,144,256]{2,1,0:T(8,128)(2,1)}), bf16[4,144,256]{2,1,0:T(8,128)(2,1)S(1)}, u32[]{:S(2)}, u32[]{:S(2)}) %all-to-all-start.7) | async-done | bytes 294944 | tf_op jit(solution)/shard_map/all_to_all | solution.py:39
  215.1 1.1 broadcast_in_dim.25
  216.2 3.5 %all-to-all-start.8 = ((bf16[4,4,144,256]{3,2,1,0:T(8,128)(2,1)}), bf16[4,4,144,256]{3,2,1,0:T(8,128)(2,1)S(1)}, u32[]{:S(2)}, u32[]{:S(2)}) async-start(bf16[4,4,144,256]{3,2,1,0:T(8,128)(2,1)} %broadcast_in_dim.25), calls=%async_computation.8 | async-start | bytes 2359296 | tf_op jit(solution)/shard_map/all_to_all | solution.py:39
  219.8 1.6 fusion.21
  221.7 3.0 %collective-permute-start.11 = (bf16[16,4096]{1,0:T(8,128)(2,1)}, bf16[16,4096]{1,0:T(8,128)(2,1)S(1)}, u32[]{:S(2)}, u32[]{:S(2)}) collective-permute-start(bf16[16,4096]{1,0:T(8,128)(2,1)} %fusion.21), channel_id=1, source_target_pairs={{0,4},{4,0},{1,5},{5,1},{2,6},{6,2},{3,7},{7,3},{8,12},{12,8},{9,1... | collective-permute-start | bytes 393224 | tf_op jit(solution)/shard_map/ppermute | solution.py:30
  224.8 9.4 %all-to-all-done.8 = bf16[4,4,144,256]{3,2,1,0:T(8,128)(2,1)S(1)} async-done(((bf16[4,4,144,256]{3,2,1,0:T(8,128)(2,1)}), bf16[4,4,144,256]{3,2,1,0:T(8,128)(2,1)S(1)}, u32[]{:S(2)}, u32[]{:S(2)}) %all-to-all-start.8) | async-done | bytes 1179680 | tf_op jit(solution)/shard_map/all_to_all | solution.py:39
  234.2 1.3 fusion.4
  235.6 1.4 collective-permute-done.18.refs_5_
  237.0 2.8 %shard_map.151.waited = bf16[144,256]{1,0:T(8,128)(2,1)S(1)} custom-call(s32[1]{0:T(128)} %bitcast.core, bf16[2,32,16,256]{3,2,1,0:T(8,128)(2,1)S(1)} %pad_maximum_fusion.3.waited.refs_0_, bf16[2,32,16,256]{3,2,1,0:T(8,128)(2,1)S(1)} %collective-permute-done.15.refs_1_, bf16[2,32,16,256]{3,2,1,0:T(8,128)(2,1)} %collective-permute-done.16.refs_2_, ...), custom_call_target="tpu_custom_call" | custom-call | tf_op jit(solution)/shard_map/pallas_call | solution.py:380
  239.9 3.7 %collective-permute-start.19 = (bf16[16,4096]{1,0:T(8,128)(2,1)S(1)}, bf16[16,4096]{1,0:T(8,128)(2,1)S(1)}, u32[]{:S(2)}, u32[]{:S(2)}) collective-permute-start(bf16[16,4096]{1,0:T(8,128)(2,1)S(1)} %shard_map.152), channel_id=1, source_target_pairs={{0,4},{4,0},{1,5},{5,1},{2,6},{6,2},{3,7},{7,3},{8,12},{12,8},{9,1... | collective-permute-start | bytes 393224 | tf_op jit(solution)/shard_map/ppermute | solution.py:30
  244.2 3.7 %all-to-all-start.9 = ((bf16[4,144,256]{2,1,0:T(8,128)(2,1)}), bf16[4,144,256]{2,1,0:T(8,128)(2,1)S(1)}, u32[]{:S(2)}, u32[]{:S(2)}) async-start(bf16[4,144,256]{2,1,0:T(8,128)(2,1)} %broadcast_in_dim.26), calls=%async_computation.9 | async-start | bytes 589824 | tf_op jit(solution)/shard_map/all_to_all | solution.py:39
  247.9 4.3 %collective-permute-done.19 = bf16[16,4096]{1,0:T(8,128)(2,1)S(1)} collective-permute-done((bf16[16,4096]{1,0:T(8,128)(2,1)S(1)}, bf16[16,4096]{1,0:T(8,128)(2,1)S(1)}, u32[]{:S(2)}, u32[]{:S(2)}) %collective-permute-start.19) | collective-permute-done | bytes 131104 | tf_op jit(solution)/shard_map/ppermute | solution.py:30
  252.2 0.8 fusion.11
  253.1 5.9 %shard_map.154 = (f32[128,512]{1,0:T(8,128)}, f32[128,512]{1,0:T(8,128)}) custom-call(bf16[2,32,16,256]{3,2,1,0:T(8,128)(2,1)S(1)} %pad_maximum_fusion.3.waited.refs_0_, bf16[2,32,16,256]{3,2,1,0:T(8,128)(2,1)S(1)} %collective-permute-done.15.refs_1_, bf16[2,32,16,256]{3,2,1,0:T(8,128)(2,1)} %collective-permute-done.16.refs_2_, ...), custom_call_target="tpu_custom_call" | custom-call | tf_op jit(solution)/shard_map/pallas_call | solution.py:336
  259.1 0.9 copy-done.7
  260.0 2.7 collective-permute-start.20
  262.7 0.8 fusion.15
  263.6 7.1 %collective-permute-done.20 = bf16[2,144,256]{2,1,0:T(8,128)(2,1)S(1)} collective-permute-done((bf16[2,144,256]{2,1,0:T(8,128)(2,1)S(1)}, bf16[2,144,256]{2,1,0:T(8,128)(2,1)S(1)}, u32[]{:S(2)}, u32[]{:S(2)}) %collective-permute-start.20) | collective-permute-done | bytes 147488 | tf_op jit(solution)/shard_map/ppermute | solution.py:30
  (144 shorter events, 12.9 us)
Async XLA Ops:
  7.2 17.8 %copy-start.16 = (bf16[1,128,4096]{2,1,0:T(8,128)(2,1)S(1)}, bf16[1,128,4096]{2,1,0:T(8,128)(2,1)}, u32[]{:S(2)}) copy-start(bf16[1,128,4096]{2,1,0:T(8,128)(2,1)} %param.10) | copy-start | bytes 3145732
  7.2 111.8 %all-gather.3.cloned.1.call-start = ((), (), s32[]{:S(2)}) async-start(), calls=%async_computation.10 | async-start | bytes 8650752 | tf_op jit(solution)/shard_map/all_gather | solution.py:441
  10.1 102.9 %copy-start.22 = (f32[16]{0:T(128)}, f32[16]{0:T(128)S(1)}, u32[]{:S(2)}) copy-start(f32[16]{0:T(128)S(1)} %add_rsqrt_fusion) | copy-start | bytes 196
  11.1 14.0 %copy-start.21 = (s32[4096]{0:T(1024)S(1)}, s32[4096]{0:T(1024)}, u32[]{:S(2)}) copy-start(s32[4096]{0:T(1024)} %param.17) | copy-start | bytes 49156
  12.8 34.4 %collective-permute-start = (bf16[16,8192]{1,0:T(8,128)(2,1)}, bf16[16,8192]{1,0:T(8,128)(2,1)}, u32[]{:S(2)}, u32[]{:S(2)}) collective-permute-start(bf16[16,8192]{1,0:T(8,128)(2,1)} %get-tuple-element.53), channel_id=1, source_target_pairs={{0,4},{4,0},{1,5},{5,1},{2,6},{6,2},{3,7},{7,3},{8,12},{12,8},{9,1... | collective-permute-start | bytes 786440 | tf_op jit(solution)/shard_map/ppermute | solution.py:30
  20.6 21.0 %all-to-all-start = ((bf16[4,128,256]{2,1,0:T(8,128)(2,1)}), bf16[4,128,256]{2,1,0:T(8,128)(2,1)S(1)}, u32[]{:S(2)}, u32[]{:S(2)}) async-start(bf16[4,128,256]{2,1,0:T(8,128)(2,1)} %broadcast_in_dim.18), calls=%async_computation | async-start | bytes 524288 | tf_op jit(solution)/shard_map/all_to_all | solution.py:39
  42.7 26.4 %all-to-all-start.1 = ((bf16[4,512,256]{2,1,0:T(8,128)(2,1)}), bf16[4,512,256]{2,1,0:T(8,128)(2,1)S(1)}, u32[]{:S(2)}, u32[]{:S(2)}) async-start(bf16[4,512,256]{2,1,0:T(8,128)(2,1)} %broadcast_in_dim.20), calls=%async_computation.1 | async-start | bytes 2097152 | tf_op jit(solution)/shard_map/all_to_all | solution.py:39
  49.0 20.2 %collective-permute-start.3 = (bf16[2,16,8192]{2,1,0:T(8,128)(2,1)S(1)}, bf16[2,16,8192]{2,1,0:T(8,128)(2,1)}, u32[]{:S(2)}, u32[]{:S(2)}) collective-permute-start(bf16[2,16,8192]{2,1,0:T(8,128)(2,1)S(1)} %get-tuple-element.49), channel_id=1, source_target_pairs={{3,0},{0,1},{1,2},{2,3},{7,4},{4,5},{5,6},{6,7},{11,8},{8,9},{9,10... | collective-permute-start | bytes 1572872 | tf_op jit(solution)/shard_map/ppermute | solution.py:34
  50.5 25.3 %collective-permute-start.2 = (bf16[2,16,8192]{2,1,0:T(8,128)(2,1)S(1)}, bf16[2,16,8192]{2,1,0:T(8,128)(2,1)}, u32[]{:S(2)}, u32[]{:S(2)}) collective-permute-start(bf16[2,16,8192]{2,1,0:T(8,128)(2,1)S(1)} %get-tuple-element.49), channel_id=1, source_target_pairs={{2,0},{3,1},{0,2},{1,3},{6,4},{7,5},{4,6},{5,7},{10,8},{11,9},{8,1... | collective-permute-start | bytes 1572872 | tf_op jit(solution)/shard_map/ppermute | solution.py:34
  53.3 22.6 %collective-permute-start.1 = (bf16[2,16,8192]{2,1,0:T(8,128)(2,1)S(1)}, bf16[2,16,8192]{2,1,0:T(8,128)(2,1)}, u32[]{:S(2)}, u32[]{:S(2)}) collective-permute-start(bf16[2,16,8192]{2,1,0:T(8,128)(2,1)S(1)} %get-tuple-element.49), channel_id=1, source_target_pairs={{1,0},{2,1},{3,2},{0,3},{5,4},{6,5},{7,6},{4,7},{9,8},{10,9},{11,1... | collective-permute-start | bytes 1572872 | tf_op jit(solution)/shard_map/ppermute | solution.py:34
  69.1 8.5 %collective-permute-start.4 = (bf16[16,1,128,256]{3,2,1,0:T(8,128)(2,1)S(1)}, bf16[16,1,128,256]{3,2,1,0:T(8,128)(2,1)S(1)}, u32[]{:S(2)}, u32[]{:S(2)}) collective-permute-start(bf16[16,1,128,256]{3,2,1,0:T(8,128)(2,1)S(1)} %bitcast.102), channel_id=1, source_target_pairs={{0,8},{8,0},{1,9},{9,1},{2,10},{10,2},{3,11},{11,3},{4,12},{12,4},... | collective-permute-start | bytes 3145736 | tf_op jit(solution)/shard_map/ppermute | solution.py:30
  77.6 41.4 %copy-start = (bf16[4,2,16,8192]{3,2,1,0:T(8,128)(2,1)}, bf16[4,2,16,8192]{3,2,1,0:T(8,128)(2,1)S(1)}, u32[]{:S(2)}) copy-start(bf16[4,2,16,8192]{3,2,1,0:T(8,128)(2,1)S(1)} %pad_maximum_fusion) | copy-start | bytes 6291460
  78.0 1.6 copy-start.1
  79.6 33.4 %copy-start.11 = (bf16[16,4096]{1,0:T(8,128)(2,1)S(1)}, bf16[16,4096]{1,0:T(8,128)(2,1)}, u32[]{:S(2)}) copy-start(bf16[16,4096]{1,0:T(8,128)(2,1)} %param.9) | copy-start | bytes 393220
  79.6 33.4 %copy-start.14 = (bf16[16,4096]{1,0:T(8,128)(2,1)S(1)}, bf16[16,4096]{1,0:T(8,128)(2,1)}, u32[]{:S(2)}) copy-start(bf16[16,4096]{1,0:T(8,128)(2,1)} %param.16) | copy-start | bytes 393220
  79.6 33.4 %copy-start.17 = (f32[4096]{0:T(1024)S(1)}, f32[4096]{0:T(1024)}, u32[]{:S(2)}) copy-start(f32[4096]{0:T(1024)} %param.11) | copy-start | bytes 49156
  113.0 11.2 %collective-permute-start.5 = (bf16[2048,256]{1,0:T(8,128)(2,1)S(1)}, bf16[2048,256]{1,0:T(8,128)(2,1)}, u32[]{:S(2)}, u32[]{:S(2)}) collective-permute-start(bf16[2048,256]{1,0:T(8,128)(2,1)S(1)} %bitcast.95), channel_id=1, source_target_pairs={{0,8},{8,0},{1,9},{9,1},{2,10},{10,2},{3,11},{11,3},{4,12},{12,4},... | collective-permute-start | bytes 3145736 | tf_op jit(solution)/shard_map/ppermute | solution.py:30
  113.2 0.7 copy-start.4
  113.9 20.5 %all-to-all-start.4 = ((bf16[32,16,256]{2,1,0:T(8,128)(2,1)}), bf16[32,16,256]{2,1,0:T(8,128)(2,1)S(1)}, u32[]{:S(2)}, u32[]{:S(2)}) async-start(bf16[32,16,256]{2,1,0:T(8,128)(2,1)} %copy-done.4), calls=%async_computation.4 | async-start | bytes 524288 | tf_op jit(solution)/shard_map/all_to_all | solution.py:495
  118.7 134.4 %all-gather.5.cloned.1.call-start = ((), (), s32[]{:S(2)}) async-start(), calls=%async_computation.11 | async-start | bytes 8650752 | tf_op jit(solution)/shard_map/all_gather | solution.py:500
  133.4 1.0 copy-start.8
  135.1 3.0 %collective-permute-start.6 = (bf16[2048,256]{1,0:T(8,128)(2,1)}, bf16[2048,256]{1,0:T(8,128)(2,1)S(1)}, u32[]{:S(2)}, u32[]{:S(2)}) collective-permute-start(bf16[2048,256]{1,0:T(8,128)(2,1)} %copy-done.8), channel_id=1, source_target_pairs={{0,8},{8,0},{1,9},{9,1},{2,10},{10,2},{3,11},{11,3},{4,12},{12,4},... | collective-permute-start | bytes 3145736 | tf_op jit(solution)/shard_map/ppermute | solution.py:30
  139.4 22.0 %collective-permute-start.7 = (bf16[32,16,256]{2,1,0:T(8,128)(2,1)S(1)}, bf16[32,16,256]{2,1,0:T(8,128)(2,1)S(1)}, u32[]{:S(2)}, u32[]{:S(2)}) collective-permute-start(bf16[32,16,256]{2,1,0:T(8,128)(2,1)S(1)} %shard_map.148), channel_id=1, source_target_pairs={{0,4},{4,0},{1,5},{5,1},{2,6},{6,2},{3,7},{7,3},{8,12},{12,8},{9,1... | collective-permute-start | bytes 786440 | tf_op jit(solution)/shard_map/ppermute | solution.py:30
  140.4 36.8 %all-to-all-start.5 = ((bf16[4,512,256]{2,1,0:T(8,128)(2,1)}), bf16[4,512,256]{2,1,0:T(8,128)(2,1)}, u32[]{:S(2)}, u32[]{:S(2)}) async-start(bf16[4,512,256]{2,1,0:T(8,128)(2,1)} %bitcast.20.waited), calls=%async_computation.5 | async-start | bytes 2097152 | tf_op jit(solution)/shard_map/all_to_all | solution.py:45
  161.5 6.1 %copy-start.9 = (bf16[4,2,16,4096]{3,2,1,0:T(8,128)(2,1)S(1)}, bf16[4,2,16,4096]{3,2,1,0:T(8,128)(2,1)}, u32[]{:S(2)}) copy-start(bf16[4,2,16,4096]{3,2,1,0:T(8,128)(2,1)} %fusion.2) | copy-start | bytes 3145732
  167.6 1.3 copy-start.5
  167.8 4.7 %copy-start.10 = (bf16[4,2,16,4096]{3,2,1,0:T(8,128)(2,1)}, bf16[4,2,16,4096]{3,2,1,0:T(8,128)(2,1)S(1)}, u32[]{:S(2)}) copy-start(bf16[4,2,16,4096]{3,2,1,0:T(8,128)(2,1)S(1)} %fusion) | copy-start | bytes 3145732
  168.8 16.2 %collective-permute-start.10 = (bf16[2,16,4096]{2,1,0:T(8,128)(2,1)}, bf16[2,16,4096]{2,1,0:T(8,128)(2,1)}, u32[]{:S(2)}, u32[]{:S(2)}) collective-permute-start(bf16[2,16,4096]{2,1,0:T(8,128)(2,1)} %get-tuple-element.46), channel_id=1, source_target_pairs={{1,0},{2,1},{3,2},{0,3},{5,4},{6,5},{7,6},{4,7},{9,8},{10,9},{11,1... | collective-permute-start | bytes 786440 | tf_op jit(solution)/shard_map/ppermute | solution.py:34
  171.6 13.4 %collective-permute-start.9 = (bf16[2,16,4096]{2,1,0:T(8,128)(2,1)}, bf16[2,16,4096]{2,1,0:T(8,128)(2,1)}, u32[]{:S(2)}, u32[]{:S(2)}) collective-permute-start(bf16[2,16,4096]{2,1,0:T(8,128)(2,1)} %get-tuple-element.47), channel_id=1, source_target_pairs={{2,0},{3,1},{0,2},{1,3},{6,4},{7,5},{4,6},{5,7},{10,8},{11,9},{8,1... | collective-permute-start | bytes 786440 | tf_op jit(solution)/shard_map/ppermute | solution.py:34
  172.4 24.5 %copy-start.2 = (bf16[16,2,128,256]{3,2,1,0:T(8,128)(2,1)S(1)}, bf16[16,2,128,256]{3,2,1,0:T(8,128)(2,1)}, u32[]{:S(2)}) copy-start(bf16[16,2,128,256]{3,2,1,0:T(8,128)(2,1)} %copy-done.1) | copy-start | bytes 6291460
  172.4 15.8 %collective-permute-start.8 = (bf16[2,16,4096]{2,1,0:T(8,128)(2,1)}, bf16[2,16,4096]{2,1,0:T(8,128)(2,1)}, u32[]{:S(2)}, u32[]{:S(2)}) collective-permute-start(bf16[2,16,4096]{2,1,0:T(8,128)(2,1)} %get-tuple-element.45), channel_id=1, source_target_pairs={{3,0},{0,1},{1,2},{2,3},{7,4},{4,5},{5,6},{6,7},{11,8},{8,9},{9,10... | collective-permute-start | bytes 786440 | tf_op jit(solution)/shard_map/ppermute | solution.py:34
  172.5 63.1 %collective-permute-start.15 = (bf16[2,32,16,256]{3,2,1,0:T(8,128)(2,1)S(1)}, bf16[2,32,16,256]{3,2,1,0:T(8,128)(2,1)S(1)}, u32[]{:S(2)}, u32[]{:S(2)}) collective-permute-start(bf16[2,32,16,256]{3,2,1,0:T(8,128)(2,1)S(1)} %pad_maximum_fusion.3.waited.refs_0_), channel_id=1, source_target_pairs={{1,0},{2,1},{3,2},{0,3},{5,4},{6,5},{7,6},{4,7},{9,8},{10,9},{11,1... | collective-permute-start | bytes 1572872 | tf_op jit(solution)/shard_map/ppermute | solution.py:34
  175.6 60.0 %collective-permute-start.16 = (bf16[2,32,16,256]{3,2,1,0:T(8,128)(2,1)S(1)}, bf16[2,32,16,256]{3,2,1,0:T(8,128)(2,1)}, u32[]{:S(2)}, u32[]{:S(2)}) collective-permute-start(bf16[2,32,16,256]{3,2,1,0:T(8,128)(2,1)S(1)} %pad_maximum_fusion.3.waited.refs_0_), channel_id=1, source_target_pairs={{2,0},{3,1},{0,2},{1,3},{6,4},{7,5},{4,6},{5,7},{10,8},{11,9},{8,1... | collective-permute-start | bytes 1572872 | tf_op jit(solution)/shard_map/ppermute | solution.py:34
  179.4 17.2 %all-to-all-start.6 = ((bf16[4,128,256]{2,1,0:T(8,128)(2,1)}), bf16[4,128,256]{2,1,0:T(8,128)(2,1)S(1)}, u32[]{:S(2)}, u32[]{:S(2)}) async-start(bf16[4,128,256]{2,1,0:T(8,128)(2,1)} %bitcast.30), calls=%async_computation.6 | async-start | bytes 524288 | tf_op jit(solution)/shard_map/all_to_all | solution.py:45
  196.8 1.2 copy-start.6
  201.1 1.0 copy-start.3
  202.9 12.3 %all-to-all-start.7 = ((bf16[4,144,256]{2,1,0:T(8,128)(2,1)}), bf16[4,144,256]{2,1,0:T(8,128)(2,1)S(1)}, u32[]{:S(2)}, u32[]{:S(2)}) async-start(bf16[4,144,256]{2,1,0:T(8,128)(2,1)} %broadcast_in_dim.24), calls=%async_computation.7 | async-start | bytes 589824 | tf_op jit(solution)/shard_map/all_to_all | solution.py:39
  208.5 12.9 %collective-permute-start.14 = (bf16[2,16,4096]{2,1,0:T(8,128)(2,1)}, bf16[2,16,4096]{2,1,0:T(8,128)(2,1)}, u32[]{:S(2)}, u32[]{:S(2)}) collective-permute-start(bf16[2,16,4096]{2,1,0:T(8,128)(2,1)} %bitcast.34), channel_id=1, source_target_pairs={{1,0},{2,1},{3,2},{0,3},{5,4},{6,5},{7,6},{4,7},{9,8},{10,9},{11,1... | collective-permute-start | bytes 786440 | tf_op jit(solution)/shard_map/ppermute | solution.py:34
  209.2 12.6 %collective-permute-start.13 = (bf16[2,16,4096]{2,1,0:T(8,128)(2,1)}, bf16[2,16,4096]{2,1,0:T(8,128)(2,1)S(1)}, u32[]{:S(2)}, u32[]{:S(2)}) collective-permute-start(bf16[2,16,4096]{2,1,0:T(8,128)(2,1)} %bitcast.33), channel_id=1, source_target_pairs={{2,0},{3,1},{0,2},{1,3},{6,4},{7,5},{4,6},{5,7},{10,8},{11,9},{8,1... | collective-permute-start | bytes 786440 | tf_op jit(solution)/shard_map/ppermute | solution.py:34
  210.5 14.3 %collective-permute-start.12 = (bf16[2,16,4096]{2,1,0:T(8,128)(2,1)}, bf16[2,16,4096]{2,1,0:T(8,128)(2,1)S(1)}, u32[]{:S(2)}, u32[]{:S(2)}) collective-permute-start(bf16[2,16,4096]{2,1,0:T(8,128)(2,1)} %bitcast.32), channel_id=1, source_target_pairs={{3,0},{0,1},{1,2},{2,3},{7,4},{4,5},{5,6},{6,7},{11,8},{8,9},{9,10... | collective-permute-start | bytes 786440 | tf_op jit(solution)/shard_map/ppermute | solution.py:34
  216.2 17.9 %all-to-all-start.8 = ((bf16[4,4,144,256]{3,2,1,0:T(8,128)(2,1)}), bf16[4,4,144,256]{3,2,1,0:T(8,128)(2,1)S(1)}, u32[]{:S(2)}, u32[]{:S(2)}) async-start(bf16[4,4,144,256]{3,2,1,0:T(8,128)(2,1)} %broadcast_in_dim.25), calls=%async_computation.8 | async-start | bytes 2359296 | tf_op jit(solution)/shard_map/all_to_all | solution.py:39
  221.4 14.2 %collective-permute-start.17 = (bf16[2,32,16,256]{3,2,1,0:T(8,128)(2,1)S(1)}, bf16[2,32,16,256]{3,2,1,0:T(8,128)(2,1)S(1)}, u32[]{:S(2)}, u32[]{:S(2)}) collective-permute-start(bf16[2,32,16,256]{3,2,1,0:T(8,128)(2,1)S(1)} %pad_maximum_fusion.3.waited.refs_0_), channel_id=1, source_target_pairs={{3,0},{0,1},{1,2},{2,3},{7,4},{4,5},{5,6},{6,7},{11,8},{8,9},{9,10... | collective-permute-start | bytes 1572872 | tf_op jit(solution)/shard_map/ppermute | solution.py:34
  221.7 12.4 %copy-start.19 = (bf16[2,16,4096]{2,1,0:T(8,128)(2,1)}, bf16[2,16,4096]{2,1,0:T(8,128)(2,1)S(1)}, u32[]{:S(2)}) copy-start(bf16[2,16,4096]{2,1,0:T(8,128)(2,1)S(1)} %collective-permute-done.13) | copy-start | bytes 786436
  221.7 13.8 %collective-permute-start.11 = (bf16[16,4096]{1,0:T(8,128)(2,1)}, bf16[16,4096]{1,0:T(8,128)(2,1)S(1)}, u32[]{:S(2)}, u32[]{:S(2)}) collective-permute-start(bf16[16,4096]{1,0:T(8,128)(2,1)} %fusion.21), channel_id=1, source_target_pairs={{0,4},{4,0},{1,5},{5,1},{2,6},{6,2},{3,7},{7,3},{8,12},{12,8},{9,1... | collective-permute-start | bytes 393224 | tf_op jit(solution)/shard_map/ppermute | solution.py:30
  224.8 9.4 %copy-start.20 = (bf16[2,16,4096]{2,1,0:T(8,128)(2,1)}, bf16[2,16,4096]{2,1,0:T(8,128)(2,1)S(1)}, u32[]{:S(2)}) copy-start(bf16[2,16,4096]{2,1,0:T(8,128)(2,1)S(1)} %collective-permute-done.12) | copy-start | bytes 786436
  234.2 2.8 %collective-permute-start.18 = (bf16[16,144,256]{2,1,0:T(8,128)(2,1)S(1)}, bf16[16,144,256]{2,1,0:T(8,128)(2,1)S(1)}, u32[]{:S(2)}, u32[]{:S(2)}) collective-permute-start(bf16[16,144,256]{2,1,0:T(8,128)(2,1)S(1)} %bitcast.98), channel_id=1, source_target_pairs={{0,8},{8,0},{1,9},{9,1},{2,10},{10,2},{3,11},{11,3},{4,12},{12,4},... | collective-permute-start | bytes 3538952 | tf_op jit(solution)/shard_map/ppermute | solution.py:30
  235.5 16.7 %copy-start.12 = (bf16[16,4096]{1,0:T(8,128)(2,1)S(1)}, bf16[16,4096]{1,0:T(8,128)(2,1)}, u32[]{:S(2)}) copy-start(bf16[16,4096]{1,0:T(8,128)(2,1)} %param.9) | copy-start | bytes 393220
  235.5 16.7 %copy-start.18 = (f32[4096]{0:T(1024)S(1)}, f32[4096]{0:T(1024)}, u32[]{:S(2)}) copy-start(f32[4096]{0:T(1024)} %param.11) | copy-start | bytes 49156
  239.9 12.3 %collective-permute-start.19 = (bf16[16,4096]{1,0:T(8,128)(2,1)S(1)}, bf16[16,4096]{1,0:T(8,128)(2,1)S(1)}, u32[]{:S(2)}, u32[]{:S(2)}) collective-permute-start(bf16[16,4096]{1,0:T(8,128)(2,1)S(1)} %shard_map.152), channel_id=1, source_target_pairs={{0,4},{4,0},{1,5},{5,1},{2,6},{6,2},{3,7},{7,3},{8,12},{12,8},{9,1... | collective-permute-start | bytes 393224 | tf_op jit(solution)/shard_map/ppermute | solution.py:30
  244.2 14.8 %all-to-all-start.9 = ((bf16[4,144,256]{2,1,0:T(8,128)(2,1)}), bf16[4,144,256]{2,1,0:T(8,128)(2,1)S(1)}, u32[]{:S(2)}, u32[]{:S(2)}) async-start(bf16[4,144,256]{2,1,0:T(8,128)(2,1)} %broadcast_in_dim.26), calls=%async_computation.9 | async-start | bytes 589824 | tf_op jit(solution)/shard_map/all_to_all | solution.py:39
  253.1 9.6 %copy-start.13 = (f32[2,16,4096]{2,1,0:T(8,128)S(1)}, f32[2,16,4096]{2,1,0:T(8,128)}, u32[]{:S(2)}) copy-start(f32[2,16,4096]{2,1,0:T(8,128)} %fusion.6) | copy-start | bytes 1572868
  253.1 9.6 %copy-start.15 = (bf16[16,4096]{1,0:T(8,128)(2,1)S(1)}, bf16[16,4096]{1,0:T(8,128)(2,1)}, u32[]{:S(2)}) copy-start(bf16[16,4096]{1,0:T(8,128)(2,1)} %param.16) | copy-start | bytes 393220
  253.1 9.6 %copy-start.23 = (f32[16]{0:T(128)S(1)}, f32[16]{0:T(128)}, u32[]{:S(2)}) copy-start(f32[16]{0:T(128)} %copy-done.22) | copy-start | bytes 196
  259.1 1.0 copy-start.7
  260.0 10.6 %collective-permute-start.20 = (bf16[2,144,256]{2,1,0:T(8,128)(2,1)S(1)}, bf16[2,144,256]{2,1,0:T(8,128)(2,1)S(1)}, u32[]{:S(2)}, u32[]{:S(2)}) collective-permute-start(bf16[2,144,256]{2,1,0:T(8,128)(2,1)S(1)} %shard_map.155), channel_id=1, source_target_pairs={{0,4},{4,0},{1,5},{5,1},{2,6},{6,2},{3,7},{7,3},{8,12},{12,8},{9,1... | collective-permute-start | bytes 442376 | tf_op jit(solution)/shard_map/ppermute | solution.py:30
Sparse Core Ops, SparseCore 0:
  10.4 92.2 all-gather.2
  135.3 83.0 all-gather.4
